TPU v7x, 32 devices: a whole 2x2x4 slice. The times are simulated.
32 devices in a mesh: ctx: 4 (over z), mp: 4 (over y, core), rep: 2 (over x).
Axes of the slice: x: 2, y: 2, z: 4, core: 2. Of those that a mesh axis runs over, the one named last changes fastest.
Arguments:
- token_pages: bfloat16 [32, 128, 2048], P('ctx'), may hold values from -13 to 13
- page_table: int32 [32], P('ctx'), may hold values from 0 to 7, as said below
- live_flags: int32 [32], P('ctx'), may hold values from 0 to 1, as said below
- lengths: int32 [32], replicated, may hold values from 1 to 256, as said below
- decay_floor: float32 [2048], P(('mp', 'rep')), may hold values from 0.85 to 0.9998
- mixer_gain: float32 [2048], replicated, may hold values from 0.5 to 1.5
- feed_gain: float32 [2048], replicated, may hold values from 0.5 to 1.5
- trainer_mixer_in: float32 [3, 2048, 2048], P(None, ('ctx', 'mp')), may hold values from -0.125 to 0.125
- trainer_mixer_out: float32 [2048, 2048], P(None, ('ctx', 'mp')), may hold values from -0.125 to 0.125
- trainer_gate_up: float32 [2, 2048, 5632], P(None, ('ctx', 'mp')), may hold values from -0.125 to 0.125
- trainer_down: float32 [5632, 2048], P(None, ('ctx', 'mp')), may hold values from -0.078125 to 0.078125
Outputs:
- layer_output: bfloat16 [4096, 2048], P(('ctx', 'rep'), 'mp')
Inputs may be any that keep to these rules, and one draw needn't show every extreme that they name: `page_table`: within each device's block of 8 entries every value 0 to 7 appears once. `live_flags`: in each device's block of 8 flags at least half (rounded down, and never fewer than one) are ones, and some device's block is all ones. The lengths sum to 128 times the number of ones in live_flags; one prompt has exactly 256 tokens.
All inputs are finite; a program needn't handle non-finite values.
Results may differ from a plain program's by a relative error of at most 0.015.
Values may be sent and summed in bfloat16 or wider, within the bound.
No kernel may reach another device: no remote copies, remote signals or barrier semaphores. Data moves between devices by JAX's collectives and lax.ppermute only.
A program may use at most 192 MiB of HBM per device.

v0:
```python
import jax
import jax.numpy as jnp
from jax import lax
from jax.sharding import PartitionSpec as P

D = 2048
HEADS = 16


norm_eps = 1e-05


def prefix(value, axis, join, neutral):
    count, mine = (lax.axis_size(axis), lax.axis_index(axis))
    pieces = lax.all_gather(value, axis)
    total = jnp.full_like(value, 0) + jnp.asarray(neutral, value.dtype)

    def prefix_step(position, total):
        longer = join(total, pieces[position])
        return jnp.where(position < mine, longer, total)

    return lax.fori_loop(0, count - 1, prefix_step, total)


def entering_2(shard, axis, combine, identity):
    peers, position = (lax.axis_size(axis), lax.axis_index(axis))
    everything = jax.tree.map(
        lambda part, kind: lax.all_gather(part.astype(kind), axis),
        shard,
        (jnp.bfloat16, jnp.bfloat16),
    )
    start = jax.tree.map(
        lambda part, zero: jnp.broadcast_to(jnp.asarray(zero, part.dtype), part.shape),
        shard,
        identity,
    )

    def entering_step(k, before):
        reached = k < position
        new = combine(
            before, jax.tree.map(lambda part, own: part[k].astype(own.dtype), everything, shard)
        )
        return jax.tree.map(lambda a, b: jnp.where(reached, a, b), new, before)

    return lax.fori_loop(0, peers, entering_step, start)


def rms_scale(values_in, gain):
    mean_sq = jnp.mean(values_in * values_in, axis=-1, keepdims=True)
    return values_in * lax.rsqrt(mean_sq + norm_eps) * gain


def block_recurrence(queries, keys_in, values_in, log_decay, reset_count, state_init, count_init):
    highest = lax.Precision.HIGHEST

    def advance(carried_in, block_data):
        state, count_before = carried_in
        q_block, k_block, v_block, decay_block, count_block = block_data
        cumulative = jnp.cumsum(decay_block, axis=0)
        q_scaled = q_block * jnp.exp(cumulative)
        k_scaled = k_block * jnp.exp(-cumulative)
        scores = jnp.einsum("thd,shd->hts", q_scaled, k_scaled, precision=highest)
        positions = jnp.arange(count_block.shape[0])
        allowed = (positions[:, None] >= positions[None, :]) & (
            count_block[:, None] == count_block[None, :]
        )
        scores = jnp.where(allowed[None], scores, 0.0)
        outputs = jnp.einsum("hts,shd->thd", scores, v_block, precision=highest)
        from_state = jnp.einsum("thd,hde->the", q_scaled, state, precision=highest)
        outputs = outputs + jnp.where((count_block == count_before)[:, None, None], from_state, 0.0)
        last_count = count_block[-1]
        final_cum = cumulative[-1]
        weight_keys = (
            k_block
            * jnp.exp(final_cum[None] - cumulative)
            * (count_block == last_count).astype(k_block.dtype)[:, None, None]
        )
        retained = jnp.where(
            last_count == count_before, jnp.exp(final_cum)[:, :, None] * state, 0.0
        )
        state_next = retained + jnp.einsum("thd,the->hde", weight_keys, v_block, precision=highest)
        return ((state_next, last_count), outputs)

    final_carry, outputs_all = lax.scan(
        advance, (state_init, count_init), (queries, keys_in, values_in, log_decay, reset_count)
    )
    return (outputs_all, final_carry[0])


def compose_states(earlier, later):
    return (earlier[0] * later[0], later[0][:, :, None] * earlier[1] + later[1])


def add_counts(earlier, later):
    return earlier + later


def shards(
    token_pages,
    page_table,
    live_flags,
    lengths,
    decay_floor,
    mixer_gain,
    feed_gain,
    trainer_mixer_in,
    trainer_mixer_out,
    trainer_gate_up,
    trainer_down,
):
    mp_count = lax.axis_size("mp")
    rep_count = lax.axis_size("rep")
    mp_index = lax.axis_index("mp")
    rep_index = lax.axis_index("rep")
    width_local = trainer_mixer_in.shape[1]
    model_width = trainer_mixer_in.shape[2]
    head_cols = decay_floor.shape[0]
    head_dim = D // HEADS
    local_heads = head_cols // head_dim
    hidden_block = trainer_gate_up.shape[2] // mp_count
    mixer_in = lax.dynamic_index_in_dim(
        trainer_mixer_in.reshape(3, width_local, mp_count, rep_count, head_cols),
        rep_index,
        3,
        keepdims=False,
    )
    mixer_in = jnp.transpose(mixer_in, (1, 2, 0, 3)).reshape(width_local, mp_count, 3 * head_cols)
    mixer_out = lax.dynamic_index_in_dim(
        trainer_mixer_out.reshape(mp_count, rep_count, head_cols, width_local),
        rep_index,
        1,
        keepdims=False,
    )
    mixer_out = jnp.transpose(mixer_out, (2, 0, 1))
    gate_up = trainer_gate_up.reshape(2, width_local, mp_count, hidden_block)
    down_rows = trainer_down.reshape(mp_count, hidden_block, width_local)
    gate_up = jnp.transpose(gate_up, (1, 2, 0, 3)).reshape(width_local, mp_count, 2 * hidden_block)
    down_rows = jnp.transpose(down_rows, (2, 0, 1))
    packed = jnp.concatenate([mixer_in, mixer_out, gate_up, down_rows], axis=2).astype(jnp.bfloat16)
    arrived = lax.all_to_all(packed, "mp", split_axis=1, concat_axis=0, tiled=True)
    arrived = arrived.reshape(mp_count * width_local, packed.shape[2])
    served = lax.all_gather(arrived, "ctx", axis=0, tiled=True)
    w_mixer = served[:, : 3 * head_cols]
    w_output_t = served[:, 3 * head_cols : 4 * head_cols]
    feed_weights = served[:, 4 * head_cols :].reshape(model_width, 3, hidden_block)
    pages_local = token_pages.shape[0]
    page_len = token_pages.shape[1]
    tok_count = pages_local * page_len
    ordered = jnp.take(token_pages, page_table, axis=0).reshape(tok_count, model_width)
    live_tokens = jnp.repeat(live_flags, page_len)
    page_live = live_flags * page_len
    live_total = jnp.sum(page_live)
    stream_base = prefix(live_total, "ctx", add_counts, jnp.zeros((), jnp.int32))
    page_start = stream_base + jnp.cumsum(page_live) - page_live
    positions = (page_start[:, None] + jnp.arange(page_len, dtype=jnp.int32)[None, :]).reshape(
        tok_count
    )
    starts = jnp.cumsum(lengths) - lengths
    resets = (live_tokens == 1) & jnp.any(positions[:, None] == starts[None, :], axis=1)
    reset_count = jnp.cumsum(resets.astype(jnp.int32))
    live_float = live_tokens.astype(jnp.float32)[:, None]
    normed = rms_scale(ordered.astype(jnp.float32), mixer_gain).astype(jnp.bfloat16)
    projected = jnp.dot(normed, w_mixer, preferred_element_type=jnp.float32).reshape(
        tok_count, 3, head_cols
    )
    queries = jax.nn.silu(projected[:, 0])
    forget = decay_floor + (1.0 - decay_floor) * jax.nn.sigmoid(projected[:, 1])
    log_decay = jnp.log(forget) * live_float
    keys_in = (1.0 - forget) * live_float
    values_in = projected[:, 2]
    shape_blocks = (pages_local, page_len, local_heads, head_dim)
    local_out, local_state = block_recurrence(
        queries.reshape(shape_blocks),
        keys_in.reshape(shape_blocks),
        values_in.reshape(shape_blocks),
        log_decay.reshape(shape_blocks),
        reset_count.reshape(pages_local, page_len),
        jnp.zeros((local_heads, head_dim, head_dim), jnp.float32),
        jnp.zeros((), jnp.int32),
    )
    device_decay = jnp.where(
        reset_count[-1] == 0, jnp.exp(jnp.sum(log_decay, axis=0)), 0.0
    ).reshape(local_heads, head_dim)
    identity = (
        jnp.ones((local_heads, head_dim), jnp.float32),
        jnp.zeros((local_heads, head_dim, head_dim), jnp.float32),
    )
    entering = entering_2((device_decay, local_state), "ctx", compose_states, identity)[1]
    cum_device = jnp.cumsum(log_decay, axis=0).reshape(tok_count, local_heads, head_dim)
    scaled_queries = queries.reshape(tok_count, local_heads, head_dim) * jnp.exp(cum_device)
    correction = jnp.einsum(
        "thd,hde->the", scaled_queries, entering, precision=lax.Precision.HIGHEST
    )
    mixed = local_out.reshape(tok_count, local_heads, head_dim) + jnp.where(
        (reset_count == 0)[:, None, None], correction, 0.0
    )
    head_normed = (
        (mixed * lax.rsqrt(jnp.mean(mixed * mixed, axis=-1, keepdims=True) + norm_eps))
        .reshape(tok_count, head_cols)
        .astype(jnp.bfloat16)
    )
    half_rows = tok_count // rep_count
    col_block = model_width // mp_count
    attn_term = lax.dot_general(
        head_normed, w_output_t, (((1,), (1,)), ((), ())), preferred_element_type=jnp.float32
    )
    attn_all = lax.psum(attn_term.astype(jnp.bfloat16), ("mp", "rep")).astype(jnp.float32)
    residual = lax.dynamic_slice_in_dim(ordered, rep_index * half_rows, half_rows, 0).astype(
        jnp.float32
    ) + lax.dynamic_slice_in_dim(attn_all, rep_index * half_rows, half_rows, 0)
    feed_in = rms_scale(residual, feed_gain).astype(jnp.bfloat16)
    gated = jnp.einsum(
        "td,dcf->tcf", feed_in, feed_weights[:, :2], preferred_element_type=jnp.float32
    )
    hidden = (jax.nn.silu(gated[:, 0]) * gated[:, 1]).astype(jnp.bfloat16)
    down_term = lax.dot_general(
        hidden, feed_weights[:, 2], (((1,), (1,)), ((), ())), preferred_element_type=jnp.float32
    )
    summed = lax.psum_scatter(
        down_term.astype(jnp.bfloat16), "mp", scatter_dimension=1, tiled=True
    ).astype(jnp.float32)
    summed = summed + lax.dynamic_slice_in_dim(residual, mp_index * col_block, col_block, 1)
    live_half = lax.dynamic_slice_in_dim(live_tokens, rep_index * half_rows, half_rows, 0)
    return jnp.where(live_half[:, None] == 1, summed, 0.0).astype(jnp.bfloat16)


def solution(mesh):
    in_specs = (
        P("ctx", None, None),
        P("ctx"),
        P("ctx"),
        P(),
        P(("mp", "rep")),
        P(),
        P(),
        P(None, ("ctx", "mp"), None),
        P(None, ("ctx", "mp")),
        P(None, ("ctx", "mp"), None),
        P(None, ("ctx", "mp")),
    )
    out_specs = P(("ctx", "rep"), "mp")
    return jax.shard_map(shards, mesh=mesh, in_specs=in_specs, out_specs=out_specs, check_vma=False)
```

profile of v0, /device:TPU:0, one launch (start us, length us, event | category | flops | bytes accessed | tf_op | source)
XLA Modules:
  0.0 761.4 jit_solution(13603331629604485685)
XLA Ops:
  9.1 5.2 copy.101
  17.1 8.0 %pad_maximum_fusion = bf16[128,4,5248]{0,2,1:T(8,128)(2,1)S(1)} fusion(bf16[128,4,1408]{0,2,1:T(8,128)(2,1)S(1)} %bitcast.188, bf16[128,4,2816]{0,2,1:T(8,128)(2,1)S(1)} %bitcast.187, bf16[128,4,256]{0,2,1:T(8,128)(2,1)S(1)} %fusion.52, bf16[128,4,768]{0,2,1:T(8,128)(2,1)S(1)} %bitcast.195), kind=kLoop, calls=%fused_computation.45 | loop fusion | flops 21495808 | bytes 10747904 | tf_op jit(solution)/shard_map/concatenate | solution.py:139
  25.1 65.0 %all_to_all.15 = bf16[128,4,5248]{0,2,1:T(8,128)(2,1)} all-to-all(bf16[128,4,5248]{0,2,1:T(8,128)(2,1)S(1)} %pad_maximum_fusion), channel_id=1, replica_groups=mesh['ctx'=4,'mp'=4,'rep'=2] {'mp'}, dimensions={1} | all-to-all | bytes 10747904 | tf_op jit(solution)/shard_map/all_to_all | solution.py:140
  90.1 8.1 %copy.103 = bf16[4,128,1,5248]{3,1,0,2:T(8,128)(2,1)} copy(bf16[4,128,1,5248]{1,3,0,2:T(8,128)(2,1)} %bitcast.183) | data formatting | bytes 10747904 | tf_op jit(solution)/shard_map/all_to_all | solution.py:140
  101.5 9.3 %all-reduce = s32[4]{0:T(128)S(1)} all-reduce(s32[4]{0:T(128)S(1)} %dynamic-update-slice), channel_id=1, replica_groups=mesh['ctx'=4,'mp'=4,'rep'=2] {'ctx'}, use_global_device_ids=true, to_apply=%add | all-reduce | flops 4 | bytes 32
  116.6 5.4 gather_fusion
  130.1 334.8 %all-gather.3.cloned.1.call-done = bf16[2048,5248]{1,0:T(8,128)(2,1)} async-done(((bf16[512,5248]{1,0:T(8,128)(2,1)}), bf16[2048,5248]{1,0:T(8,128)(2,1)}) %all-gather.3.cloned.1.call-update) | async-done | bytes 21495824 | tf_op jit(solution)/shard_map/all_gather | solution.py:142
  473.4 6.2 fusion.64
  493.3 89.2 %while.43 = (s32[]{:T(128)}, f32[2,128,128]{2,1,0:T(8,128)S(1)}, s32[]{:T(128)}, f32[8,128,2,128]{1,0,3,2:T(8,128)}, s32[8,128]{1,0:T(8,128)S(1)}, /*index=5*/f3...) while((s32[]{:T(128)}, f32[2,128,128]{2,1,0:T(8,128)S(1)}, ...), condition=%wide.region_11.12_spmd.clone, body=%wide.region_9.11_spmd.clone.sunk | while | flops 205996416 | bytes 3712430 | solution.py:84
  498.0 4.7 dynamic_update_slice.6
  509.2 4.7 dynamic_update_slice.6
  520.3 4.7 dynamic_update_slice.6
  531.5 4.7 dynamic_update_slice.6
  542.6 4.7 dynamic_update_slice.6
  553.8 4.7 dynamic_update_slice.6
  564.9 4.7 dynamic_update_slice.6
  582.6 14.8 %all-gather = bf16[8,128,128]{2,1,0:T(8,128)(2,1)S(1)} all-gather(bf16[2,128,128]{2,1,0:T(8,128)(2,1)S(1)} %convert_element_type.128), channel_id=2, replica_groups=mesh['ctx'=4,'mp'=4,'rep'=2] {'ctx'}, dimensions={0}, use_global_device_ids=true | all-gather | bytes 327680 | tf_op jit(solution)/shard_map/all_gather | solution.py:28
  599.1 7.6 all_gather.22
  618.5 14.2 %slice.81 = bf16[2048,4224]{1,0:T(8,128)(2,1)} slice(bf16[2048,5248]{1,0:T(8,128)(2,1)} %all-gather.3.cloned.1.call-done), slice={[0:2048], [1024:5248]} | slice | bytes 34603008 | tf_op jit(solution)/shard_map/slice | solution.py:145
  632.6 22.8 %copy.114 = bf16[2048,4224]{0,1:T(8,128)(2,1)} copy(bf16[2048,4224]{1,0:T(8,128)(2,1)} %slice.81) | data formatting | bytes 34603008 | tf_op jit(solution)/shard_map/slice | solution.py:145
  655.4 43.5 %all-reduce.3.cloned.1.call-done = bf16[1024,2048]{1,0:T(8,128)(2,1)} async-done(((bf16[1024,2048]{1,0:T(8,128)(2,1)}), bf16[1024,2048]{1,0:T(8,128)(2,1)}) %all-reduce.3.cloned.1.call-update) | async-done | bytes 4194320 | tf_op jit(solution)/shard_map/psum | solution.py:207
  702.1 11.2 %fusion.19 = f32[512,2,1408]{2,0,1:T(8,128)S(1)} fusion(bf16[2048,3,1408]{0,2,1:T(8,128)(2,1)} %bitcast.184, f32[512,2048]{1,0:T(8,128)S(1)} %get-tuple-element.362, f32[2048]{0:T(1024)S(1)} %copy-done.14, f32[512]{0:T(512)S(1)} %add_rsqrt_fusion.2), kind=kOutput, calls=%fused_computation.36 | convolution fusion | flops 5908725760 | bytes 21506048 | tf_op jit(solution)/shard_map/td,dcf->tcf/dot_general | solution.py:212
  713.4 7.5 fusion.25
  721.0 31.6 %reduce-scatter.2.cloned.1.call-done = bf16[512,512]{1,0:T(8,128)(2,1)} async-done(((bf16[512,2048]{1,0:T(8,128)(2,1)}), bf16[512,512]{1,0:T(8,128)(2,1)}) %reduce-scatter.2.cloned.1.call-update) | async-done | bytes 524304 | tf_op jit(solution)/shard_map/reduce_scatter | solution.py:219
  (230 shorter events, 110.3 us)
Async XLA Ops:
  6.5 2.5 copy-start
  6.5 458.4 %all-gather.3.cloned.1.call-start = ((), (), s32[]{:S(2)}) async-start(), calls=%async_computation.2 | async-start | bytes 26869760 | tf_op jit(solution)/shard_map/all_gather | solution.py:142
  14.3 2.7 copy-start.5
  98.2 0.7 copy-start.15
  98.2 1.2 copy-start.11
  98.2 1.2 copy-start.13
  98.2 12.7 %copy-start.12 = (s32[32]{0:T(128)S(1)}, s32[32]{0:T(128)}, u32[]{:S(2)}) copy-start(s32[32]{0:T(128)} %param.20) | copy-start | bytes 388
  98.2 600.7 %all-reduce.3.cloned.1.call-start = ((), (), s32[]{:S(2)}) async-start(), calls=%async_computation.3 | async-start | bytes 8388608 | tf_op jit(solution)/shard_map/psum | solution.py:207
  116.6 6.2 copy-start.9
  122.0 4.7 copy-start.2
  122.0 4.7 copy-start.10
  479.6 1.7 copy-start.4
  582.5 24.8 %copy-start.7 = (f32[8,128,2,128]{1,0,3,2:T(8,128)S(1)}, f32[8,128,2,128]{1,0,3,2:T(8,128)}, u32[]{:S(2)}) copy-start(f32[8,128,2,128]{1,0,3,2:T(8,128)} %get-tuple-element.227) | copy-start | bytes 3145732
  608.5 2.5 copy-start.6
  609.1 1.9 copy-start.8
  618.2 134.4 %reduce-scatter.2.cloned.1.call-start = ((), (), s32[]{:S(2)}) async-start(), calls=%async_computation.4 | async-start | bytes 2621440 | tf_op jit(solution)/shard_map/reduce_scatter | solution.py:219
  698.9 3.2 copy-start.14
  702.1 11.2 %copy-start.3 = (f32[512,2048]{1,0:T(8,128)}, f32[512,2048]{1,0:T(8,128)S(1)}, u32[]{:S(2)}) copy-start(f32[512,2048]{1,0:T(8,128)S(1)} %get-tuple-element.362) | copy-start | bytes 12582916
  713.4 41.5 %copy-start.1 = (f32[2048,128]{1,0:T(8,128)S(1)}, f32[2048,128]{1,0:T(8,128)}, u32[]{:S(2)}) copy-start(f32[2048,128]{1,0:T(8,128)} %param.25) | copy-start | bytes 3145732
Sparse Core Ops, SparseCore 0:
  98.3 366.5 all-gather.2
  618.4 80.4 all-reduce.2
  721.1 31.4 reduce-scatter.1
where the time goes:
time: 764 us; the launch traced here: 761 us
  waiting for transfers between devices  410 us (54%)
  local copies, waits for them, and re-layouts  137 us (18%)
  blocking collectives  96.6 us (13%)
  other arithmetic  48.2 us (6%)
  matrix products  42.6 us (6%)
  between operations  14.2 us (2%)
  loops' own time  13.1 us (2%)
    all_gather x1, waiting for transfers between devices, shards(): served = lax.all_gather(arrived, 'ctx', axis=0, tiled=True)  335 us
    all_to_all x1, blocking collectives, shards(): lax.all_to_all(packed, 'mp', split_axis=1, concat_axis=0, tiled=True)  65 us
    psum x1, waiting for transfers between devices, shards(): lax.psum(attn_term.astype(jnp.bfloat16), ('mp', 'rep')).astype(jnp.float32)  43.5 us
    dynamic_update_slice x16, local copies, waits for them, and re-layouts, block_recurrence(): lax.scan(advance, (state_init, count_init), (queries, keys_in, values_in,...  38.7 us
    slice x2, local copies, waits for them, and re-layouts, shards(): served[:, 4 * head_cols:].reshape(model_width, 3, hidden_block)  36.9 us
    reduce_scatter x1, waiting for transfers between devices, shards(): lax.psum_scatter(down_term.astype(jnp.bfloat16), 'mp', scatter_dimension=...  31.6 us
    all_gather x2, blocking collectives, entering_2(): lax.all_gather(part.astype(kind), axis)  22.4 us
  transfers between devices with their start and end apart: 3, of which 3 were waited for; matrix products, arithmetic and copies ran while one was open for 7% of the time, Pallas kernels for 0%

commit v1 on v0

v1 whole, which is shorter than its diff:
```python
import functools

import jax
import jax.numpy as jnp
from jax import lax
from jax.experimental import pallas as pl
from jax.experimental.pallas import tpu as pltpu
from jax.sharding import PartitionSpec as P

HEAD = 128
EPS = 1e-05
BF = jnp.bfloat16
F32 = jnp.float32
VMEM_LIMIT = 48 * 1024 * 1024


def nt(a, b):
    return lax.dot_general(a, b, (((1,), (1,)), ((), ())), preferred_element_type=F32)


def tn(a, b):
    return lax.dot_general(a, b, (((0,), (0,)), ((), ())), preferred_element_type=F32)


def nn(a, b):
    return jnp.dot(a, b, preferred_element_type=F32)


def sigmoid(v):
    return 1.0 / (1.0 + jnp.exp(-v))


def call(body, grid, in_specs, out_specs, out_shape, scratch=(), prefetch=1, cost=None):
    return pl.pallas_call(
        body,
        out_shape=out_shape,
        grid_spec=pltpu.PrefetchScalarGridSpec(
            num_scalar_prefetch=prefetch,
            grid=grid,
            in_specs=in_specs,
            out_specs=out_specs,
            scratch_shapes=list(scratch),
        ),
        compiler_params=pltpu.CompilerParams(
            dimension_semantics=("arbitrary",) * len(grid), vmem_limit_bytes=VMEM_LIMIT
        ),
        cost_estimate=None
        if cost is None
        else pl.CostEstimate(flops=cost[0], bytes_accessed=cost[1], transcendentals=0),
    )


def whole(shape):
    zeros = (0,) * len(shape)
    return pl.BlockSpec(shape, lambda *_: zeros, pipeline_mode=pl.Buffered(1))


def pack_mixer(ids, mixer_in, mixer_out):
    width = mixer_in.shape[1]
    cols = mixer_in.shape[2] // 8

    def body(ids_ref, q_ref, f_ref, v_ref, o_ref, out_ref):
        out_ref[0, :, 0:cols] = q_ref[0].astype(BF)
        out_ref[0, :, cols : 2 * cols] = f_ref[0].astype(BF)
        out_ref[0, :, 2 * cols : 3 * cols] = v_ref[0].astype(BF)
        out_ref[0, :, 3 * cols : 4 * cols] = o_ref[...].T.astype(BF)

    def dest(s, ids_ref):
        return 2 * (ids_ref[0] ^ s) + ids_ref[1]

    def part(i):
        return pl.BlockSpec((1, width, cols), lambda s, r: (i, 0, dest(s, r)))

    return call(
        body,
        (4,),
        [part(0), part(1), part(2), pl.BlockSpec((cols, width), lambda s, r: (dest(s, r), 0))],
        pl.BlockSpec((1, width, 4 * cols), lambda s, r: (s, 0, 0)),
        jax.ShapeDtypeStruct((4, width, 4 * cols), BF),
        cost=(0, 4 * width * cols * 24),
    )(ids, mixer_in, mixer_in, mixer_in, mixer_out)


def feed_sizes(hidden_all):
    full = hidden_all // 128 // 8 * 128
    half = (hidden_all - 8 * full) // 8
    return full, half


def pack_feed(ids, gate_up, down):
    width = gate_up.shape[1]
    full, half = feed_sizes(gate_up.shape[2])
    assert half == 64
    gu = 2 * full + 128
    total = gu + full + 128

    def body(ids_ref, g_ref, u_ref, gh_ref, uh_ref, d_ref, dh_ref, out_ref):
        odd = (ids_ref[0] ^ pl.program_id(0)) % 2
        out_ref[0, :, 0:full] = g_ref[0].astype(BF)
        lane = lax.broadcasted_iota(jnp.int32, (width, 128), 1)
        gh, uh = gh_ref[0], uh_ref[0]
        even_mix = jnp.where(lane < 64, gh, pltpu.roll(uh, 64, 1))
        odd_mix = jnp.where(lane < 64, pltpu.roll(gh, 64, 1), uh)
        out_ref[0, :, full : full + 128] = jnp.where(odd == 1, odd_mix, even_mix).astype(BF)
        out_ref[0, :, full + 128 : gu] = u_ref[0].astype(BF)
        out_ref[0, :, gu : gu + full] = d_ref[...].T.astype(BF)
        last = jnp.concatenate([dh_ref[...], jnp.zeros((64, width), F32)], axis=0)
        out_ref[0, :, gu + full : total] = last.T.astype(BF)

    def dest(s, r):
        return 4 * r[1] + (r[0] ^ s)

    def tile(s, r):
        return 8 * full // 128 + 2 * r[1] + (r[0] ^ s) // 2

    def cols(i):
        return pl.BlockSpec((1, width, full), lambda s, r: (i, 0, dest(s, r)))

    def mix(i):
        return pl.BlockSpec((1, width, 128), lambda s, r: (i, 0, tile(s, r)))

    return call(
        body,
        (4,),
        [
            cols(0),
            cols(1),
            mix(0),
            mix(1),
            pl.BlockSpec((full, width), lambda s, r: (dest(s, r), 0)),
            pl.BlockSpec((64, width), lambda s, r: (8 * full // 64 + dest(s, r), 0)),
        ],
        pl.BlockSpec((1, width, total), lambda s, r: (s, 0, 0)),
        jax.ShapeDtypeStruct((4, width, total), BF),
        cost=(0, 4 * width * total * 6),
    )(ids, gate_up, gate_up, gate_up, gate_up, down, down)


def mp_perm(value, s):
    return lax.ppermute(value, "mp", [(i, i ^ s) for i in range(4)])


def rep_perm(value):
    return lax.ppermute(value, "rep", [(0, 1), (1, 0)])


def across_plane(packed, mp_index):
    arrived = [packed[0]] + [mp_perm(packed[s], s) for s in (1, 2, 3)]
    out = jnp.zeros(packed.shape, packed.dtype)
    for s in range(4):
        out = lax.dynamic_update_index_in_dim(out, arrived[s], mp_index ^ s, 0)
    return out.reshape(4 * packed.shape[1], packed.shape[2])


def along_line(block, ctx_index, count):
    if count != 4:
        return lax.all_gather(block, "ctx", axis=0)
    out = jnp.zeros((3 * count - 2, *block.shape), block.dtype)
    out = lax.dynamic_update_index_in_dim(out, block, ctx_index + count - 1, 0)
    low = high = block
    for d in range(1, count):
        low = lax.ppermute(low, "ctx", [(i, i + 1) for i in range(count - 1)])
        high = lax.ppermute(high, "ctx", [(i + 1, i) for i in range(count - 1)])
        out = lax.dynamic_update_index_in_dim(out, low, ctx_index - d + count - 1, 0)
        out = lax.dynamic_update_index_in_dim(out, high, ctx_index + d + count - 1, 0)
    return out[count - 1 : 2 * count - 1]


def from_earlier(value, count):
    return [
        lax.ppermute(value, "ctx", [(i, i + d) for i in range(count - d)]) for d in range(1, count)
    ]


def normalise(page_table, token_pages, gain):
    pages, page, width = token_pages.shape

    def body(table_ref, x_ref, g_ref, out_ref):
        x = x_ref[0].astype(F32)
        scale = lax.rsqrt(jnp.mean(x * x, axis=-1, keepdims=True) + EPS)
        out_ref[...] = (x * scale * g_ref[...]).astype(BF)

    return call(
        body,
        (pages,),
        [pl.BlockSpec((1, page, width), lambda i, t: (t[i], 0, 0)), whole((1, width))],
        pl.BlockSpec((page, width), lambda i, t: (i, 0)),
        jax.ShapeDtypeStruct((pages * page, width), BF),
        cost=(pages * page * width * 4, pages * page * width * 4),
    )(page_table, token_pages, gain.reshape(1, width))


def step_state(state, ks, v, same_last, keep, final):
    update = tn(v, jnp.where(same_last, ks, jnp.zeros_like(ks)))
    return (jnp.where(keep, state, 0.0) + update) * final


def project(live, last, normed, weights, floor, cnt_col):
    rows, width = normed.shape
    cols = floor.shape[1]
    heads = cols // HEAD
    pages = live.shape[0]
    page = rows // pages
    group = 2
    steps = pages // group

    def body(live_ref, last_ref, x_ref, w_ref, fl_ref, cnt_ref, qs_ref, ks_ref, v_ref, fin_ref, st_ref, state, total):
        step = pl.program_id(0)

        @pl.when(step == 0)
        def _():
            state[...] = jnp.zeros_like(state)
            total[...] = jnp.zeros_like(total)

        proj = nn(x_ref[...], w_ref[:, 0 : 3 * cols])
        row = lax.broadcasted_iota(jnp.int32, (page, page), 0)
        col = lax.broadcasted_iota(jnp.int32, (page, page), 1)
        lower = (row >= col).astype(F32)
        floor_row = fl_ref[...]
        for j in range(group):
            p = step * group + j
            here = slice(j * page, (j + 1) * page)
            alive = live_ref[p].astype(F32)
            now = last_ref[p]
            before = jnp.where(p == 0, 0, last_ref[jnp.maximum(p - 1, 0)])
            q = proj[here, 0:cols]
            q = q * sigmoid(q)
            f = proj[here, cols : 2 * cols]
            gate = sigmoid(f)
            forget = floor_row + (1.0 - floor_row) * gate
            key = (1.0 - forget) * alive
            log_decay = jnp.log(forget) * alive
            cum = jnp.dot(lower, log_decay, precision=lax.Precision.HIGHEST, preferred_element_type=F32)
            final_log = cum[page - 1 : page, :]
            final = jnp.exp(final_log)
            ks = (key * jnp.exp(-cum)).astype(BF)
            v = proj[here, 2 * cols : 3 * cols].astype(BF)
            qs_ref[here, :] = (q * jnp.exp(cum)).astype(BF)
            ks_ref[here, :] = ks
            v_ref[here, :] = v
            fin_ref[j] = final
            total[...] += final_log
            same_last = cnt_ref[here, :] == now
            for h in range(heads):
                hc = slice(h * HEAD, (h + 1) * HEAD)
                state[h] = step_state(state[h], ks[:, hc], v[:, hc], same_last, now == before, final[:, hc])

        @pl.when(step == steps - 1)
        def _():
            none = last_ref[pages - 1] == 0
            decay = jnp.where(none, jnp.exp(total[...]), 0.0)
            for h in range(heads):
                st_ref[h, 0:HEAD, :] = state[h].astype(BF)
                st_ref[h, HEAD : HEAD + 16, :] = jnp.broadcast_to(
                    decay[:, h * HEAD : (h + 1) * HEAD], (16, HEAD)
                ).astype(BF)

    block = group * page
    return call(
        body,
        (steps,),
        [
            pl.BlockSpec((block, width), lambda i, *_: (i, 0)),
            whole((width, weights.shape[1])),
            whole((1, cols)),
            pl.BlockSpec((block, 1), lambda i, *_: (i, 0)),
        ],
        [
            pl.BlockSpec((block, cols), lambda i, *_: (i, 0)),
            pl.BlockSpec((block, cols), lambda i, *_: (i, 0)),
            pl.BlockSpec((block, cols), lambda i, *_: (i, 0)),
            pl.BlockSpec((group, 1, cols), lambda i, *_: (i, 0, 0)),
            whole((heads, HEAD + 16, HEAD)),
        ],
        [
            jax.ShapeDtypeStruct((rows, cols), BF),
            jax.ShapeDtypeStruct((rows, cols), BF),
            jax.ShapeDtypeStruct((rows, cols), BF),
            jax.ShapeDtypeStruct((pages, 1, cols), F32),
            jax.ShapeDtypeStruct((heads, HEAD + 16, HEAD), BF),
        ],
        scratch=[pltpu.VMEM((heads, HEAD, HEAD), F32), pltpu.VMEM((1, cols), F32)],
        prefetch=2,
        cost=(2 * rows * width * 3 * cols, rows * width * 2 + width * cols * 8),
    )(live, last, normed, weights, floor, cnt_col)


def mix(last, ids, earlier, qs, ks, v, fin, weights, cnt_col, cnt_row):
    rows, cols = qs.shape
    heads = cols // HEAD
    pages = fin.shape[0]
    page = rows // pages
    group = 2
    steps = pages // group
    width = weights.shape[1] * 4
    n = len(earlier)

    def body(last_ref, ids_ref, *refs):
        packs = refs[:n]
        qs_ref, ks_ref, v_ref, fin_ref, w_ref, cc_ref, cr_ref, out_ref, state = refs[n:]
        step = pl.program_id(0)
        mp_index = ids_ref[0]

        @pl.when(step == 0)
        def _():
            for h in range(heads):
                total = jnp.zeros((HEAD, HEAD), F32)
                for pack in reversed(packs):
                    total = total * pack[h, HEAD : HEAD + 1, :].astype(F32) + pack[h, 0:HEAD, :].astype(F32)
                state[h] = total

        row = lax.broadcasted_iota(jnp.int32, (page, page), 0)
        col = lax.broadcasted_iota(jnp.int32, (page, page), 1)
        lower = row >= col
        normed = []
        for j in range(group):
            p = step * group + j
            here = slice(j * page, (j + 1) * page)
            now = last_ref[p]
            before = jnp.where(p == 0, 0, last_ref[jnp.maximum(p - 1, 0)])
            cc, cr = cc_ref[here, :], cr_ref[j]
            allowed = lower & (cc == cr)
            reached = cc == before
            same_last = cc == now
            for h in range(heads):
                hc = slice(h * HEAD, (h + 1) * HEAD)
                q_h, k_h, v_h = qs_ref[here, hc], ks_ref[here, hc], v_ref[here, hc]
                scores = jnp.where(allowed, nt(q_h, k_h), 0.0).astype(BF)
                out = nn(scores, v_h)
                out = out + jnp.where(reached, nt(q_h, state[h].astype(BF)), 0.0)
                state[h] = step_state(state[h], k_h, v_h, same_last, now == before, fin_ref[j, :, hc])
                scale = lax.rsqrt(jnp.mean(out * out, axis=-1, keepdims=True) + EPS)
                normed.append((out * scale).astype(BF))
        hn = jnp.concatenate(
            [jnp.concatenate(normed[j * heads : (j + 1) * heads], axis=1) for j in range(group)], axis=0
        )
        for dc in range(2):
            for dy in range(2):
                w = w_ref[mp_index ^ (2 * dy + dc)]
                out_ref[dc, 0, 0, dy] = nt(hn, w[:, 3 * cols : 4 * cols]).astype(BF)

    block = group * page
    rowspec = pl.BlockSpec((block, cols), lambda i, *_: (i, 0))
    return call(
        body,
        (steps,),
        [whole(e.shape) for e in earlier]
        + [
            rowspec,
            rowspec,
            rowspec,
            pl.BlockSpec((group, 1, cols), lambda i, *_: (i, 0, 0)),
            whole(weights.shape),
            pl.BlockSpec((block, 1), lambda i, *_: (i, 0)),
            pl.BlockSpec((group, 1, page), lambda i, *_: (i, 0, 0)),
        ],
        pl.BlockSpec(
            (2, 1, 1, 2, block, width // 4), lambda i, l, r: (0, i % 2, (i // 2) ^ r[1], 0, 0, 0)
        ),
        jax.ShapeDtypeStruct((2, 2, 2, 2, block, width // 4), BF),
        scratch=[pltpu.VMEM((heads, HEAD, HEAD), F32)],
        prefetch=2,
        cost=(2 * rows * cols * width, rows * width * 2),
    )(last, ids, *earlier, qs, ks, v, fin, weights, cnt_col, cnt_row)


def add(a, b):
    return (a.astype(F32) + b.astype(F32)).astype(BF)


def sum_scatter(terms):
    total = add(terms[0], mp_perm(terms[1], 1))
    a_first = add(total[0, 0], rep_perm(total[0, 1]))
    b_first = add(total[1, :, 0], mp_perm(total[1, :, 1], 2))
    a = a_first[0].astype(F32) + mp_perm(a_first[1], 2).astype(F32)
    b = b_first[0].astype(F32) + rep_perm(b_first[1]).astype(F32)
    return jnp.concatenate([a, b], axis=0)


def gather_plane(value):
    half = value.shape[0] // 2
    a, b = value[:half], value[half:]
    a_y, b_x = mp_perm(a, 2), rep_perm(b)
    a_pair, b_pair = jnp.stack([a, a_y]), jnp.stack([b, b_x])
    a_x, b_y = rep_perm(a_pair), mp_perm(b_pair, 2)
    mine = jnp.stack([jnp.stack([a_pair, a_x]), jnp.stack([b_pair, b_y], axis=1)])
    return mine, mp_perm(mine, 1)


def feed_forward(ids, mine, other, gain, weights, full):
    rows, kwide = mine.shape[-2:]
    total = weights.shape[2]
    gu = 2 * full + 128

    def body(ids_ref, m_ref, o_ref, g_ref, w_ref, out_ref):
        mp_index = ids_ref[0]
        places = [(dy, dc) for dy in range(2) for dc in range(2)]
        blocks = [(m_ref, o_ref)[dc][0, 0, dy].astype(F32) for dy, dc in places]
        square = sum(jnp.sum(b * b, axis=-1, keepdims=True) for b in blocks)
        scale = lax.rsqrt(square / (4 * kwide) + EPS)
        h = None
        for (dy, dc), b in zip(places, blocks):
            k = mp_index ^ (2 * dy + dc)
            x = (b * scale * g_ref[k]).astype(BF)
            term = nn(x, w_ref[k, :, 0:gu])
            h = term if h is None else h + term
        gate, up = h[:, 0:full], h[:, full + 128 : gu]
        edge = h[:, full : full + 128]
        hidden = gate * sigmoid(gate) * up
        mixed = edge * sigmoid(edge) * pltpu.roll(edge, 64, 1)
        lane = lax.broadcasted_iota(jnp.int32, mixed.shape, 1)
        mixed = jnp.where(lane < 64, mixed, 0.0)
        hidden = jnp.concatenate([hidden, mixed], axis=1).astype(BF)
        for dy, dc in places:
            k = mp_index ^ (2 * dy + dc)
            out_ref[dc, 0, 0, dy] = nt(hidden, w_ref[k, :, gu:total]).astype(BF)

    spec = pl.BlockSpec((1, 1, 2, rows, kwide), lambda i, r: (i % 2, i // 2, 0, 0, 0))
    return call(
        body,
        (4,),
        [spec, spec, whole(gain.shape), whole(weights.shape)],
        pl.BlockSpec((2, 1, 1, 2, rows, kwide), lambda i, r: (0, i % 2, i // 2, 0, 0, 0)),
        jax.ShapeDtypeStruct((2, 2, 2, 2, rows, kwide), BF),
        cost=(2 * 4 * rows * 4 * kwide * total, 4 * kwide * total * 2 + 32 * rows * kwide * 2),
    )(ids, mine, other, gain, weights)


def shards(
    token_pages,
    page_table,
    live_flags,
    lengths,
    decay_floor,
    mixer_gain,
    feed_gain,
    trainer_mixer_in,
    trainer_mixer_out,
    trainer_gate_up,
    trainer_down,
):
    ctx_count = lax.axis_size("ctx")
    ctx_index = lax.axis_index("ctx")
    mp_index = lax.axis_index("mp")
    rep_index = lax.axis_index("rep")
    ids = jnp.stack([mp_index, rep_index]).astype(jnp.int32)
    pages, page, width = token_pages.shape
    rows = pages * page
    cols = decay_floor.shape[0]
    kwide = width // 4
    full, _ = feed_sizes(trainer_gate_up.shape[2])

    packed_mixer = pack_mixer(ids, trainer_mixer_in, trainer_mixer_out)
    plane_mixer = across_plane(packed_mixer, mp_index)
    w_mixer = along_line(plane_mixer, ctx_index, ctx_count).reshape(width, 4 * cols)

    packed_feed = pack_feed(ids, trainer_gate_up, trainer_down)
    plane_feed = across_plane(packed_feed, mp_index)
    w_feed = lax.all_gather(plane_feed, "ctx", axis=0, tiled=True).reshape(4, kwide, -1)

    page_live = live_flags * page
    live_total = jnp.broadcast_to(jnp.sum(page_live), (8, 128)).astype(jnp.int32)
    base = sum(part[0, 0] for part in from_earlier(live_total, ctx_count))
    page_start = base + jnp.cumsum(page_live) - page_live
    positions = (page_start[:, None] + jnp.arange(page, dtype=jnp.int32)[None, :]).reshape(rows)
    starts = jnp.cumsum(lengths) - lengths
    live_tokens = jnp.repeat(live_flags, page)
    resets = (live_tokens == 1) & jnp.any(positions[:, None] == starts[None, :], axis=1)
    count = jnp.cumsum(resets.astype(jnp.int32))
    cnt_col = count.reshape(rows, 1)
    cnt_row = count.reshape(pages, 1, page)
    last = count.reshape(pages, page)[:, -1]

    normed = normalise(page_table, token_pages, mixer_gain)
    half_pages = pages // 2
    table_half = lax.dynamic_slice_in_dim(page_table, rep_index * half_pages, half_pages, 0)
    token_cols = lax.dynamic_slice_in_dim(token_pages, mp_index * kwide, kwide, 2)
    ordered = jnp.take(token_cols, table_half, axis=0).reshape(rows // 2, kwide)

    qs, ks, v, fin, pack = project(
        live_flags, last, normed, w_mixer, decay_floor.reshape(1, cols), cnt_col
    )
    earlier = from_earlier(pack, ctx_count)
    terms = mix(
        last, ids, earlier, qs, ks, v, fin, w_mixer.reshape(4, kwide, 4 * cols), cnt_col, cnt_row
    )
    residual = ordered.astype(F32) + sum_scatter(terms)
    mine, other = gather_plane(residual.astype(BF))
    down_terms = feed_forward(ids, mine, other, feed_gain.reshape(4, 1, kwide), w_feed, full)
    summed = residual + sum_scatter(down_terms)
    live_half = lax.dynamic_slice_in_dim(live_tokens, rep_index * (rows // 2), rows // 2, 0)
    return jnp.where(live_half[:, None] == 1, summed, 0.0).astype(BF)


def solution(mesh):
    in_specs = (
        P("ctx", None, None),
        P("ctx"),
        P("ctx"),
        P(),
        P(("mp", "rep")),
        P(),
        P(),
        P(None, ("ctx", "mp"), None),
        P(None, ("ctx", "mp")),
        P(None, ("ctx", "mp"), None),
        P(None, ("ctx", "mp")),
    )
    out_specs = P(("ctx", "rep"), "mp")
    return jax.shard_map(shards, mesh=mesh, in_specs=in_specs, out_specs=out_specs, check_vma=False)
```

time: 764 us -> 403 us (0.53)
  waiting for transfers between devices: 410 us -> 222 us
  local copies, waits for them, and re-layouts: 137 us -> 39 us
  blocking collectives: 96.6 us -> 0 us
  starting transfers between devices: 0.09 us -> 68.7 us
  Pallas kernels: 0 us -> 47 us
  matrix products: 42.6 us -> 0 us
  other arithmetic: 48.2 us -> 9.35 us
  loops' own time: 13.1 us -> 0 us
    all_gather x1, waiting for transfers between devices: 335 us -> 0.01 us  [shards(): lax.all_gather(plane_feed, 'ctx', axis=0, tiled=True).reshape(4, kwide, -1)]
    ppermute x0 -> x33, waiting for transfers between devices: none -> 222 us  [the longest x3 112 us: along_line(): high = lax.ppermute(high, 'ctx', [(i + 1, i) for i in range(count - 1)])]
    ppermute x0 -> x33, starting transfers between devices: none -> 68.7 us  [the longest x3 30.7 us: along_line(): low = lax.ppermute(low, 'ctx', [(i, i + 1) for i in range(count - 1)])]
    all_to_all x1 -> x0, blocking collectives: 65 us -> none  [shards(): lax.all_to_all(packed, 'mp', split_axis=1, concat_axis=0, tiled=True)]
    pallas_call x0 -> x6, Pallas kernels: none -> 47 us  [the longest x1 16.8 us: feed_forward(): call(body, (4,), [spec, spec, whole(gain.shape), whole(weights.shape)], p...]
    psum x1 -> x0, waiting for transfers between devices: 43.5 us -> none  [shards(): lax.psum(attn_term.astype(jnp.bfloat16), ('mp', 'rep')).astype(jnp.float32)]
    dot_general x37 -> x0, matrix products: 42.6 us -> none  [the longest x1 11.2 us: shards(): jnp.einsum('td,dcf->tcf', feed_in, feed_weights[:, :2], preferred_element...]
    slice x12 -> x8, local copies, waits for them, and re-layouts: 42.5 us -> 9.24 us  [the longest x2 4.98 us: sum_scatter(): total = add(terms[0], mp_perm(terms[1], 1))]
  transfers between devices with their start and end apart: 3 -> 34, of which waited for: 3 -> 24; matrix products, arithmetic and copies ran while one was open for 7% -> 7% of each run, Pallas kernels for 0% -> 7%
where the time goes in v1:
time: 403 us; the launch traced here: 402 us
  waiting for transfers between devices  222 us (55%)
  starting transfers between devices  68.7 us (17%)
  Pallas kernels  47 us (12%)
  local copies, waits for them, and re-layouts  39 us (10%)
  between operations  15.9 us (4%)
  other arithmetic  9.35 us (2%)
    ppermute x3, waiting for transfers between devices, along_line(): high = lax.ppermute(high, 'ctx', [(i + 1, i) for i in range(count - 1)])  112 us
    ppermute x15, waiting for transfers between devices, mp_perm(): return lax.ppermute(value, 'mp', [(i, i ^ s) for i in range(4)])  47.4 us
    ppermute x6, waiting for transfers between devices, rep_perm(): return lax.ppermute(value, 'rep', [(0, 1), (1, 0)])  35 us
    ppermute x3, starting transfers between devices, along_line(): low = lax.ppermute(low, 'ctx', [(i, i + 1) for i in range(count - 1)])  30.7 us
    ppermute x3, waiting for transfers between devices, along_line(): low = lax.ppermute(low, 'ctx', [(i, i + 1) for i in range(count - 1)])  25.6 us
    ppermute x6, starting transfers between devices, from_earlier(): lax.ppermute(value, 'ctx', [(i, i + d) for i in range(count - d)])  17.1 us
    pallas_call x1, Pallas kernels, feed_forward(): call(body, (4,), [spec, spec, whole(gain.shape), whole(weights.shape)], p...  16.8 us
    ppermute x15, starting transfers between devices, mp_perm(): return lax.ppermute(value, 'mp', [(i, i ^ s) for i in range(4)])  11.8 us
  transfers between devices with their start and end apart: 34, of which 24 were waited for; matrix products, arithmetic and copies ran while one was open for 7% of the time, Pallas kernels for 7%

profile of v1, /device:TPU:0, one launch (start us, length us, event | category | flops | bytes accessed | tf_op | source)
XLA Modules:
  0.0 401.9 jit_solution(18073147270794744586)
XLA Ops:
  28.7 4.5 %collective-permute-start.6 = (bf16[512,1024]{1,0:T(8,128)(2,1)S(1)}, bf16[512,1024]{1,0:T(8,128)(2,1)}, u32[]{:S(2)}, u32[]{:S(2)}) collective-permute-start(bf16[512,1024]{1,0:T(8,128)(2,1)S(1)} %bitcast.171), channel_id=1, source_target_pairs={{0,8},{8,16},{16,24},{1,9},{9,17},{17,25},{2,10},{10,18},{18,26},{... | collective-permute-start | bytes 3145736 | tf_op jit(solution)/shard_map/ppermute | solution.py:162
  34.4 5.7 %collective-permute-done.26 = bf16[128,2176]{1,0:T(8,128)(2,1)} collective-permute-done((bf16[128,2176]{1,0:T(8,128)(2,1)}, bf16[128,2176]{1,0:T(8,128)(2,1)}, u32[]{:S(2)}, u32[]{:S(2)}) %collective-permute-start.26) | collective-permute-done | bytes 557088 | tf_op jit(solution)/shard_map/ppermute | solution.py:140
  41.2 10.4 %collective-permute-done.27 = bf16[128,2176]{1,0:T(8,128)(2,1)S(1)} collective-permute-done((bf16[128,2176]{1,0:T(8,128)(2,1)}, bf16[128,2176]{1,0:T(8,128)(2,1)S(1)}, u32[]{:S(2)}, u32[]{:S(2)}) %collective-permute-start.27) | collective-permute-done | bytes 557088 | tf_op jit(solution)/shard_map/ppermute | solution.py:140
  55.6 4.5 %collective-permute-start = (s32[8,128]{1,0:T(8,128)S(1)}, s32[8,128]{1,0:T(8,128)S(1)}, u32[]{:S(2)}, u32[]{:S(2)}) collective-permute-start(s32[8,128]{1,0:T(8,128)S(1)} %broadcast_in_dim.101), channel_id=1, source_target_pairs={{0,8},{8,16},{16,24},{1,9},{9,17},{17,25},{2,10},{10,18},{18,26},{... | collective-permute-start | bytes 12296 | tf_op jit(solution)/shard_map/ppermute | solution.py:171
  60.1 4.6 %collective-permute-start.1 = (s32[8,128]{1,0:T(8,128)S(1)}, s32[8,128]{1,0:T(8,128)S(1)}, u32[]{:S(2)}, u32[]{:S(2)}) collective-permute-start(s32[8,128]{1,0:T(8,128)S(1)} %broadcast_in_dim.101), channel_id=1, source_target_pairs={{0,16},{8,24},{1,17},{9,25},{2,18},{10,26},{3,19},{11,27},{4,20},{... | collective-permute-start | bytes 12296 | tf_op jit(solution)/shard_map/ppermute | solution.py:171
  66.5 6.1 %shard_map.109.x_ref = bf16[1024,2048]{1,0:T(8,128)(2,1)S(1)} custom-call(s32[8]{0:T(128)S(1)} %copy-done.5, bf16[8,128,2048]{2,1,0:T(8,128)(2,1)} %x_ref.1, f32[1,2048]{1,0:T(1,128)S(1)} %bitcast.166), custom_call_target="tpu_custom_call" | custom-call | flops 8388608 | bytes 8388608 | tf_op jit(solution)/shard_map/pallas_call | solution.py:183
  80.6 26.6 %collective-permute-done.7 = bf16[512,1024]{1,0:T(8,128)(2,1)S(1)} collective-permute-done((bf16[512,1024]{1,0:T(8,128)(2,1)S(1)}, bf16[512,1024]{1,0:T(8,128)(2,1)S(1)}, u32[]{:S(2)}, u32[]{:S(2)}) %collective-permute-start.7) | collective-permute-done | bytes 1048608 | tf_op jit(solution)/shard_map/ppermute | solution.py:163
  111.0 14.4 %collective-permute-done.8 = bf16[512,1024]{1,0:T(8,128)(2,1)} collective-permute-done((bf16[512,1024]{1,0:T(8,128)(2,1)}, bf16[512,1024]{1,0:T(8,128)(2,1)}, u32[]{:S(2)}, u32[]{:S(2)}) %collective-permute-start.8) | collective-permute-done | bytes 1048608 | tf_op jit(solution)/shard_map/ppermute | solution.py:162
  125.4 23.9 %collective-permute-start.10 = (bf16[512,1024]{1,0:T(8,128)(2,1)}, bf16[512,1024]{1,0:T(8,128)(2,1)S(1)}, u32[]{:S(2)}, u32[]{:S(2)}) collective-permute-start(bf16[512,1024]{1,0:T(8,128)(2,1)} %collective-permute-done.8), channel_id=1, source_target_pairs={{0,8},{8,16},{16,24},{1,9},{9,17},{17,25},{2,10},{10,18},{18,26},{... | collective-permute-start | bytes 3145736 | tf_op jit(solution)/shard_map/ppermute | solution.py:162
  150.7 29.3 %collective-permute-done.9 = bf16[512,1024]{1,0:T(8,128)(2,1)} collective-permute-done((bf16[512,1024]{1,0:T(8,128)(2,1)S(1)}, bf16[512,1024]{1,0:T(8,128)(2,1)}, u32[]{:S(2)}, u32[]{:S(2)}) %collective-permute-start.9) | collective-permute-done | bytes 1048608 | tf_op jit(solution)/shard_map/ppermute | solution.py:163
  184.0 11.2 %collective-permute-done.10 = bf16[512,1024]{1,0:T(8,128)(2,1)S(1)} collective-permute-done((bf16[512,1024]{1,0:T(8,128)(2,1)}, bf16[512,1024]{1,0:T(8,128)(2,1)S(1)}, u32[]{:S(2)}, u32[]{:S(2)}) %collective-permute-start.10) | collective-permute-done | bytes 1048608 | tf_op jit(solution)/shard_map/ppermute | solution.py:162
  195.4 56.4 %collective-permute-done.11 = bf16[512,1024]{1,0:T(8,128)(2,1)S(1)} collective-permute-done((bf16[512,1024]{1,0:T(8,128)(2,1)}, bf16[512,1024]{1,0:T(8,128)(2,1)S(1)}, u32[]{:S(2)}, u32[]{:S(2)}) %collective-permute-start.11) | collective-permute-done | bytes 1048608 | tf_op jit(solution)/shard_map/ppermute | solution.py:163
  254.3 10.4 %shard_map.111 = (bf16[1024,256]{1,0:T(8,128)(2,1)S(1)}, bf16[1024,256]{1,0:T(8,128)(2,1)S(1)}, bf16[1024,256]{1,0:T(8,128)(2,1)S(1)}, f32[8,1,256]{2,1,0:T(1,128)S(1)}, bf16[2,144,128]{2,1,0:T(8,128)(2,1)S(1)}) custom-call(s32[8]{0:T(128)S(1)} %copy-done.6, s32[8]{0:T(128)S(1)} %slice_reduce_fusion.1.last_ref, bf16[1024,2048]{1,0:T(8,128)(2,1)} %copy-done.2, ...), custom_call_target="tpu_custom_call" | custom-call | flops 3221225472 | bytes 8388608 | tf_op jit(solution)/shard_map/pallas_call | solution.py:259
  273.2 8.9 %shard_map.112 = bf16[2,2,2,2,256,512]{5,4,3,2,1,0:T(8,128)(2,1)} custom-call(s32[8]{0:T(128)S(1)} %slice_reduce_fusion.1.last_ref, s32[2]{0:T(128)S(1)} %pad_add_fusion.ids_ref, bf16[2,144,128]{2,1,0:T(8,128)(2,1)S(1)} %collective-permute-done.12.refs_0_, bf16[2,144,128]{2,1,0:T(8,128)(2,1)S(1)} %collective-permute-done.13.refs_1_, ...), custom_call_target="tpu_custom_call" | custom-call | flops 1073741824 | bytes 4194304 | tf_op jit(solution)/shard_map/pallas_call | solution.py:344
  284.8 4.1 %collective-permute-done.15 = bf16[2,2,2,256,512]{4,3,1,2,0:T(8,128)(2,1)S(1)} collective-permute-done((bf16[2,2,2,256,512]{4,3,1,2,0:T(8,128)(2,1)S(1)}, bf16[2,2,2,256,512]{4,3,1,2,0:T(8,128)(2,1)S(1)}, u32[]{:S(2)}, u32[]{:S(2)}) %collective-permute-start.15) | collective-permute-done | bytes 2097184 | tf_op jit(solution)/shard_map/ppermute | solution.py:140
  295.7 9.8 %collective-permute-done.16 = bf16[2,256,512]{2,1,0:T(8,128)(2,1)} collective-permute-done((bf16[2,256,512]{2,1,0:T(8,128)(2,1)}, bf16[2,256,512]{2,1,0:T(8,128)(2,1)}, u32[]{:S(2)}, u32[]{:S(2)}) %collective-permute-start.16) | collective-permute-done | bytes 524320 | tf_op jit(solution)/shard_map/ppermute | solution.py:144
  311.1 4.5 %collective-permute-done.17 = bf16[256,512]{1,0:T(8,128)(2,1)} collective-permute-done((bf16[256,512]{1,0:T(8,128)(2,1)S(1)}, bf16[256,512]{1,0:T(8,128)(2,1)}, u32[]{:S(2)}, u32[]{:S(2)}) %collective-permute-start.17) | collective-permute-done | bytes 262176 | tf_op jit(solution)/shard_map/ppermute | solution.py:140
  319.3 4.3 %collective-permute-done.20 = bf16[256,512]{1,0:T(8,128)(2,1)S(1)} collective-permute-done((bf16[256,512]{1,0:T(8,128)(2,1)S(1)}, bf16[256,512]{1,0:T(8,128)(2,1)S(1)}, u32[]{:S(2)}, u32[]{:S(2)}) %collective-permute-start.20) | collective-permute-done | bytes 262176 | tf_op jit(solution)/shard_map/ppermute | solution.py:140
  327.1 9.2 %collective-permute-done.21 = bf16[2,256,512]{2,1,0:T(8,128)(2,1)S(1)} collective-permute-done((bf16[2,256,512]{2,1,0:T(8,128)(2,1)S(1)}, bf16[2,256,512]{2,1,0:T(8,128)(2,1)S(1)}, u32[]{:S(2)}, u32[]{:S(2)}) %collective-permute-start.21) | collective-permute-done | bytes 524320 | tf_op jit(solution)/shard_map/ppermute | solution.py:144
  336.8 4.1 %collective-permute-done.24.o_ref = bf16[2,2,2,256,512]{4,3,2,1,0:T(8,128)(2,1)S(1)} collective-permute-done((bf16[2,2,2,256,512]{4,3,2,1,0:T(8,128)(2,1)S(1)}, bf16[2,2,2,256,512]{4,3,2,1,0:T(8,128)(2,1)S(1)}, u32[]{:S(2)}, u32[]{:S(2)}) %collective-permute-start.24) | collective-permute-done | bytes 2097184 | tf_op jit(solution)/shard_map/ppermute | solution.py:140
  343.9 16.8 %shard_map.114 = bf16[2,2,2,2,256,512]{5,4,3,2,1,0:T(8,128)(2,1)} custom-call(s32[2]{0:T(128)S(1)} %pad_add_fusion.ids_ref, bf16[2,2,2,256,512]{4,3,2,1,0:T(8,128)(2,1)S(1)} %pad_maximum_fusion.m_ref, bf16[2,2,2,256,512]{4,3,2,1,0:T(8,128)(2,1)S(1)} %copy-done.8, f32[4,1,512]{2,1,0:T(1,128)S(1)} %bitcast.167, bf16[4,512,2176]{2,1,0:T(8,128)(2,1)} %bitcast.183), custom_call_target="tpu_custom_call" | custom-call | flops 9126805504 | bytes 17301504 | tf_op jit(solution)/shard_map/pallas_call | solution.py:419
  363.5 4.0 %collective-permute-done.28 = bf16[2,2,2,256,512]{4,3,1,2,0:T(8,128)(2,1)S(1)} collective-permute-done((bf16[2,2,2,256,512]{4,3,1,2,0:T(8,128)(2,1)S(1)}, bf16[2,2,2,256,512]{4,3,1,2,0:T(8,128)(2,1)S(1)}, u32[]{:S(2)}, u32[]{:S(2)}) %collective-permute-start.28) | collective-permute-done | bytes 2097184 | tf_op jit(solution)/shard_map/ppermute | solution.py:140
  371.4 12.8 %collective-permute-done.29 = bf16[2,256,512]{2,1,0:T(8,128)(2,1)} collective-permute-done((bf16[2,256,512]{2,1,0:T(8,128)(2,1)}, bf16[2,256,512]{2,1,0:T(8,128)(2,1)}, u32[]{:S(2)}, u32[]{:S(2)}) %collective-permute-start.29) | collective-permute-done | bytes 524320 | tf_op jit(solution)/shard_map/ppermute | solution.py:144
  388.3 5.0 %collective-permute-done.30 = bf16[256,512]{1,0:T(8,128)(2,1)S(1)} collective-permute-done((bf16[256,512]{1,0:T(8,128)(2,1)S(1)}, bf16[256,512]{1,0:T(8,128)(2,1)S(1)}, u32[]{:S(2)}, u32[]{:S(2)}) %collective-permute-start.30) | collective-permute-done | bytes 262176 | tf_op jit(solution)/shard_map/ppermute | solution.py:140
  (165 shorter events, 94.5 us)
Async XLA Ops:
  6.5 335.8 %all-gather.2.cloned.1.call-start = ((), (), s32[]{:S(2)}) async-start(), calls=%async_computation | async-start | bytes 11141120 | tf_op jit(solution)/shard_map/all_gather | solution.py:459
  12.1 10.1 %collective-permute-start.3 = (bf16[128,1024]{1,0:T(8,128)(2,1)}, bf16[128,1024]{1,0:T(8,128)(2,1)}, u32[]{:S(2)}, u32[]{:S(2)}) collective-permute-start(bf16[128,1024]{1,0:T(8,128)(2,1)} %get-tuple-element.31), channel_id=1, source_target_pairs={{0,2},{2,0},{4,6},{6,4},{1,3},{3,1},{5,7},{7,5},{8,10},{10,8},{12,... | collective-permute-start | bytes 786440 | tf_op jit(solution)/shard_map/ppermute | solution.py:140
  12.5 10.6 %collective-permute-start.4 = (bf16[128,1024]{1,0:T(8,128)(2,1)}, bf16[128,1024]{1,0:T(8,128)(2,1)}, u32[]{:S(2)}, u32[]{:S(2)}) collective-permute-start(bf16[128,1024]{1,0:T(8,128)(2,1)} %get-tuple-element.30), channel_id=1, source_target_pairs={{0,4},{2,6},{4,0},{6,2},{1,5},{3,7},{5,1},{7,3},{8,12},{10,14},{12... | collective-permute-start | bytes 786440 | tf_op jit(solution)/shard_map/ppermute | solution.py:140
  15.0 12.7 %collective-permute-start.5 = (bf16[128,1024]{1,0:T(8,128)(2,1)}, bf16[128,1024]{1,0:T(8,128)(2,1)}, u32[]{:S(2)}, u32[]{:S(2)}) collective-permute-start(bf16[128,1024]{1,0:T(8,128)(2,1)} %get-tuple-element.29), channel_id=1, source_target_pairs={{0,6},{2,4},{4,2},{6,0},{1,7},{3,5},{5,3},{7,1},{8,14},{10,12},{12... | collective-permute-start | bytes 786440 | tf_op jit(solution)/shard_map/ppermute | solution.py:140
  20.2 13.1 %collective-permute-start.25 = (bf16[128,2176]{1,0:T(8,128)(2,1)}, bf16[128,2176]{1,0:T(8,128)(2,1)}, u32[]{:S(2)}, u32[]{:S(2)}) collective-permute-start(bf16[128,2176]{1,0:T(8,128)(2,1)} %get-tuple-element.23), channel_id=1, source_target_pairs={{0,2},{2,0},{4,6},{6,4},{1,3},{3,1},{5,7},{7,5},{8,10},{10,8},{12,... | collective-permute-start | bytes 1671176 | tf_op jit(solution)/shard_map/ppermute | solution.py:140
  20.2 19.8 %collective-permute-start.26 = (bf16[128,2176]{1,0:T(8,128)(2,1)}, bf16[128,2176]{1,0:T(8,128)(2,1)}, u32[]{:S(2)}, u32[]{:S(2)}) collective-permute-start(bf16[128,2176]{1,0:T(8,128)(2,1)} %get-tuple-element.22), channel_id=1, source_target_pairs={{0,4},{2,6},{4,0},{6,2},{1,5},{3,7},{5,1},{7,3},{8,12},{10,14},{12... | collective-permute-start | bytes 1671176 | tf_op jit(solution)/shard_map/ppermute | solution.py:140
  22.2 29.4 %collective-permute-start.27 = (bf16[128,2176]{1,0:T(8,128)(2,1)}, bf16[128,2176]{1,0:T(8,128)(2,1)S(1)}, u32[]{:S(2)}, u32[]{:S(2)}) collective-permute-start(bf16[128,2176]{1,0:T(8,128)(2,1)} %get-tuple-element.21), channel_id=1, source_target_pairs={{0,6},{2,4},{4,2},{6,0},{1,7},{3,5},{5,3},{7,1},{8,14},{10,12},{12... | collective-permute-start | bytes 1671176 | tf_op jit(solution)/shard_map/ppermute | solution.py:140
  28.7 49.4 %collective-permute-start.6 = (bf16[512,1024]{1,0:T(8,128)(2,1)S(1)}, bf16[512,1024]{1,0:T(8,128)(2,1)}, u32[]{:S(2)}, u32[]{:S(2)}) collective-permute-start(bf16[512,1024]{1,0:T(8,128)(2,1)S(1)} %bitcast.171), channel_id=1, source_target_pairs={{0,8},{8,16},{16,24},{1,9},{9,17},{17,25},{2,10},{10,18},{18,26},{... | collective-permute-start | bytes 3145736 | tf_op jit(solution)/shard_map/ppermute | solution.py:162
  53.0 54.2 %collective-permute-start.7 = (bf16[512,1024]{1,0:T(8,128)(2,1)S(1)}, bf16[512,1024]{1,0:T(8,128)(2,1)S(1)}, u32[]{:S(2)}, u32[]{:S(2)}) collective-permute-start(bf16[512,1024]{1,0:T(8,128)(2,1)S(1)} %bitcast.172), channel_id=1, source_target_pairs={{8,0},{16,8},{24,16},{9,1},{17,9},{25,17},{10,2},{18,10},{26,18},{... | collective-permute-start | bytes 3145736 | tf_op jit(solution)/shard_map/ppermute | solution.py:163
  55.6 19.1 %collective-permute-start = (s32[8,128]{1,0:T(8,128)S(1)}, s32[8,128]{1,0:T(8,128)S(1)}, u32[]{:S(2)}, u32[]{:S(2)}) collective-permute-start(s32[8,128]{1,0:T(8,128)S(1)} %broadcast_in_dim.101), channel_id=1, source_target_pairs={{0,8},{8,16},{16,24},{1,9},{9,17},{17,25},{2,10},{10,18},{18,26},{... | collective-permute-start | bytes 12296 | tf_op jit(solution)/shard_map/ppermute | solution.py:171
  60.1 15.0 %collective-permute-start.1 = (s32[8,128]{1,0:T(8,128)S(1)}, s32[8,128]{1,0:T(8,128)S(1)}, u32[]{:S(2)}, u32[]{:S(2)}) collective-permute-start(s32[8,128]{1,0:T(8,128)S(1)} %broadcast_in_dim.101), channel_id=1, source_target_pairs={{0,16},{8,24},{1,17},{9,25},{2,18},{10,26},{3,19},{11,27},{4,20},{... | collective-permute-start | bytes 12296 | tf_op jit(solution)/shard_map/ppermute | solution.py:171
  64.7 12.2 %collective-permute-start.2 = (s32[8,128]{1,0:T(8,128)S(1)}, s32[8,128]{1,0:T(8,128)S(1)}, u32[]{:S(2)}, u32[]{:S(2)}) collective-permute-start(s32[8,128]{1,0:T(8,128)S(1)} %broadcast_in_dim.101), channel_id=1, source_target_pairs={{0,24},{1,25},{2,26},{3,27},{4,28},{5,29},{6,30},{7,31}} | collective-permute-start | bytes 12296 | tf_op jit(solution)/shard_map/ppermute | solution.py:171
  78.1 47.3 %collective-permute-start.8 = (bf16[512,1024]{1,0:T(8,128)(2,1)}, bf16[512,1024]{1,0:T(8,128)(2,1)}, u32[]{:S(2)}, u32[]{:S(2)}) collective-permute-start(bf16[512,1024]{1,0:T(8,128)(2,1)} %collective-permute-done.6), channel_id=1, source_target_pairs={{0,8},{8,16},{16,24},{1,9},{9,17},{17,25},{2,10},{10,18},{18,26},{... | collective-permute-start | bytes 3145736 | tf_op jit(solution)/shard_map/ppermute | solution.py:162
  107.2 72.7 %collective-permute-start.9 = (bf16[512,1024]{1,0:T(8,128)(2,1)S(1)}, bf16[512,1024]{1,0:T(8,128)(2,1)}, u32[]{:S(2)}, u32[]{:S(2)}) collective-permute-start(bf16[512,1024]{1,0:T(8,128)(2,1)S(1)} %collective-permute-done.7), channel_id=1, source_target_pairs={{8,0},{16,8},{24,16},{9,1},{17,9},{25,17},{10,2},{18,10},{26,18},{... | collective-permute-start | bytes 3145736 | tf_op jit(solution)/shard_map/ppermute | solution.py:163
  125.4 69.8 %collective-permute-start.10 = (bf16[512,1024]{1,0:T(8,128)(2,1)}, bf16[512,1024]{1,0:T(8,128)(2,1)S(1)}, u32[]{:S(2)}, u32[]{:S(2)}) collective-permute-start(bf16[512,1024]{1,0:T(8,128)(2,1)} %collective-permute-done.8), channel_id=1, source_target_pairs={{0,8},{8,16},{16,24},{1,9},{9,17},{17,25},{2,10},{10,18},{18,26},{... | collective-permute-start | bytes 3145736 | tf_op jit(solution)/shard_map/ppermute | solution.py:162
  179.9 71.8 %collective-permute-start.11 = (bf16[512,1024]{1,0:T(8,128)(2,1)}, bf16[512,1024]{1,0:T(8,128)(2,1)S(1)}, u32[]{:S(2)}, u32[]{:S(2)}) collective-permute-start(bf16[512,1024]{1,0:T(8,128)(2,1)} %collective-permute-done.9), channel_id=1, source_target_pairs={{8,0},{16,8},{24,16},{9,1},{17,9},{25,17},{10,2},{18,10},{26,18},{... | collective-permute-start | bytes 3145736 | tf_op jit(solution)/shard_map/ppermute | solution.py:163
  291.2 14.3 %collective-permute-start.16 = (bf16[2,256,512]{2,1,0:T(8,128)(2,1)}, bf16[2,256,512]{2,1,0:T(8,128)(2,1)}, u32[]{:S(2)}, u32[]{:S(2)}) collective-permute-start(bf16[2,256,512]{2,1,0:T(8,128)(2,1)} %slice_bitcast_fusion.9), channel_id=1, source_target_pairs={{0,1},{1,0},{2,3},{3,2},{4,5},{5,4},{6,7},{7,6},{8,9},{9,8},{10,11... | collective-permute-start | bytes 1572872 | tf_op jit(solution)/shard_map/ppermute | solution.py:144
  292.7 14.0 %collective-permute-start.18 = (bf16[2,256,512]{2,1,0:T(8,128)(2,1)}, bf16[2,256,512]{2,1,0:T(8,128)(2,1)}, u32[]{:S(2)}, u32[]{:S(2)}) collective-permute-start(bf16[2,256,512]{2,1,0:T(8,128)(2,1)} %slice_bitcast_fusion.7), channel_id=1, source_target_pairs={{0,4},{2,6},{4,0},{6,2},{1,5},{3,7},{5,1},{7,3},{8,12},{10,14},{12... | collective-permute-start | bytes 1572872 | tf_op jit(solution)/shard_map/ppermute | solution.py:140
  308.2 7.4 %collective-permute-start.17 = (bf16[256,512]{1,0:T(8,128)(2,1)S(1)}, bf16[256,512]{1,0:T(8,128)(2,1)}, u32[]{:S(2)}, u32[]{:S(2)}) collective-permute-start(bf16[256,512]{1,0:T(8,128)(2,1)S(1)} %slice_bitcast_fusion.17), channel_id=1, source_target_pairs={{0,4},{2,6},{4,0},{6,2},{1,5},{3,7},{5,1},{7,3},{8,12},{10,14},{12... | collective-permute-start | bytes 786440 | tf_op jit(solution)/shard_map/ppermute | solution.py:140
  318.7 8.3 %collective-permute-start.22 = (bf16[256,512]{1,0:T(8,128)(2,1)S(1)}, bf16[256,512]{1,0:T(8,128)(2,1)S(1)}, u32[]{:S(2)}, u32[]{:S(2)}) collective-permute-start(bf16[256,512]{1,0:T(8,128)(2,1)S(1)} %get-tuple-element.37), channel_id=1, source_target_pairs={{0,1},{1,0},{2,3},{3,2},{4,5},{5,4},{6,7},{7,6},{8,9},{9,8},{10,11... | collective-permute-start | bytes 786440 | tf_op jit(solution)/shard_map/ppermute | solution.py:144
  323.7 12.6 %collective-permute-start.21 = (bf16[2,256,512]{2,1,0:T(8,128)(2,1)S(1)}, bf16[2,256,512]{2,1,0:T(8,128)(2,1)S(1)}, u32[]{:S(2)}, u32[]{:S(2)}) collective-permute-start(bf16[2,256,512]{2,1,0:T(8,128)(2,1)S(1)} %get-tuple-element.34), channel_id=1, source_target_pairs={{0,1},{1,0},{2,3},{3,2},{4,5},{5,4},{6,7},{7,6},{8,9},{9,8},{10,11... | collective-permute-start | bytes 1572872 | tf_op jit(solution)/shard_map/ppermute | solution.py:144
  327.0 9.4 %collective-permute-start.23 = (bf16[2,256,512]{2,1,0:T(8,128)(2,1)S(1)}, bf16[2,256,512]{2,1,0:T(8,128)(2,1)S(1)}, u32[]{:S(2)}, u32[]{:S(2)}) collective-permute-start(bf16[2,256,512]{2,1,0:T(8,128)(2,1)S(1)} %get-tuple-element.40), channel_id=1, source_target_pairs={{0,4},{2,6},{4,0},{6,2},{1,5},{3,7},{5,1},{7,3},{8,12},{10,14},{12... | collective-permute-start | bytes 1572872 | tf_op jit(solution)/shard_map/ppermute | solution.py:140
  369.9 14.3 %collective-permute-start.29 = (bf16[2,256,512]{2,1,0:T(8,128)(2,1)}, bf16[2,256,512]{2,1,0:T(8,128)(2,1)}, u32[]{:S(2)}, u32[]{:S(2)}) collective-permute-start(bf16[2,256,512]{2,1,0:T(8,128)(2,1)} %slice_bitcast_fusion.5), channel_id=1, source_target_pairs={{0,1},{1,0},{2,3},{3,2},{4,5},{5,4},{6,7},{7,6},{8,9},{9,8},{10,11... | collective-permute-start | bytes 1572872 | tf_op jit(solution)/shard_map/ppermute | solution.py:144
  370.5 14.0 %collective-permute-start.31 = (bf16[2,256,512]{2,1,0:T(8,128)(2,1)}, bf16[2,256,512]{2,1,0:T(8,128)(2,1)}, u32[]{:S(2)}, u32[]{:S(2)}) collective-permute-start(bf16[2,256,512]{2,1,0:T(8,128)(2,1)} %slice_bitcast_fusion.3), channel_id=1, source_target_pairs={{0,4},{2,6},{4,0},{6,2},{1,5},{3,7},{5,1},{7,3},{8,12},{10,14},{12... | collective-permute-start | bytes 1572872 | tf_op jit(solution)/shard_map/ppermute | solution.py:140
  (28 other events, 216.5 us)
Sparse Core Ops, SparseCore 0:
  53.1 217.0 all-gather.1

commit v2 on v1

--- a/solution.py
+++ b/solution.py
@@ -12,6 +12,7 @@
 BF = jnp.bfloat16
 F32 = jnp.float32
 VMEM_LIMIT = 48 * 1024 * 1024
+FAR_TILES = 2
 
 
 def nt(a, b):
@@ -55,15 +56,19 @@
     return pl.BlockSpec(shape, lambda *_: zeros, pipeline_mode=pl.Buffered(1))
 
 
+def place(shape, index):
+    return pl.BlockSpec(shape, lambda *_: (index, 0, 0), pipeline_mode=pl.Buffered(1))
+
+
 def pack_mixer(ids, mixer_in, mixer_out):
     width = mixer_in.shape[1]
     cols = mixer_in.shape[2] // 8
 
-    def body(ids_ref, q_ref, f_ref, v_ref, o_ref, out_ref):
-        out_ref[0, :, 0:cols] = q_ref[0].astype(BF)
-        out_ref[0, :, cols : 2 * cols] = f_ref[0].astype(BF)
-        out_ref[0, :, 2 * cols : 3 * cols] = v_ref[0].astype(BF)
-        out_ref[0, :, 3 * cols : 4 * cols] = o_ref[...].T.astype(BF)
+    def body(ids_ref, q_ref, f_ref, v_ref, o_ref, in_ref, out_ref):
+        in_ref[0, :, 0:cols] = q_ref[0].astype(BF)
+        in_ref[0, :, cols : 2 * cols] = f_ref[0].astype(BF)
+        in_ref[0, :, 2 * cols : 3 * cols] = v_ref[0].astype(BF)
+        out_ref[0] = o_ref[...].T.astype(BF)
 
     def dest(s, ids_ref):
         return 2 * (ids_ref[0] ^ s) + ids_ref[1]
@@ -75,65 +80,93 @@
         body,
         (4,),
         [part(0), part(1), part(2), pl.BlockSpec((cols, width), lambda s, r: (dest(s, r), 0))],
-        pl.BlockSpec((1, width, 4 * cols), lambda s, r: (s, 0, 0)),
-        jax.ShapeDtypeStruct((4, width, 4 * cols), BF),
+        [
+            pl.BlockSpec((1, width, 3 * cols), lambda s, r: (s, 0, 0)),
+            pl.BlockSpec((1, width, cols), lambda s, r: (s, 0, 0)),
+        ],
+        [
+            jax.ShapeDtypeStruct((4, width, 3 * cols), BF),
+            jax.ShapeDtypeStruct((4, width, cols), BF),
+        ],
         cost=(0, 4 * width * cols * 24),
     )(ids, mixer_in, mixer_in, mixer_in, mixer_out)
 
 
-def feed_sizes(hidden_all):
-    full = hidden_all // 128 // 8 * 128
-    half = (hidden_all - 8 * full) // 8
-    return full, half
-
-
-def pack_feed(ids, gate_up, down):
+class Feed:
+    def __init__(self, hidden_all, far):
+        tiles = hidden_all // 128 // 8
+        self.half_at = 8 * tiles
+        assert hidden_all == (8 * tiles + 4) * 128
+        self.far, self.near = far * 128, (tiles - far) * 128
+        self.near_up = 2 * self.near + 128
+        self.near_all = self.near_up + self.near + 128
+        self.far_all = 3 * self.far
+
+
+def pack_feed(ids, gate_up, down, feed):
     width = gate_up.shape[1]
-    full, half = feed_sizes(gate_up.shape[2])
-    assert half == 64
-    gu = 2 * full + 128
-    total = gu + full + 128
-
-    def body(ids_ref, g_ref, u_ref, gh_ref, uh_ref, d_ref, dh_ref, out_ref):
+    near, far, up, both = feed.near, feed.far, feed.near_up, feed.near_all
+    total = both + feed.far_all
+
+    def body(ids_ref, *refs):
+        g_ref, u_ref, gh_ref, uh_ref, d_ref, dh_ref = refs[:6]
+        out_ref = refs[-1]
         odd = (ids_ref[0] ^ pl.program_id(0)) % 2
-        out_ref[0, :, 0:full] = g_ref[0].astype(BF)
+        out_ref[0, :, 0:near] = g_ref[0].astype(BF)
         lane = lax.broadcasted_iota(jnp.int32, (width, 128), 1)
         gh, uh = gh_ref[0], uh_ref[0]
         even_mix = jnp.where(lane < 64, gh, pltpu.roll(uh, 64, 1))
         odd_mix = jnp.where(lane < 64, pltpu.roll(gh, 64, 1), uh)
-        out_ref[0, :, full : full + 128] = jnp.where(odd == 1, odd_mix, even_mix).astype(BF)
-        out_ref[0, :, full + 128 : gu] = u_ref[0].astype(BF)
-        out_ref[0, :, gu : gu + full] = d_ref[...].T.astype(BF)
+        out_ref[0, :, near : near + 128] = jnp.where(odd == 1, odd_mix, even_mix).astype(BF)
+        out_ref[0, :, near + 128 : up] = u_ref[0].astype(BF)
+        out_ref[0, :, up : up + near] = d_ref[...].T.astype(BF)
         last = jnp.concatenate([dh_ref[...], jnp.zeros((64, width), F32)], axis=0)
-        out_ref[0, :, gu + full : total] = last.T.astype(BF)
+        out_ref[0, :, up + near : both] = last.T.astype(BF)
+        if far:
+            fg_ref, fu_ref, fd_ref = refs[6:9]
+            out_ref[0, :, both : both + far] = fg_ref[0].astype(BF)
+            out_ref[0, :, both + far : both + 2 * far] = fu_ref[0].astype(BF)
+            out_ref[0, :, both + 2 * far : total] = fd_ref[...].T.astype(BF)
 
     def dest(s, r):
         return 4 * r[1] + (r[0] ^ s)
 
     def tile(s, r):
-        return 8 * full // 128 + 2 * r[1] + (r[0] ^ s) // 2
+        return feed.half_at + 2 * r[1] + (r[0] ^ s) // 2
+
+    skip = 8 * near // far if far else 0
+    assert skip * far == (8 * near if far else 0)
 
     def cols(i):
-        return pl.BlockSpec((1, width, full), lambda s, r: (i, 0, dest(s, r)))
+        return pl.BlockSpec((1, width, near), lambda s, r: (i, 0, dest(s, r)))
 
     def mix(i):
         return pl.BlockSpec((1, width, 128), lambda s, r: (i, 0, tile(s, r)))
 
+    in_specs = [
+        cols(0),
+        cols(1),
+        mix(0),
+        mix(1),
+        pl.BlockSpec((near, width), lambda s, r: (dest(s, r), 0)),
+        pl.BlockSpec((64, width), lambda s, r: (2 * feed.half_at + dest(s, r), 0)),
+    ]
+    args = [gate_up, gate_up, gate_up, gate_up, down, down]
+    if far:
+        in_specs += [
+            pl.BlockSpec((1, width, far), lambda s, r: (0, 0, skip + dest(s, r))),
+            pl.BlockSpec((1, width, far), lambda s, r: (1, 0, skip + dest(s, r))),
+            pl.BlockSpec((far, width), lambda s, r: (skip + dest(s, r), 0)),
+        ]
+        args += [gate_up, gate_up, down]
     return call(
         body,
         (4,),
-        [
-            cols(0),
-            cols(1),
-            mix(0),
-            mix(1),
-            pl.BlockSpec((full, width), lambda s, r: (dest(s, r), 0)),
-            pl.BlockSpec((64, width), lambda s, r: (8 * full // 64 + dest(s, r), 0)),
-        ],
+        in_specs,
         pl.BlockSpec((1, width, total), lambda s, r: (s, 0, 0)),
         jax.ShapeDtypeStruct((4, width, total), BF),
         cost=(0, 4 * width * total * 6),
-    )(ids, gate_up, gate_up, gate_up, gate_up, down, down)
+    )(ids, *args)
 
 
 def mp_perm(value, s):
@@ -144,26 +177,33 @@
     return lax.ppermute(value, "rep", [(0, 1), (1, 0)])
 
 
-def across_plane(packed, mp_index):
+def across_plane(packed, mp_index, cuts):
     arrived = [packed[0]] + [mp_perm(packed[s], s) for s in (1, 2, 3)]
-    out = jnp.zeros(packed.shape, packed.dtype)
-    for s in range(4):
-        out = lax.dynamic_update_index_in_dim(out, arrived[s], mp_index ^ s, 0)
-    return out.reshape(4 * packed.shape[1], packed.shape[2])
+    outs = []
+    for low, high in zip(cuts[:-1], cuts[1:]):
+        out = jnp.zeros((4, packed.shape[1], high - low), packed.dtype)
+        for s in range(4):
+            out = lax.dynamic_update_index_in_dim(out, arrived[s][:, low:high], mp_index ^ s, 0)
+        outs.append(out.reshape(4 * packed.shape[1], high - low))
+    return outs, arrived[1:]
 
 
 def along_line(block, ctx_index, count):
-    if count != 4:
-        return lax.all_gather(block, "ctx", axis=0)
     out = jnp.zeros((3 * count - 2, *block.shape), block.dtype)
     out = lax.dynamic_update_index_in_dim(out, block, ctx_index + count - 1, 0)
     low = high = block
+    steps = []
     for d in range(1, count):
         low = lax.ppermute(low, "ctx", [(i, i + 1) for i in range(count - 1)])
         high = lax.ppermute(high, "ctx", [(i + 1, i) for i in range(count - 1)])
+        steps.append((low, high))
         out = lax.dynamic_update_index_in_dim(out, low, ctx_index - d + count - 1, 0)
         out = lax.dynamic_update_index_in_dim(out, high, ctx_index + d + count - 1, 0)
-    return out[count - 1 : 2 * count - 1]
+    return out, steps
+
+
+def after(value, *others):
+    return lax.optimization_barrier((value, *others))[0]
 
 
 def from_earlier(value, count):
@@ -195,7 +235,7 @@
     return (jnp.where(keep, state, 0.0) + update) * final
 
 
-def project(live, last, normed, weights, floor, cnt_col):
+def project(live, last, normed, weights, first, floor, cnt_col):
     rows, width = normed.shape
     cols = floor.shape[1]
     heads = cols // HEAD
@@ -203,8 +243,11 @@
     page = rows // pages
     group = 2
     steps = pages // group
-
-    def body(live_ref, last_ref, x_ref, w_ref, fl_ref, cnt_ref, qs_ref, ks_ref, v_ref, fin_ref, st_ref, state, total):
+    deep = width // 4
+
+    def body(live_ref, last_ref, x_ref, *refs):
+        w_refs = refs[:4]
+        fl_ref, cnt_ref, qs_ref, ks_ref, v_ref, fin_ref, st_ref, state, total = refs[4:]
         step = pl.program_id(0)
 
         @pl.when(step == 0)
@@ -212,7 +255,10 @@
             state[...] = jnp.zeros_like(state)
             total[...] = jnp.zeros_like(total)
 
-        proj = nn(x_ref[...], w_ref[:, 0 : 3 * cols])
+        proj = None
+        for k in range(4):
+            term = nn(x_ref[:, k * deep : (k + 1) * deep], w_refs[k][0])
+            proj = term if proj is None else proj + term
         row = lax.broadcasted_iota(jnp.int32, (page, page), 0)
         col = lax.broadcasted_iota(jnp.int32, (page, page), 1)
         lower = (row >= col).astype(F32)
@@ -261,7 +307,9 @@
         (steps,),
         [
             pl.BlockSpec((block, width), lambda i, *_: (i, 0)),
-            whole((width, weights.shape[1])),
+        ]
+        + [place((1, deep, 3 * cols), first + k) for k in range(4)]
+        + [
             whole((1, cols)),
             pl.BlockSpec((block, 1), lambda i, *_: (i, 0)),
         ],
@@ -282,10 +330,10 @@
         scratch=[pltpu.VMEM((heads, HEAD, HEAD), F32), pltpu.VMEM((1, cols), F32)],
         prefetch=2,
         cost=(2 * rows * width * 3 * cols, rows * width * 2 + width * cols * 8),
-    )(live, last, normed, weights, floor, cnt_col)
-
-
-def mix(last, ids, earlier, qs, ks, v, fin, weights, cnt_col, cnt_row):
+    )(live, last, normed, *[weights] * 4, floor, cnt_col)
+
+
+def mix(last, ids, earlier, qs, ks, v, fin, weights, first, cnt_col, cnt_row):
     rows, cols = qs.shape
     heads = cols // HEAD
     pages = fin.shape[0]
@@ -297,9 +345,10 @@
 
     def body(last_ref, ids_ref, *refs):
         packs = refs[:n]
-        qs_ref, ks_ref, v_ref, fin_ref, w_ref, cc_ref, cr_ref, out_ref, state = refs[n:]
+        qs_ref, ks_ref, v_ref, fin_ref = refs[n : n + 4]
+        w_refs = refs[n + 4 : n + 8]
+        cc_ref, cr_ref, out_ref, state = refs[n + 8 :]
         step = pl.program_id(0)
-        mp_index = ids_ref[0]
 
         @pl.when(step == 0)
         def _():
@@ -336,11 +385,18 @@
         )
         for dc in range(2):
             for dy in range(2):
-                w = w_ref[mp_index ^ (2 * dy + dc)]
-                out_ref[dc, 0, 0, dy] = nt(hn, w[:, 3 * cols : 4 * cols]).astype(BF)
+                out_ref[dc, 0, 0, dy] = nt(hn, w_refs[2 * dy + dc][0]).astype(BF)
 
     block = group * page
     rowspec = pl.BlockSpec((block, cols), lambda i, *_: (i, 0))
+
+    def by_mp(d):
+        return pl.BlockSpec(
+            (1, *weights.shape[1:]),
+            lambda i, l, r: (first + (r[0] ^ d), 0, 0),
+            pipeline_mode=pl.Buffered(1),
+        )
+
     return call(
         body,
         (steps,),
@@ -350,7 +406,9 @@
             rowspec,
             rowspec,
             pl.BlockSpec((group, 1, cols), lambda i, *_: (i, 0, 0)),
-            whole(weights.shape),
+        ]
+        + [by_mp(d) for d in range(4)]
+        + [
             pl.BlockSpec((block, 1), lambda i, *_: (i, 0)),
             pl.BlockSpec((group, 1, page), lambda i, *_: (i, 0, 0)),
         ],
@@ -361,7 +419,7 @@
         scratch=[pltpu.VMEM((heads, HEAD, HEAD), F32)],
         prefetch=2,
         cost=(2 * rows * cols * width, rows * width * 2),
-    )(last, ids, *earlier, qs, ks, v, fin, weights, cnt_col, cnt_row)
+    )(last, ids, *earlier, qs, ks, v, fin, *[weights] * 4, cnt_col, cnt_row)
 
 
 def add(a, b):
@@ -387,42 +445,85 @@
     return mine, mp_perm(mine, 1)
 
 
-def feed_forward(ids, mine, other, gain, weights, full):
+def feed_inputs(ids_ref, m_ref, o_ref, g_ref):
+    mp_index = ids_ref[0]
+    places = [(dy, dc) for dy in range(2) for dc in range(2)]
+    blocks = [(m_ref, o_ref)[dc][0, 0, dy].astype(F32) for dy, dc in places]
+    square = sum(jnp.sum(b * b, axis=-1, keepdims=True) for b in blocks)
+    scale = lax.rsqrt(square / (4 * blocks[0].shape[1]) + EPS)
+    at = [mp_index ^ (2 * dy + dc) for dy, dc in places]
+    return places, at, [(b * scale * g_ref[k]).astype(BF) for k, b in zip(at, blocks)]
+
+
+def total_of(terms):
+    out = None
+    for term in terms:
+        out = term if out is None else out + term
+    return out
+
+
+def feed_specs(mine, gain):
     rows, kwide = mine.shape[-2:]
-    total = weights.shape[2]
-    gu = 2 * full + 128
-
-    def body(ids_ref, m_ref, o_ref, g_ref, w_ref, out_ref):
-        mp_index = ids_ref[0]
-        places = [(dy, dc) for dy in range(2) for dc in range(2)]
-        blocks = [(m_ref, o_ref)[dc][0, 0, dy].astype(F32) for dy, dc in places]
-        square = sum(jnp.sum(b * b, axis=-1, keepdims=True) for b in blocks)
-        scale = lax.rsqrt(square / (4 * kwide) + EPS)
-        h = None
-        for (dy, dc), b in zip(places, blocks):
-            k = mp_index ^ (2 * dy + dc)
-            x = (b * scale * g_ref[k]).astype(BF)
-            term = nn(x, w_ref[k, :, 0:gu])
-            h = term if h is None else h + term
-        gate, up = h[:, 0:full], h[:, full + 128 : gu]
-        edge = h[:, full : full + 128]
-        hidden = gate * sigmoid(gate) * up
+    spec = pl.BlockSpec((1, 1, 2, rows, kwide), lambda i, r: (i % 2, i // 2, 0, 0, 0))
+    out_spec = pl.BlockSpec((2, 1, 1, 2, rows, kwide), lambda i, r: (0, i % 2, i // 2, 0, 0, 0))
+    return [spec, spec, whole(gain.shape)], out_spec, jax.ShapeDtypeStruct((2, 2, 2, 2, rows, kwide), BF)
+
+
+def feed_near(ids, mine, other, gain, weights, feed, extra=None):
+    near, up, both = feed.near, feed.near_up, feed.near_all
+    specs, out_spec, out_shape = feed_specs(mine, gain)
+
+    def body(ids_ref, m_ref, o_ref, g_ref, w_ref, *rest):
+        out_ref = rest[-1]
+        places, at, xs = feed_inputs(ids_ref, m_ref, o_ref, g_ref)
+        h = total_of(nn(x, w_ref[k, :, 0:up]) for k, x in zip(at, xs))
+        gate, upward = h[:, 0:near], h[:, near + 128 : up]
+        edge = h[:, near : near + 128]
+        hidden = gate * sigmoid(gate) * upward
         mixed = edge * sigmoid(edge) * pltpu.roll(edge, 64, 1)
         lane = lax.broadcasted_iota(jnp.int32, mixed.shape, 1)
         mixed = jnp.where(lane < 64, mixed, 0.0)
         hidden = jnp.concatenate([hidden, mixed], axis=1).astype(BF)
-        for dy, dc in places:
-            k = mp_index ^ (2 * dy + dc)
-            out_ref[dc, 0, 0, dy] = nt(hidden, w_ref[k, :, gu:total]).astype(BF)
-
-    spec = pl.BlockSpec((1, 1, 2, rows, kwide), lambda i, r: (i % 2, i // 2, 0, 0, 0))
+        for (dy, dc), k in zip(places, at):
+            term = nt(hidden, w_ref[k, :, up:both])
+            if extra is not None:
+                term = term + jnp.where(ids_ref[2] == 1, rest[0][dc, 0, 0, dy].astype(F32), 0.0)
+            out_ref[dc, 0, 0, dy] = term.astype(BF)
+
+    rows = out_shape.shape[-2] * 4
     return call(
         body,
         (4,),
-        [spec, spec, whole(gain.shape), whole(weights.shape)],
-        pl.BlockSpec((2, 1, 1, 2, rows, kwide), lambda i, r: (0, i % 2, i // 2, 0, 0, 0)),
-        jax.ShapeDtypeStruct((2, 2, 2, 2, rows, kwide), BF),
-        cost=(2 * 4 * rows * 4 * kwide * total, 4 * kwide * total * 2 + 32 * rows * kwide * 2),
+        specs + [whole(weights.shape)] + ([] if extra is None else [out_spec]),
+        out_spec,
+        out_shape,
+        cost=(2 * rows * weights.size, weights.size * 2 + 3 * out_shape.size * 2),
+    )(ids, mine, other, gain, weights, *([] if extra is None else [extra]))
+
+
+def feed_far(ids, mine, other, gain, weights, feed):
+    far = feed.far
+    specs, out_spec, out_shape = feed_specs(mine, gain)
+
+    def body(ids_ref, m_ref, o_ref, g_ref, w_ref, out_ref):
+        @pl.when(ids_ref[2] == 1)
+        def _():
+            places, at, xs = feed_inputs(ids_ref, m_ref, o_ref, g_ref)
+            where = [ids_ref[3 + k] for k in at]
+            h = total_of(nn(x, w_ref[k, :, 0 : 2 * far]) for k, x in zip(where, xs))
+            gate, upward = h[:, 0:far], h[:, far : 2 * far]
+            hidden = (gate * sigmoid(gate) * upward).astype(BF)
+            for (dy, dc), k in zip(places, where):
+                out_ref[dc, 0, 0, dy] = nt(hidden, w_ref[k, :, 2 * far : 3 * far]).astype(BF)
+
+    rows = out_shape.shape[-2] * 4
+    return call(
+        body,
+        (4,),
+        specs + [whole(weights.shape)],
+        out_spec,
+        out_shape,
+        cost=(2 * rows * weights.size, weights.size * 2 + 2 * out_shape.size * 2),
     )(ids, mine, other, gain, weights)
 
 
@@ -443,20 +544,43 @@
     ctx_index = lax.axis_index("ctx")
     mp_index = lax.axis_index("mp")
     rep_index = lax.axis_index("rep")
-    ids = jnp.stack([mp_index, rep_index]).astype(jnp.int32)
+    split = ctx_count == 4
+    middle = (ctx_index == 1) | (ctx_index == 2)
+    beyond = jnp.where(ctx_index == 1, 0, 3)
+    order = [
+        jnp.where(k == ctx_index, 0, 1) if k in (1, 2) else jnp.where(k == beyond, 2, 3) for k in range(4)
+    ]
+    ids = jnp.stack([mp_index, rep_index, middle.astype(jnp.int32), *order]).astype(jnp.int32)
     pages, page, width = token_pages.shape
     rows = pages * page
     cols = decay_floor.shape[0]
     kwide = width // 4
-    full, _ = feed_sizes(trainer_gate_up.shape[2])
-
-    packed_mixer = pack_mixer(ids, trainer_mixer_in, trainer_mixer_out)
-    plane_mixer = across_plane(packed_mixer, mp_index)
-    w_mixer = along_line(plane_mixer, ctx_index, ctx_count).reshape(width, 4 * cols)
-
-    packed_feed = pack_feed(ids, trainer_gate_up, trainer_down)
-    plane_feed = across_plane(packed_feed, mp_index)
-    w_feed = lax.all_gather(plane_feed, "ctx", axis=0, tiled=True).reshape(4, kwide, -1)
+    feed = Feed(trainer_gate_up.shape[2], FAR_TILES if split else 0)
+
+    packed_in, packed_out = pack_mixer(ids, trainer_mixer_in, trainer_mixer_out)
+    (plane_in,), moved = across_plane(packed_in, mp_index, (0, 3 * cols))
+    packed_feed = pack_feed(ids, trainer_gate_up, trainer_down, feed)
+    packed_out, packed_feed, *_ = lax.optimization_barrier((packed_out, packed_feed, *moved))
+    (plane_out,), _ = across_plane(packed_out, mp_index, (0, cols))
+    cuts = (0, feed.near_all, feed.near_all + feed.far_all)
+    plane_feed, _ = across_plane(packed_feed, mp_index, cuts if split else cuts[:2])
+    if split:
+        w_in, steps = along_line(plane_in, ctx_index, ctx_count)
+        w_out, _ = along_line(after(plane_out, *steps[2]), ctx_index, ctx_count)
+        first = ctx_count - 1
+        plane_near, plane_far = plane_feed
+        plane_far = after(plane_far, *steps[1])
+        across = lax.ppermute(plane_far, "ctx", [(1, 2), (2, 1)])
+        inward = lax.ppermute(plane_far, "ctx", [(0, 1), (3, 2)])
+        onward = lax.ppermute(inward, "ctx", [(1, 2), (2, 1)])
+        w_far = jnp.stack([plane_far, across, inward, onward])
+        plane_near = after(plane_near, *steps[1])
+    else:
+        w_in = lax.all_gather(plane_in, "ctx", axis=0, tiled=True).reshape(4, kwide, -1)
+        w_out = lax.all_gather(plane_out, "ctx", axis=0, tiled=True).reshape(4, kwide, -1)
+        first = 0
+        plane_near = plane_feed[0]
+    w_near = lax.all_gather(plane_near, "ctx", axis=0, tiled=True).reshape(4, kwide, -1)
 
     page_live = live_flags * page
     live_total = jnp.broadcast_to(jnp.sum(page_live), (8, 128)).astype(jnp.int32)
@@ -478,16 +602,25 @@
     ordered = jnp.take(token_cols, table_half, axis=0).reshape(rows // 2, kwide)
 
     qs, ks, v, fin, pack = project(
-        live_flags, last, normed, w_mixer, decay_floor.reshape(1, cols), cnt_col
+        live_flags, last, normed, w_in, first, decay_floor.reshape(1, cols), cnt_col
     )
     earlier = from_earlier(pack, ctx_count)
-    terms = mix(
-        last, ids, earlier, qs, ks, v, fin, w_mixer.reshape(4, kwide, 4 * cols), cnt_col, cnt_row
-    )
+    terms = mix(last, ids, earlier, qs, ks, v, fin, w_out, first, cnt_col, cnt_row)
     residual = ordered.astype(F32) + sum_scatter(terms)
-    mine, other = gather_plane(residual.astype(BF))
-    down_terms = feed_forward(ids, mine, other, feed_gain.reshape(4, 1, kwide), w_feed, full)
-    summed = residual + sum_scatter(down_terms)
+    value = residual.astype(BF)
+    gain = feed_gain.reshape(4, 1, kwide)
+    if split:
+        foreign = lax.ppermute(value, "ctx", [(0, 1), (3, 2)])
+        mine, other = gather_plane(value)
+        extra = feed_far(ids, mine, other, gain, w_far, feed)
+        theirs = gather_plane(foreign)
+        given = sum_scatter(feed_far(ids, *theirs, gain, w_far, feed))
+        back = lax.ppermute(given.astype(BF), "ctx", [(1, 0), (2, 3)])
+        down_terms = feed_near(ids, mine, other, gain, w_near, feed, extra)
+        summed = residual + sum_scatter(down_terms) + back.astype(F32)
+    else:
+        mine, other = gather_plane(value)
+        summed = residual + sum_scatter(feed_near(ids, mine, other, gain, w_near, feed))
     live_half = lax.dynamic_slice_in_dim(live_tokens, rep_index * (rows // 2), rows // 2, 0)
     return jnp.where(live_half[:, None] == 1, summed, 0.0).astype(BF)
 

time: 403 us -> 455 us (1.13); the launches traced: 402 us -> 449 us
  starting transfers between devices: 68.7 us -> 86.6 us
  other arithmetic: 9.35 us -> 26.5 us
  local copies, waits for them, and re-layouts: 39 us -> 53.2 us
  waiting for transfers between devices: 222 us -> 215 us
    ppermute x3 -> x6, waiting for transfers between devices: 112 us -> 14.9 us  [along_line(): high = lax.ppermute(high, 'ctx', [(i + 1, i) for i in range(count - 1)])]
    ppermute x0 -> x5, waiting for transfers between devices: none -> 73.3 us  [the longest x1 27.4 us: shards(): back = lax.ppermute(given.astype(BF), 'ctx', [(1, 0), (2, 3)])]
    ppermute x3 -> x6, waiting for transfers between devices: 25.6 us -> 42.5 us  [along_line(): low = lax.ppermute(low, 'ctx', [(i, i + 1) for i in range(count - 1)])]
    unnamed x38 -> x71, local copies, waits for them, and re-layouts: 9.79 us -> 23.1 us
    ppermute x3 -> x6, starting transfers between devices: 30.7 us -> 21.6 us  [along_line(): low = lax.ppermute(low, 'ctx', [(i, i + 1) for i in range(count - 1)])]
    ppermute x0 -> x5, starting transfers between devices: none -> 9.03 us  [the longest x1 4.56 us: shards(): inward = lax.ppermute(plane_far, 'ctx', [(0, 1), (3, 2)])]
    ppermute x15 -> x24, starting transfers between devices: 11.8 us -> 20.6 us  [mp_perm(): return lax.ppermute(value, 'mp', [(i, i ^ s) for i in range(4)])]
    ppermute x6 -> x10, waiting for transfers between devices: 35 us -> 43.2 us  [rep_perm(): return lax.ppermute(value, 'rep', [(0, 1), (1, 0)])]
  transfers between devices with their start and end apart: 34 -> 58, of which waited for: 24 -> 32; matrix products, arithmetic and copies ran while one was open for 7% -> 12% of each run, Pallas kernels for 7% -> 10%
where the time goes in v2:
time: 455 us; the launch traced here: 449 us
  waiting for transfers between devices  215 us (47%)
  starting transfers between devices  86.6 us (19%)
  local copies, waits for them, and re-layouts  53.2 us (12%)
  Pallas kernels  50.8 us (11%)
  other arithmetic  26.5 us (6%)
  between operations  16.5 us (4%)
    ppermute x10, waiting for transfers between devices, rep_perm(): return lax.ppermute(value, 'rep', [(0, 1), (1, 0)])  43.2 us
    ppermute x6, waiting for transfers between devices, along_line(): low = lax.ppermute(low, 'ctx', [(i, i + 1) for i in range(count - 1)])  42.5 us
    ppermute x24, waiting for transfers between devices, mp_perm(): return lax.ppermute(value, 'mp', [(i, i ^ s) for i in range(4)])  41.2 us
    ppermute x1, waiting for transfers between devices, shards(): back = lax.ppermute(given.astype(BF), 'ctx', [(1, 0), (2, 3)])  27.4 us
    ppermute x1, waiting for transfers between devices, shards(): inward = lax.ppermute(plane_far, 'ctx', [(0, 1), (3, 2)])  23.5 us
    unnamed x71, local copies, waits for them, and re-layouts  23.1 us
    ppermute x1, waiting for transfers between devices, shards(): foreign = lax.ppermute(value, 'ctx', [(0, 1), (3, 2)])  22.4 us
    ppermute x6, starting transfers between devices, along_line(): low = lax.ppermute(low, 'ctx', [(i, i + 1) for i in range(count - 1)])  21.6 us
  transfers between devices with their start and end apart: 58, of which 32 were waited for; matrix products, arithmetic and copies ran while one was open for 12% of the time, Pallas kernels for 10%

profile of v2, /device:TPU:0, one launch (start us, length us, event | category | flops | bytes accessed | tf_op | source)
XLA Modules:
  0.0 448.6 jit_solution(4802933149004052992)
XLA Ops:
  9.1 5.5 %collective-permute-start = (s32[8,128]{1,0:T(8,128)S(1)}, s32[8,128]{1,0:T(8,128)}, u32[]{:S(2)}, u32[]{:S(2)}) collective-permute-start(s32[8,128]{1,0:T(8,128)S(1)} %broadcast_in_dim.151), channel_id=1, source_target_pairs={{0,8},{8,16},{16,24},{1,9},{9,17},{17,25},{2,10},{10,18},{18,26},{... | collective-permute-start | bytes 12296 | tf_op jit(solution)/shard_map/ppermute | solution.py:211
  40.5 6.0 %shard_map.109.x_ref = bf16[1024,2048]{1,0:T(8,128)(2,1)S(1)} custom-call(s32[8]{0:T(128)S(1)} %copy-done.10, bf16[8,128,2048]{2,1,0:T(8,128)(2,1)} %x_ref.1, f32[1,2048]{1,0:T(1,128)S(1)} %bitcast.286), custom_call_target="tpu_custom_call" | custom-call | flops 8388608 | bytes 8388608 | tf_op jit(solution)/shard_map/pallas_call | solution.py:223
  62.0 12.3 %collective-permute-done.6 = bf16[512,768]{1,0:T(8,128)(2,1)S(1)} collective-permute-done((bf16[512,768]{1,0:T(8,128)(2,1)S(1)}, bf16[512,768]{1,0:T(8,128)(2,1)S(1)}, u32[]{:S(2)}, u32[]{:S(2)}) %collective-permute-start.6) | collective-permute-done | bytes 786464 | tf_op jit(solution)/shard_map/ppermute | solution.py:197
  80.2 15.2 %collective-permute-done.8 = bf16[512,768]{1,0:T(8,128)(2,1)S(1)} collective-permute-done((bf16[512,768]{1,0:T(8,128)(2,1)S(1)}, bf16[512,768]{1,0:T(8,128)(2,1)S(1)}, u32[]{:S(2)}, u32[]{:S(2)}) %collective-permute-start.8) | collective-permute-done | bytes 786464 | tf_op jit(solution)/shard_map/ppermute | solution.py:197
  101.4 14.3 %collective-permute-done.10 = bf16[512,768]{1,0:T(8,128)(2,1)S(1)} collective-permute-done((bf16[512,768]{1,0:T(8,128)(2,1)S(1)}, bf16[512,768]{1,0:T(8,128)(2,1)S(1)}, u32[]{:S(2)}, u32[]{:S(2)}) %collective-permute-start.10) | collective-permute-done | bytes 786464 | tf_op jit(solution)/shard_map/ppermute | solution.py:197
  125.6 9.9 %shard_map.111 = (bf16[1024,256]{1,0:T(8,128)(2,1)S(1)}, bf16[1024,256]{1,0:T(8,128)(2,1)S(1)}, bf16[1024,256]{1,0:T(8,128)(2,1)S(1)}, f32[8,1,256]{2,1,0:T(1,128)S(1)}, bf16[2,144,128]{2,1,0:T(8,128)(2,1)S(1)}) custom-call(s32[8]{0:T(128)S(1)} %copy-done.9, s32[8]{0:T(128)S(1)} %slice_reduce_fusion.1.last_ref, bf16[1024,2048]{1,0:T(8,128)(2,1)} %copy-done.2, ...), custom_call_target="tpu_custom_call" | custom-call | flops 3221225472 | bytes 8388608 | tf_op jit(solution)/shard_map/pallas_call | solution.py:305
  141.9 4.6 %collective-permute-start.20 = (bf16[512,256]{1,0:T(8,128)(2,1)S(1)}, bf16[512,256]{1,0:T(8,128)(2,1)S(1)}, u32[]{:S(2)}, u32[]{:S(2)}) collective-permute-start(bf16[512,256]{1,0:T(8,128)(2,1)S(1)} %collective-permute-done.18), channel_id=1, source_target_pairs={{0,8},{8,16},{16,24},{1,9},{9,17},{17,25},{2,10},{10,18},{18,26},{... | collective-permute-start | bytes 786440 | tf_op jit(solution)/shard_map/ppermute | solution.py:197
  158.6 6.5 %collective-permute-done.23 = bf16[512,256]{1,0:T(8,128)(2,1)S(1)} collective-permute-done((bf16[512,256]{1,0:T(8,128)(2,1)S(1)}, bf16[512,256]{1,0:T(8,128)(2,1)S(1)}, u32[]{:S(2)}, u32[]{:S(2)}) %collective-permute-start.23) | collective-permute-done | bytes 262176 | tf_op jit(solution)/shard_map/ppermute | solution.py:198
  165.2 6.7 %shard_map.113 = bf16[2,2,2,2,256,512]{5,4,3,2,1,0:T(8,128)(2,1)} custom-call(s32[8]{0:T(128)S(1)} %slice_reduce_fusion.1.last_ref, s32[7]{0:T(128)S(1)} %stack.140.ids_ref, bf16[2,144,128]{2,1,0:T(8,128)(2,1)S(1)} %collective-permute-done.12.refs_0_, bf16[2,144,128]{2,1,0:T(8,128)(2,1)S(1)} %collective-permute-done.13.refs_1_, ...), custom_call_target="tpu_custom_call" | custom-call | flops 1073741824 | bytes 4194304 | tf_op jit(solution)/shard_map/pallas_call | solution.py:400
  182.2 11.7 %collective-permute-done.35 = bf16[128,2176]{1,0:T(8,128)(2,1)S(1)} collective-permute-done((bf16[128,2176]{1,0:T(8,128)(2,1)S(1)}, bf16[128,2176]{1,0:T(8,128)(2,1)S(1)}, u32[]{:S(2)}, u32[]{:S(2)}) %collective-permute-start.35) | collective-permute-done | bytes 557088 | tf_op jit(solution)/shard_map/ppermute | solution.py:173
  193.9 11.0 %collective-permute-done.36 = bf16[128,2176]{1,0:T(8,128)(2,1)S(1)} collective-permute-done((bf16[128,2176]{1,0:T(8,128)(2,1)S(1)}, bf16[128,2176]{1,0:T(8,128)(2,1)S(1)}, u32[]{:S(2)}, u32[]{:S(2)}) %collective-permute-start.36) | collective-permute-done | bytes 557088 | tf_op jit(solution)/shard_map/ppermute | solution.py:173
  217.3 9.9 %collective-permute-done.25 = bf16[2,256,512]{2,1,0:T(8,128)(2,1)} collective-permute-done((bf16[2,256,512]{2,1,0:T(8,128)(2,1)}, bf16[2,256,512]{2,1,0:T(8,128)(2,1)}, u32[]{:S(2)}, u32[]{:S(2)}) %collective-permute-start.25) | collective-permute-done | bytes 524320 | tf_op jit(solution)/shard_map/ppermute | solution.py:177
  232.8 4.6 %collective-permute-done.28 = bf16[256,512]{1,0:T(8,128)(2,1)S(1)} collective-permute-done((bf16[256,512]{1,0:T(8,128)(2,1)S(1)}, bf16[256,512]{1,0:T(8,128)(2,1)S(1)}, u32[]{:S(2)}, u32[]{:S(2)}) %collective-permute-start.28) | collective-permute-done | bytes 262176 | tf_op jit(solution)/shard_map/ppermute | solution.py:177
  241.3 22.4 %collective-permute-done.45 = bf16[512,512]{1,0:T(8,128)(2,1)S(1)} collective-permute-done((bf16[512,512]{1,0:T(8,128)(2,1)S(1)}, bf16[512,512]{1,0:T(8,128)(2,1)S(1)}, u32[]{:S(2)}, u32[]{:S(2)}) %collective-permute-start.45) | collective-permute-done | bytes 524320 | tf_op jit(solution)/shard_map/ppermute | solution.py:613
  276.2 6.1 %collective-permute-done.49 = bf16[2,256,512]{2,1,0:T(8,128)(2,1)S(1)} collective-permute-done((bf16[2,256,512]{2,1,0:T(8,128)(2,1)S(1)}, bf16[2,256,512]{2,1,0:T(8,128)(2,1)S(1)}, u32[]{:S(2)}, u32[]{:S(2)}) %collective-permute-start.49) | collective-permute-done | bytes 524320 | tf_op jit(solution)/shard_map/ppermute | solution.py:173
  285.2 4.6 %collective-permute-start.38 = (bf16[512,768]{1,0:T(8,128)(2,1)S(1)}, bf16[512,768]{1,0:T(8,128)(2,1)S(1)}, u32[]{:S(2)}, u32[]{:S(2)}) collective-permute-start(bf16[512,768]{1,0:T(8,128)(2,1)S(1)} %bitcast.295), channel_id=1, source_target_pairs={{0,8},{24,16},{1,9},{25,17},{2,10},{26,18},{3,11},{27,19},{4,12},{... | collective-permute-start | bytes 2359304 | tf_op jit(solution)/shard_map/ppermute | solution.py:574
  293.3 5.7 %collective-permute-done.29 = bf16[256,512]{1,0:T(8,128)(2,1)S(1)} collective-permute-done((bf16[256,512]{1,0:T(8,128)(2,1)S(1)}, bf16[256,512]{1,0:T(8,128)(2,1)S(1)}, u32[]{:S(2)}, u32[]{:S(2)}) %collective-permute-start.29) | collective-permute-done | bytes 262176 | tf_op jit(solution)/shard_map/ppermute | solution.py:173
  300.7 23.5 %collective-permute-done.38 = bf16[512,768]{1,0:T(8,128)(2,1)S(1)} collective-permute-done((bf16[512,768]{1,0:T(8,128)(2,1)S(1)}, bf16[512,768]{1,0:T(8,128)(2,1)S(1)}, u32[]{:S(2)}, u32[]{:S(2)}) %collective-permute-start.38) | collective-permute-done | bytes 786464 | tf_op jit(solution)/shard_map/ppermute | solution.py:574
  327.4 4.8 %shard_map.116 = bf16[2,2,2,2,256,512]{5,4,3,2,1,0:T(8,128)(2,1)} custom-call(s32[7]{0:T(128)S(1)} %stack.140.ids_ref, bf16[2,2,2,256,512]{4,3,2,1,0:T(8,128)(2,1)S(1)} %pad_maximum_fusion.2.m_ref, bf16[2,2,2,256,512]{4,3,2,1,0:T(8,128)(2,1)S(1)} %collective-permute-done.50.o_ref, f32[4,1,512]{2,1,0:T(1,128)S(1)} %bitcast.288, ...), custom_call_target="tpu_custom_call" | custom-call | flops 3221225472 | bytes 11534336 | tf_op jit(solution)/shard_map/pallas_call | solution.py:520
  338.5 4.8 %shard_map.114.rest_0_ = bf16[2,2,2,2,256,512]{5,4,3,2,1,0:T(8,128)(2,1)} custom-call(s32[7]{0:T(128)S(1)} %stack.140.ids_ref, bf16[2,2,2,256,512]{4,3,2,1,0:T(8,128)(2,1)S(1)} %copy.55.m_ref, bf16[2,2,2,256,512]{4,3,2,1,0:T(8,128)(2,1)S(1)} %copy.56.o_ref, f32[4,1,512]{2,1,0:T(1,128)S(1)} %bitcast.289, bf16[4,512,768]{2,1,0:T(8,128)(2,1)} %pad_maximum_fusion.w_ref), custom_call_target="tpu_custom_call" | custom-call | flops 3221225472 | bytes 11534336 | tf_op jit(solution)/shard_map/pallas_call | solution.py:520
  346.4 13.4 %shard_map.115 = bf16[2,2,2,2,256,512]{5,4,3,2,1,0:T(8,128)(2,1)} custom-call(s32[7]{0:T(128)S(1)} %stack.140.ids_ref, bf16[2,2,2,256,512]{4,3,2,1,0:T(8,128)(2,1)S(1)} %copy.55.m_ref, bf16[2,2,2,256,512]{4,3,2,1,0:T(8,128)(2,1)S(1)} %copy-done.6, f32[4,1,512]{2,1,0:T(1,128)S(1)} %bitcast.290, bf16[4,512,1408]{2,1,0:T(8,128)(2,1)} %bitcast.315, ...), custom_call_target="tpu_custom_call" | custom-call | flops 5905580032 | bytes 18350080 | tf_op jit(solution)/shard_map/pallas_call | solution.py:494
  372.0 12.0 %collective-permute-done.52 = bf16[2,256,512]{2,1,0:T(8,128)(2,1)} collective-permute-done((bf16[2,256,512]{2,1,0:T(8,128)(2,1)}, bf16[2,256,512]{2,1,0:T(8,128)(2,1)}, u32[]{:S(2)}, u32[]{:S(2)}) %collective-permute-start.52) | collective-permute-done | bytes 524320 | tf_op jit(solution)/shard_map/ppermute | solution.py:177
  397.3 7.1 %collective-permute-done.41 = bf16[2,256,512]{2,1,0:T(8,128)(2,1)S(1)} collective-permute-done((bf16[2,256,512]{2,1,0:T(8,128)(2,1)S(1)}, bf16[2,256,512]{2,1,0:T(8,128)(2,1)S(1)}, u32[]{:S(2)}, u32[]{:S(2)}) %collective-permute-start.41) | collective-permute-done | bytes 524320 | tf_op jit(solution)/shard_map/ppermute | solution.py:177
  413.2 27.4 %collective-permute-done.56 = bf16[512,512]{1,0:T(8,128)(2,1)S(1)} collective-permute-done((bf16[512,512]{1,0:T(8,128)(2,1)S(1)}, bf16[512,512]{1,0:T(8,128)(2,1)S(1)}, u32[]{:S(2)}, u32[]{:S(2)}) %collective-permute-start.56) | collective-permute-done | bytes 524320 | tf_op jit(solution)/shard_map/ppermute | solution.py:618
  (285 shorter events, 182.2 us)
Async XLA Ops:
  6.5 338.2 %all-gather.2.cloned.1.call-start = ((), (), s32[]{:S(2)}) async-start(), calls=%async_computation | async-start | bytes 7208960 | tf_op jit(solution)/shard_map/all_gather | solution.py:583
  9.1 39.5 %collective-permute-start = (s32[8,128]{1,0:T(8,128)S(1)}, s32[8,128]{1,0:T(8,128)}, u32[]{:S(2)}, u32[]{:S(2)}) collective-permute-start(s32[8,128]{1,0:T(8,128)S(1)} %broadcast_in_dim.151), channel_id=1, source_target_pairs={{0,8},{8,16},{16,24},{1,9},{9,17},{17,25},{2,10},{10,18},{18,26},{... | collective-permute-start | bytes 12296 | tf_op jit(solution)/shard_map/ppermute | solution.py:211
  14.6 35.5 %collective-permute-start.1 = (s32[8,128]{1,0:T(8,128)S(1)}, s32[8,128]{1,0:T(8,128)}, u32[]{:S(2)}, u32[]{:S(2)}) collective-permute-start(s32[8,128]{1,0:T(8,128)S(1)} %broadcast_in_dim.151), channel_id=1, source_target_pairs={{0,16},{8,24},{1,17},{9,25},{2,18},{10,26},{3,19},{11,27},{4,20},{... | collective-permute-start | bytes 12296 | tf_op jit(solution)/shard_map/ppermute | solution.py:211
  19.1 33.6 %collective-permute-start.2 = (s32[8,128]{1,0:T(8,128)S(1)}, s32[8,128]{1,0:T(8,128)}, u32[]{:S(2)}, u32[]{:S(2)}) collective-permute-start(s32[8,128]{1,0:T(8,128)S(1)} %broadcast_in_dim.151), channel_id=1, source_target_pairs={{0,24},{1,25},{2,26},{3,27},{4,28},{5,29},{6,30},{7,31}} | collective-permute-start | bytes 12296 | tf_op jit(solution)/shard_map/ppermute | solution.py:211
  27.2 28.1 %collective-permute-start.3 = (bf16[128,768]{1,0:T(8,128)(2,1)}, bf16[128,768]{1,0:T(8,128)(2,1)S(1)}, u32[]{:S(2)}, u32[]{:S(2)}) collective-permute-start(bf16[128,768]{1,0:T(8,128)(2,1)} %get-tuple-element.49), channel_id=1, source_target_pairs={{0,2},{2,0},{4,6},{6,4},{1,3},{3,1},{5,7},{7,5},{8,10},{10,8},{12,... | collective-permute-start | bytes 589832 | tf_op jit(solution)/shard_map/ppermute | solution.py:173
  27.2 28.1 %collective-permute-start.4 = (bf16[128,768]{1,0:T(8,128)(2,1)}, bf16[128,768]{1,0:T(8,128)(2,1)S(1)}, u32[]{:S(2)}, u32[]{:S(2)}) collective-permute-start(bf16[128,768]{1,0:T(8,128)(2,1)} %get-tuple-element.48), channel_id=1, source_target_pairs={{0,4},{2,6},{4,0},{6,2},{1,5},{3,7},{5,1},{7,3},{8,12},{10,14},{12... | collective-permute-start | bytes 589832 | tf_op jit(solution)/shard_map/ppermute | solution.py:173
  56.8 21.9 %collective-permute-start.7 = (bf16[512,768]{1,0:T(8,128)(2,1)S(1)}, bf16[512,768]{1,0:T(8,128)(2,1)S(1)}, u32[]{:S(2)}, u32[]{:S(2)}) collective-permute-start(bf16[512,768]{1,0:T(8,128)(2,1)S(1)} %bitcast.293), channel_id=1, source_target_pairs={{8,0},{16,8},{24,16},{9,1},{17,9},{25,17},{10,2},{18,10},{26,18},{... | collective-permute-start | bytes 2359304 | tf_op jit(solution)/shard_map/ppermute | solution.py:198
  74.3 21.1 %collective-permute-start.8 = (bf16[512,768]{1,0:T(8,128)(2,1)S(1)}, bf16[512,768]{1,0:T(8,128)(2,1)S(1)}, u32[]{:S(2)}, u32[]{:S(2)}) collective-permute-start(bf16[512,768]{1,0:T(8,128)(2,1)S(1)} %collective-permute-done.6), channel_id=1, source_target_pairs={{0,8},{8,16},{16,24},{1,9},{9,17},{17,25},{2,10},{10,18},{18,26},{... | collective-permute-start | bytes 2359304 | tf_op jit(solution)/shard_map/ppermute | solution.py:197
  78.7 21.1 %collective-permute-start.9 = (bf16[512,768]{1,0:T(8,128)(2,1)S(1)}, bf16[512,768]{1,0:T(8,128)(2,1)S(1)}, u32[]{:S(2)}, u32[]{:S(2)}) collective-permute-start(bf16[512,768]{1,0:T(8,128)(2,1)S(1)} %collective-permute-done.7), channel_id=1, source_target_pairs={{8,0},{16,8},{24,16},{9,1},{17,9},{25,17},{10,2},{18,10},{26,18},{... | collective-permute-start | bytes 2359304 | tf_op jit(solution)/shard_map/ppermute | solution.py:198
  119.8 22.1 %collective-permute-start.18 = (bf16[512,256]{1,0:T(8,128)(2,1)S(1)}, bf16[512,256]{1,0:T(8,128)(2,1)S(1)}, u32[]{:S(2)}, u32[]{:S(2)}) collective-permute-start(bf16[512,256]{1,0:T(8,128)(2,1)S(1)} %bitcast.298), channel_id=1, source_target_pairs={{0,8},{8,16},{16,24},{1,9},{9,17},{17,25},{2,10},{10,18},{18,26},{... | collective-permute-start | bytes 786440 | tf_op jit(solution)/shard_map/ppermute | solution.py:197
  135.5 29.7 %collective-permute-start.12 = (bf16[2,144,128]{2,1,0:T(8,128)(2,1)S(1)}, bf16[2,144,128]{2,1,0:T(8,128)(2,1)S(1)}, u32[]{:S(2)}, u32[]{:S(2)}) collective-permute-start(bf16[2,144,128]{2,1,0:T(8,128)(2,1)S(1)} %get-tuple-element.18), channel_id=1, source_target_pairs={{0,8},{8,16},{16,24},{1,9},{9,17},{17,25},{2,10},{10,18},{18,26},{... | collective-permute-start | bytes 221192 | tf_op jit(solution)/shard_map/ppermute | solution.py:211
  137.7 27.5 %collective-permute-start.13 = (bf16[2,144,128]{2,1,0:T(8,128)(2,1)S(1)}, bf16[2,144,128]{2,1,0:T(8,128)(2,1)S(1)}, u32[]{:S(2)}, u32[]{:S(2)}) collective-permute-start(bf16[2,144,128]{2,1,0:T(8,128)(2,1)S(1)} %get-tuple-element.18), channel_id=1, source_target_pairs={{0,16},{8,24},{1,17},{9,25},{2,18},{10,26},{3,19},{11,27},{4,20},{... | collective-permute-start | bytes 221192 | tf_op jit(solution)/shard_map/ppermute | solution.py:211
  139.0 26.1 %collective-permute-start.14 = (bf16[2,144,128]{2,1,0:T(8,128)(2,1)S(1)}, bf16[2,144,128]{2,1,0:T(8,128)(2,1)S(1)}, u32[]{:S(2)}, u32[]{:S(2)}) collective-permute-start(bf16[2,144,128]{2,1,0:T(8,128)(2,1)S(1)} %get-tuple-element.18), channel_id=1, source_target_pairs={{0,24},{1,25},{2,26},{3,27},{4,28},{5,29},{6,30},{7,31}} | collective-permute-start | bytes 221192 | tf_op jit(solution)/shard_map/ppermute | solution.py:211
  177.2 29.8 %collective-permute-start.24 = (bf16[2,2,2,256,512]{4,3,1,2,0:T(8,128)(2,1)}, bf16[2,2,2,256,512]{4,3,1,2,0:T(8,128)(2,1)S(1)}, u32[]{:S(2)}, u32[]{:S(2)}) collective-permute-start(bf16[2,2,2,256,512]{4,3,1,2,0:T(8,128)(2,1)} %bitcast.284), channel_id=1, source_target_pairs={{0,2},{2,0},{4,6},{6,4},{1,3},{3,1},{5,7},{7,5},{8,10},{10,8},{12,... | collective-permute-start | bytes 6291464 | tf_op jit(solution)/shard_map/ppermute | solution.py:173
  180.0 24.9 %collective-permute-start.36 = (bf16[128,2176]{1,0:T(8,128)(2,1)S(1)}, bf16[128,2176]{1,0:T(8,128)(2,1)S(1)}, u32[]{:S(2)}, u32[]{:S(2)}) collective-permute-start(bf16[128,2176]{1,0:T(8,128)(2,1)S(1)} %get-tuple-element.37), channel_id=1, source_target_pairs={{0,6},{2,4},{4,2},{6,0},{1,7},{3,5},{5,3},{7,1},{8,14},{10,12},{12... | collective-permute-start | bytes 1671176 | tf_op jit(solution)/shard_map/ppermute | solution.py:173
  239.7 24.1 %collective-permute-start.45 = (bf16[512,512]{1,0:T(8,128)(2,1)S(1)}, bf16[512,512]{1,0:T(8,128)(2,1)S(1)}, u32[]{:S(2)}, u32[]{:S(2)}) collective-permute-start(bf16[512,512]{1,0:T(8,128)(2,1)S(1)} %fusion.12), channel_id=1, source_target_pairs={{0,8},{24,16},{1,9},{25,17},{2,10},{26,18},{3,11},{27,19},{4,12},{... | collective-permute-start | bytes 1572872 | tf_op jit(solution)/shard_map/ppermute | solution.py:613
  282.8 44.6 %collective-permute-start.50 = (bf16[2,2,2,256,512]{4,3,2,1,0:T(8,128)(2,1)S(1)}, bf16[2,2,2,256,512]{4,3,2,1,0:T(8,128)(2,1)S(1)}, u32[]{:S(2)}, u32[]{:S(2)}) collective-permute-start(bf16[2,2,2,256,512]{4,3,2,1,0:T(8,128)(2,1)S(1)} %pad_maximum_fusion.2.m_ref), channel_id=1, source_target_pairs={{0,2},{2,0},{4,6},{6,4},{1,3},{3,1},{5,7},{7,5},{8,10},{10,8},{12,... | collective-permute-start | bytes 6291464 | tf_op jit(solution)/shard_map/ppermute | solution.py:173
  285.2 39.0 %collective-permute-start.38 = (bf16[512,768]{1,0:T(8,128)(2,1)S(1)}, bf16[512,768]{1,0:T(8,128)(2,1)S(1)}, u32[]{:S(2)}, u32[]{:S(2)}) collective-permute-start(bf16[512,768]{1,0:T(8,128)(2,1)S(1)} %bitcast.295), channel_id=1, source_target_pairs={{0,8},{24,16},{1,9},{25,17},{2,10},{26,18},{3,11},{27,19},{4,12},{... | collective-permute-start | bytes 2359304 | tf_op jit(solution)/shard_map/ppermute | solution.py:574
  291.9 33.0 %collective-permute-start.32 = (bf16[2,256,512]{2,1,0:T(8,128)(2,1)S(1)}, bf16[2,256,512]{2,1,0:T(8,128)(2,1)S(1)}, u32[]{:S(2)}, u32[]{:S(2)}) collective-permute-start(bf16[2,256,512]{2,1,0:T(8,128)(2,1)S(1)} %get-tuple-element.66), channel_id=1, source_target_pairs={{0,4},{2,6},{4,0},{6,2},{1,5},{3,7},{5,1},{7,3},{8,12},{10,14},{12... | collective-permute-start | bytes 1572872 | tf_op jit(solution)/shard_map/ppermute | solution.py:173
  299.1 25.9 %collective-permute-start.30 = (bf16[2,256,512]{2,1,0:T(8,128)(2,1)S(1)}, bf16[2,256,512]{2,1,0:T(8,128)(2,1)S(1)}, u32[]{:S(2)}, u32[]{:S(2)}) collective-permute-start(bf16[2,256,512]{2,1,0:T(8,128)(2,1)S(1)} %get-tuple-element.60), channel_id=1, source_target_pairs={{0,1},{1,0},{2,3},{3,2},{4,5},{5,4},{6,7},{7,6},{8,9},{9,8},{10,11... | collective-permute-start | bytes 1572872 | tf_op jit(solution)/shard_map/ppermute | solution.py:177
  300.0 25.4 %collective-permute-start.37 = (bf16[512,768]{1,0:T(8,128)(2,1)S(1)}, bf16[512,768]{1,0:T(8,128)(2,1)S(1)}, u32[]{:S(2)}, u32[]{:S(2)}) collective-permute-start(bf16[512,768]{1,0:T(8,128)(2,1)S(1)} %bitcast.296), channel_id=1, source_target_pairs={{8,16},{16,8},{9,17},{17,9},{10,18},{18,10},{11,19},{19,11},{12,20... | collective-permute-start | bytes 2359304 | tf_op jit(solution)/shard_map/ppermute | solution.py:573
  337.6 27.4 %collective-permute-start.51 = (bf16[2,2,2,256,512]{4,3,1,2,0:T(8,128)(2,1)}, bf16[2,2,2,256,512]{4,3,1,2,0:T(8,128)(2,1)}, u32[]{:S(2)}, u32[]{:S(2)}) collective-permute-start(bf16[2,2,2,256,512]{4,3,1,2,0:T(8,128)(2,1)} %bitcast.282), channel_id=1, source_target_pairs={{0,2},{2,0},{4,6},{6,4},{1,3},{3,1},{5,7},{7,5},{8,10},{10,8},{12,... | collective-permute-start | bytes 6291464 | tf_op jit(solution)/shard_map/ppermute | solution.py:173
  365.1 23.9 %collective-permute-start.40 = (bf16[2,2,2,256,512]{4,3,1,2,0:T(8,128)(2,1)}, bf16[2,2,2,256,512]{4,3,1,2,0:T(8,128)(2,1)}, u32[]{:S(2)}, u32[]{:S(2)}) collective-permute-start(bf16[2,2,2,256,512]{4,3,1,2,0:T(8,128)(2,1)} %bitcast.283), channel_id=1, source_target_pairs={{0,2},{2,0},{4,6},{6,4},{1,3},{3,1},{5,7},{7,5},{8,10},{10,8},{12,... | collective-permute-start | bytes 6291464 | tf_op jit(solution)/shard_map/ppermute | solution.py:173
  395.9 44.7 %collective-permute-start.56 = (bf16[512,512]{1,0:T(8,128)(2,1)S(1)}, bf16[512,512]{1,0:T(8,128)(2,1)S(1)}, u32[]{:S(2)}, u32[]{:S(2)}) collective-permute-start(bf16[512,512]{1,0:T(8,128)(2,1)S(1)} %pad_maximum_fusion.7), channel_id=1, source_target_pairs={{8,0},{16,24},{9,1},{17,25},{10,2},{18,26},{11,3},{19,27},{12,4},{... | collective-permute-start | bytes 1572872 | tf_op jit(solution)/shard_map/ppermute | solution.py:618
  (68 other events, 690.2 us)
Sparse Core Ops, SparseCore 0:
  207.1 128.7 all-gather.1

commit v3 on v1

v3 whole, which is shorter than its diff:
```python
import functools

import jax
import jax.numpy as jnp
from jax import lax
from jax.experimental import pallas as pl
from jax.experimental.pallas import tpu as pltpu
from jax.sharding import PartitionSpec as P

HEAD = 128
EPS = 1e-05
BF = jnp.bfloat16
F32 = jnp.float32
VMEM_LIMIT = 48 * 1024 * 1024


def nt(a, b):
    return lax.dot_general(a, b, (((1,), (1,)), ((), ())), preferred_element_type=F32)


def tn(a, b):
    return lax.dot_general(a, b, (((0,), (0,)), ((), ())), preferred_element_type=F32)


def nn(a, b):
    return jnp.dot(a, b, preferred_element_type=F32)


def sigmoid(v):
    return 1.0 / (1.0 + jnp.exp(-v))


def call(body, grid, in_specs, out_specs, out_shape, scratch=(), prefetch=1, cost=None):
    return pl.pallas_call(
        body,
        out_shape=out_shape,
        grid_spec=pltpu.PrefetchScalarGridSpec(
            num_scalar_prefetch=prefetch,
            grid=grid,
            in_specs=in_specs,
            out_specs=out_specs,
            scratch_shapes=list(scratch),
        ),
        compiler_params=pltpu.CompilerParams(
            dimension_semantics=("arbitrary",) * len(grid), vmem_limit_bytes=VMEM_LIMIT
        ),
        cost_estimate=None
        if cost is None
        else pl.CostEstimate(flops=cost[0], bytes_accessed=cost[1], transcendentals=0),
    )


def whole(shape):
    zeros = (0,) * len(shape)
    return pl.BlockSpec(shape, lambda *_: zeros, pipeline_mode=pl.Buffered(1))


ANY = pl.BlockSpec(memory_space=pl.ANY)


class Rows:
    def __init__(self, arrays, low=0, high=None):
        self.arrays = list(arrays)
        self.planes, self.rows, columns = (
            self.arrays[0].shape if len(self.arrays) == 1 else (len(arrays), *self.arrays[0].shape)
        )
        self.part = slice(low, columns if high is None else high)
        self.scratch = [
            pltpu.VMEM((self.planes * self.rows, self.part.stop - low), BF),
            pltpu.SemaphoreType.DMA((self.planes * 4,)),
        ]

    def copies(self, ids_ref, refs, held, sems):
        rows = self.rows // 4
        for i in range(self.planes):
            ref, plane = (refs[0].at[i], i) if len(refs) == 1 else (refs[i], ids_ref[3 + i])
            for s in range(4):
                to = pl.multiple_of((plane * 4 + (ids_ref[0] ^ s)) * rows, rows)
                yield pltpu.make_async_copy(
                    ref.at[pl.ds(s * rows, rows), self.part], held.at[pl.ds(to, rows)], sems.at[4 * i + s]
                )

    def start(self, *where):
        for copy in self.copies(*where):
            copy.start()

    def wait(self, *where):
        for copy in self.copies(*where):
            copy.wait()


def pack_mixer(ids, mixer_in, mixer_out):
    width = mixer_in.shape[1]
    cols = mixer_in.shape[2] // 8

    def body(ids_ref, q_ref, f_ref, v_ref, o_ref, out_ref):
        out_ref[0, :, 0:cols] = q_ref[0].astype(BF)
        out_ref[0, :, cols : 2 * cols] = f_ref[0].astype(BF)
        out_ref[0, :, 2 * cols : 3 * cols] = v_ref[0].astype(BF)
        out_ref[0, :, 3 * cols : 4 * cols] = o_ref[...].T.astype(BF)

    def dest(s, ids_ref):
        return 2 * (ids_ref[0] ^ s) + ids_ref[1]

    def part(i):
        return pl.BlockSpec((1, width, cols), lambda s, r: (i, 0, dest(s, r)))

    return call(
        body,
        (4,),
        [part(0), part(1), part(2), pl.BlockSpec((cols, width), lambda s, r: (dest(s, r), 0))],
        pl.BlockSpec((1, width, 4 * cols), lambda s, r: (s, 0, 0)),
        jax.ShapeDtypeStruct((4, width, 4 * cols), BF),
        cost=(0, 4 * width * cols * 24),
    )(ids, mixer_in, mixer_in, mixer_in, mixer_out)


class Feed:
    def __init__(self, hidden_all):
        tiles = hidden_all // 128 // 8
        self.half_at = 8 * tiles
        assert hidden_all == (8 * tiles + 4) * 128
        self.near = tiles * 128
        self.near_up = 2 * self.near + 128
        self.near_all = self.near_up + self.near + 128


def pack_feed(ids, gate_up, down, feed):
    width = gate_up.shape[1]
    near, up, both = feed.near, feed.near_up, feed.near_all

    def body(ids_ref, *refs):
        g_ref, u_ref, gh_ref, uh_ref, d_ref, dh_ref = refs[:6]
        out_ref = refs[-1]
        odd = (ids_ref[0] ^ pl.program_id(0)) % 2
        out_ref[0, :, 0:near] = g_ref[0].astype(BF)
        lane = lax.broadcasted_iota(jnp.int32, (width, 128), 1)
        gh, uh = gh_ref[0], uh_ref[0]
        even_mix = jnp.where(lane < 64, gh, pltpu.roll(uh, 64, 1))
        odd_mix = jnp.where(lane < 64, pltpu.roll(gh, 64, 1), uh)
        out_ref[0, :, near : near + 128] = jnp.where(odd == 1, odd_mix, even_mix).astype(BF)
        out_ref[0, :, near + 128 : up] = u_ref[0].astype(BF)
        out_ref[0, :, up : up + near] = d_ref[...].T.astype(BF)
        last = jnp.concatenate([dh_ref[...], jnp.zeros((64, width), F32)], axis=0)
        out_ref[0, :, up + near : both] = last.T.astype(BF)

    def dest(s, r):
        return 4 * r[1] + (r[0] ^ s)

    def tile(s, r):
        return feed.half_at + 2 * r[1] + (r[0] ^ s) // 2


    def cols(i):
        return pl.BlockSpec((1, width, near), lambda s, r: (i, 0, dest(s, r)))

    def mix(i):
        return pl.BlockSpec((1, width, 128), lambda s, r: (i, 0, tile(s, r)))

    in_specs = [
        cols(0),
        cols(1),
        mix(0),
        mix(1),
        pl.BlockSpec((near, width), lambda s, r: (dest(s, r), 0)),
        pl.BlockSpec((64, width), lambda s, r: (2 * feed.half_at + dest(s, r), 0)),
    ]
    args = [gate_up, gate_up, gate_up, gate_up, down, down]
    return call(
        body,
        (4,),
        in_specs,
        pl.BlockSpec((1, width, both), lambda s, r: (s, 0, 0)),
        jax.ShapeDtypeStruct((4, width, both), BF),
        cost=(0, 4 * width * both * 6),
    )(ids, *args)


def mp_perm(value, s):
    return lax.ppermute(value, "mp", [(i, i ^ s) for i in range(4)])


def rep_perm(value):
    return lax.ppermute(value, "rep", [(0, 1), (1, 0)])


def across_plane(packed):
    moved = [mp_perm(packed[s], s) for s in (1, 2, 3)]
    return jnp.concatenate([packed[0], *moved], axis=0), moved


def after(value, *others):
    return lax.optimization_barrier((value, *others))[0]


def from_earlier(value, count):
    return [
        lax.ppermute(value, "ctx", [(i, i + d) for i in range(count - d)]) for d in range(1, count)
    ]


def total_before(value, count):
    shift = 1
    total = lax.ppermute(value, "ctx", [(i, i + 1) for i in range(count - 1)])
    so_far = total + value
    while 2 * shift < count:
        came = lax.ppermute(so_far, "ctx", [(i, i + 2 * shift) for i in range(count - 2 * shift)])
        total, so_far, shift = total + came, so_far + came, 2 * shift
    return total


def normalise(table, token_pages, gain):
    _, page, width = token_pages.shape
    pages = table.shape[0]

    def body(table_ref, x_ref, g_ref, out_ref):
        x = x_ref[0].astype(F32)
        scale = lax.rsqrt(jnp.mean(x * x, axis=-1, keepdims=True) + EPS)
        out_ref[...] = (x * scale * g_ref[...]).astype(BF)

    return call(
        body,
        (pages,),
        [pl.BlockSpec((1, page, width), lambda i, t: (t[i], 0, 0)), whole((1, width))],
        pl.BlockSpec((page, width), lambda i, t: (i, 0)),
        jax.ShapeDtypeStruct((pages * page, width), BF),
        cost=(pages * page * width * 4, pages * page * width * 4),
    )(table, token_pages, gain.reshape(1, width))


def step_state(state, ks, v, same_last, keep, final):
    update = tn(v, jnp.where(same_last, ks, jnp.zeros_like(ks)))
    return (jnp.where(keep, state, 0.0) + update) * final


def project(ids, live, last, normed, foreign, weights, floor, cnt_col):
    width = normed.shape[1]
    cols = floor.shape[1]
    heads = cols // HEAD
    pages = live.shape[0]
    rows = cnt_col.shape[0]
    page = rows // pages
    group = 2
    steps = pages // group

    n = len(weights.arrays)

    def body(ids_ref, *refs):
        pl.when(ids_ref[2] == 1)(lambda: work(ids_ref, *refs))

    def work(ids_ref, live_ref, last_ref, x_ref, *refs):
        f_refs, refs = refs[: len(foreign)], refs[len(foreign) :]
        w_refs = refs[:n]
        fl_ref, cnt_ref, qs_ref, ks_ref, v_ref, fin_ref, st_ref, state, total, held, sems = refs[n:]
        step = pl.program_id(0)

        @pl.when(step == 0)
        def _():
            weights.start(ids_ref, w_refs, held, sems)
            state[...] = jnp.zeros_like(state)
            total[...] = jnp.zeros_like(total)
            weights.wait(ids_ref, w_refs, held, sems)

        x = x_ref[...]
        if foreign:
            mine, other = (f[:, 0, 0].reshape(page, width) for f in f_refs)
            low = (ids_ref[0] & 1) == 0
            pair = jnp.concatenate([jnp.where(low, mine, other), jnp.where(low, other, mine)], axis=0)
            x = jnp.where((step >> 2) == ids_ref[8], x, pair)
        proj = nn(x, held[...])
        row = lax.broadcasted_iota(jnp.int32, (page, page), 0)
        col = lax.broadcasted_iota(jnp.int32, (page, page), 1)
        lower = (row >= col).astype(F32)
        floor_row = fl_ref[...]
        for j in range(group):
            p = step * group + j
            here = slice(j * page, (j + 1) * page)
            alive = live_ref[p].astype(F32)
            now = last_ref[p]
            before = jnp.where(p == 0, 0, last_ref[jnp.maximum(p - 1, 0)])
            q = proj[here, 0:cols]
            q = q * sigmoid(q)
            f = proj[here, cols : 2 * cols]
            gate = sigmoid(f)
            forget = floor_row + (1.0 - floor_row) * gate
            key = (1.0 - forget) * alive
            log_decay = jnp.log(forget) * alive
            cum = jnp.dot(lower, log_decay, precision=lax.Precision.HIGHEST, preferred_element_type=F32)
            final_log = cum[page - 1 : page, :]
            final = jnp.exp(final_log)
            ks = (key * jnp.exp(-cum)).astype(BF)
            v = proj[here, 2 * cols : 3 * cols].astype(BF)
            qs_ref[here, :] = (q * jnp.exp(cum)).astype(BF)
            ks_ref[here, :] = ks
            v_ref[here, :] = v
            fin_ref[j] = final
            total[...] += final_log
            same_last = cnt_ref[here, :] == now
            for h in range(heads):
                hc = slice(h * HEAD, (h + 1) * HEAD)
                state[h] = step_state(state[h], ks[:, hc], v[:, hc], same_last, now == before, final[:, hc])

        @pl.when(step == steps - 1)
        def _():
            none = last_ref[pages - 1] == 0
            decay = jnp.where(none, jnp.exp(total[...]), 0.0)
            for h in range(heads):
                st_ref[h, 0:HEAD, :] = state[h].astype(BF)
                st_ref[h, HEAD : HEAD + 16, :] = jnp.broadcast_to(
                    decay[:, h * HEAD : (h + 1) * HEAD], (16, HEAD)
                ).astype(BF)

    block = group * page
    return call(
        body,
        (steps,),
        [
            pl.BlockSpec((block, width), lambda i, *_: (i & 3, 0)),
        ]
        + [
            pl.BlockSpec(
                (2, 1, 1, page // 2, width),
                lambda i, r, *_: (0, ((i >> 1) & 1) ^ r[1], (i & 1) ^ (r[0] >> 1), 0, 0),
            )
        ]
        * len(foreign)
        + [ANY] * n
        + [
            whole((1, cols)),
            pl.BlockSpec((block, 1), lambda i, *_: (i, 0)),
        ],
        [
            pl.BlockSpec((block, cols), lambda i, *_: (i, 0)),
            pl.BlockSpec((block, cols), lambda i, *_: (i, 0)),
            pl.BlockSpec((block, cols), lambda i, *_: (i, 0)),
            pl.BlockSpec((group, 1, cols), lambda i, *_: (i, 0, 0)),
            whole((heads, HEAD + 16, HEAD)),
        ],
        [
            jax.ShapeDtypeStruct((rows, cols), BF),
            jax.ShapeDtypeStruct((rows, cols), BF),
            jax.ShapeDtypeStruct((rows, cols), BF),
            jax.ShapeDtypeStruct((pages, 1, cols), F32),
            jax.ShapeDtypeStruct((heads, HEAD + 16, HEAD), BF),
        ],
        scratch=[pltpu.VMEM((heads, HEAD, HEAD), F32), pltpu.VMEM((1, cols), F32), *weights.scratch],
        prefetch=3,
        cost=(2 * rows * width * 3 * cols, rows * width * 2 + width * cols * 8),
    )(ids, live, last, normed, *foreign, *weights.arrays, floor, cnt_col)


def mix(ids, last, earlier, qs, ks, v, fin, weights, cnt_col, cnt_row):
    rows, cols = qs.shape
    heads = cols // HEAD
    pages = fin.shape[0]
    page = rows // pages
    group = 2
    steps = pages // group
    width = weights.planes * weights.rows
    n = len(earlier)
    spans = steps // 4
    m = n + 4 + len(weights.arrays)

    def body(ids_ref, *refs):
        pl.when(ids_ref[2] == 1)(lambda: work(ids_ref, *refs))

    def work(ids_ref, last_ref, *refs):
        packs = refs[:n]
        qs_ref, ks_ref, v_ref, fin_ref = refs[n : n + 4]
        w_refs = refs[n + 4 : m]
        cc_ref, cr_ref = refs[m : m + 2]
        outs = refs[m + 2 : m + 2 + 2 * spans]
        state, held, sems = refs[m + 2 + 2 * spans :]
        step = pl.program_id(0)

        @pl.when(step == 0)
        def _():
            weights.start(ids_ref, w_refs, held, sems)
            for h in range(heads):
                total = jnp.zeros((HEAD, HEAD), F32)
                for pack in reversed(packs):
                    total = total * pack[h, HEAD : HEAD + 1, :].astype(F32) + pack[h, 0:HEAD, :].astype(F32)
                state[h] = total

        row = lax.broadcasted_iota(jnp.int32, (page, page), 0)
        col = lax.broadcasted_iota(jnp.int32, (page, page), 1)
        lower = row >= col
        normed = []
        for j in range(group):
            p = step * group + j
            here = slice(j * page, (j + 1) * page)
            now = last_ref[p]
            before = jnp.where(p == 0, 0, last_ref[jnp.maximum(p - 1, 0)])
            cc, cr = cc_ref[here, :], cr_ref[j]
            allowed = lower & (cc == cr)
            reached = cc == before
            same_last = cc == now
            for h in range(heads):
                hc = slice(h * HEAD, (h + 1) * HEAD)
                q_h, k_h, v_h = qs_ref[here, hc], ks_ref[here, hc], v_ref[here, hc]
                scores = jnp.where(allowed, nt(q_h, k_h), 0.0).astype(BF)
                out = nn(scores, v_h)
                out = out + jnp.where(reached, nt(q_h, state[h].astype(BF)), 0.0)
                state[h] = step_state(state[h], k_h, v_h, same_last, now == before, fin_ref[j, :, hc])
                scale = lax.rsqrt(jnp.mean(out * out, axis=-1, keepdims=True) + EPS)
                normed.append((out * scale).astype(BF))
        hn = jnp.concatenate(
            [jnp.concatenate(normed[j * heads : (j + 1) * heads], axis=1) for j in range(group)], axis=0
        )

        @pl.when(step == 0)
        def _():
            weights.wait(ids_ref, w_refs, held, sems)

        for dc in range(2):
            for dy in range(2):
                term = nt(hn, held[block_of(ids_ref[0] ^ (2 * dy + dc), width // 4), :]).astype(BF)
                for span in range(spans):

                    @pl.when((step // 4) ^ ids_ref[8] == span)
                    def _(span=span, dc=dc, dy=dy, term=term):
                        outs[2 * span + dc][0, 0, dy] = term

    block = group * page
    rowspec = pl.BlockSpec((block, cols), lambda i, *_: (i, 0))

    def terms(span):
        def index(i, r, l):
            low = 4 * (span ^ r[8])
            i = jnp.minimum(jnp.maximum(i, low), low + 3) & 3
            return (i % 2, (i // 2) ^ r[1], 0, 0, 0)

        return pl.BlockSpec((1, 1, 2, block, width // 4), index)

    return call(
        body,
        (steps,),
        [whole(e.shape) for e in earlier]
        + [
            rowspec,
            rowspec,
            rowspec,
            pl.BlockSpec((group, 1, cols), lambda i, *_: (i, 0, 0)),
        ]
        + [ANY] * len(weights.arrays)
        + [
            pl.BlockSpec((block, 1), lambda i, *_: (i, 0)),
            pl.BlockSpec((group, 1, page), lambda i, *_: (i, 0, 0)),
        ],
        [terms(span) for span in range(spans) for _ in range(2)],
        [jax.ShapeDtypeStruct((2, 2, 2, block, width // 4), BF)] * (2 * spans),
        scratch=[pltpu.VMEM((heads, HEAD, HEAD), F32), *weights.scratch],
        prefetch=2,
        cost=(2 * rows * cols * width, rows * width * 2),
    )(ids, last, *earlier, qs, ks, v, fin, *weights.arrays, cnt_col, cnt_row)


def add(a, b):
    return (a.astype(F32) + b.astype(F32)).astype(BF)


def sum_scatter(terms):
    mine, other = terms[0], mp_perm(terms[1], 1)
    a_keep, a_send = add(mine[0, 0], other[0, 0]), add(mine[0, 1], other[0, 1])
    b_keep, b_send = add(mine[1, :, 0], other[1, :, 0]), add(mine[1, :, 1], other[1, :, 1])
    a_came, b_came = rep_perm(a_send), mp_perm(b_send, 2)
    a_send, b_send = add(a_keep[1], a_came[1]), add(b_keep[1], b_came[1])
    a_last, b_last = mp_perm(a_send, 2), rep_perm(b_send)
    a = a_keep[0].astype(F32) + a_came[0].astype(F32) + a_last.astype(F32)
    b = b_keep[0].astype(F32) + b_came[0].astype(F32) + b_last.astype(F32)
    return jnp.concatenate([a, b], axis=0), (a_came, b_came)


def gather_plane(value, *others):
    half = value.shape[0] // 2
    a, b = value[:half], value[half:]
    a_y, b_x = mp_perm(a, 2), rep_perm(b)
    a_pair, b_pair = jnp.stack([a, a_y]), jnp.stack([b, b_x])
    a_x, b_y = rep_perm(a_pair), mp_perm(b_pair, 2)
    mine = jnp.stack([jnp.stack([a_pair, a_x]), jnp.stack([b_pair, b_y], axis=1)])
    mine = after(mine, *others)
    return mine, mp_perm(mine, 1)


def feed_inputs(ids_ref, m_ref, o_ref, g_ref):
    mp_index = ids_ref[0]
    places = [(dy, dc) for dy in range(2) for dc in range(2)]
    blocks = [(m_ref, o_ref)[dc][0, 0, dy].astype(F32) for dy, dc in places]
    square = sum(jnp.sum(b * b, axis=-1, keepdims=True) for b in blocks)
    scale = lax.rsqrt(square / (4 * blocks[0].shape[1]) + EPS)
    at = [mp_index ^ (2 * dy + dc) for dy, dc in places]
    return places, at, [(b * scale * g_ref[k]).astype(BF) for k, b in zip(at, blocks)]


def block_of(k, rows):
    return pl.ds(pl.multiple_of(k * rows, rows), rows)


def total_of(terms):
    out = None
    for term in terms:
        out = term if out is None else out + term
    return out


def feed_specs(mine, gain):
    rows, kwide = mine.shape[-2:]
    spec = pl.BlockSpec((1, 1, 2, rows, kwide), lambda i, r: (i % 2, i // 2, 0, 0, 0))
    return [spec, spec, whole(gain.shape)], [spec, spec], [jax.ShapeDtypeStruct((2, 2, 2, rows, kwide), BF)] * 2


def feed_forward(ids, mine, other, gain, weights, feed):
    near, up, both = feed.near, feed.near_up, feed.near_all
    specs, out_spec, out_shape = feed_specs(mine, gain)

    n = len(weights.arrays)

    def body(ids_ref, m_ref, o_ref, g_ref, *rest):
        w_refs, outs, (held, sems) = rest[:n], rest[n : n + 2], rest[n + 2 :]
        first = pl.program_id(0) == 0
        pl.when(first)(lambda: weights.start(ids_ref, w_refs, held, sems))
        places, at, xs = feed_inputs(ids_ref, m_ref, o_ref, g_ref)
        pl.when(first)(lambda: weights.wait(ids_ref, w_refs, held, sems))

        h = total_of(nn(x, held[block_of(k, kwide), 0:up]) for k, x in zip(at, xs))
        gate, upward = h[:, 0:near], h[:, near + 128 : up]
        edge = h[:, near : near + 128]
        hidden = gate * sigmoid(gate) * upward
        mixed = edge * sigmoid(edge) * pltpu.roll(edge, 64, 1)
        lane = lax.broadcasted_iota(jnp.int32, mixed.shape, 1)
        mixed = jnp.where(lane < 64, mixed, 0.0)
        hidden = jnp.concatenate([hidden, mixed], axis=1).astype(BF)
        for (dy, dc), k in zip(places, at):
            term = nt(hidden, held[block_of(k, kwide), up:both])
            outs[dc][0, 0, dy] = term.astype(BF)

    rows, kwide = out_shape[0].shape[-2] * 4, out_shape[0].shape[-1]
    return call(
        body,
        (4,),
        specs + [ANY] * n,
        out_spec,
        out_shape,
        scratch=weights.scratch,
        cost=(rows * 4 * kwide * both * 2, 4 * kwide * both * 2 + 6 * out_shape[0].size * 2),
    )(ids, mine, other, gain, *weights.arrays)


def shards(
    token_pages,
    page_table,
    live_flags,
    lengths,
    decay_floor,
    mixer_gain,
    feed_gain,
    trainer_mixer_in,
    trainer_mixer_out,
    trainer_gate_up,
    trainer_down,
):
    ctx_count = lax.axis_size("ctx")
    ctx_index = lax.axis_index("ctx")
    mp_index = lax.axis_index("mp")
    rep_index = lax.axis_index("rep")
    pages, page, width = token_pages.shape
    cols = decay_floor.shape[0]
    kwide = width // 4
    feed = Feed(trainer_gate_up.shape[2])
    line = ctx_count == 4 and pages == 8
    middle = (ctx_index == 1) | (ctx_index == 2)
    beyond = jnp.where(ctx_index == 1, 0, 3)
    order = [ctx_index, 3 - ctx_index, beyond, 3 - beyond]
    own_span = (ctx_index == 1).astype(jnp.int32) if line else 0
    active = middle.astype(jnp.int32) if line else 1
    ids = jnp.stack([mp_index, rep_index, active, *order, ctx_index, own_span]).astype(jnp.int32)

    def gather(value):
        return Rows([lax.all_gather(value, "ctx", axis=0)])

    if line:
        sent = lax.dynamic_slice_in_dim(page_table, rep_index * 4 + mp_index, 1, 0)
        chunk = normalise(sent, token_pages, mixer_gain)
        ids_next = after(ids, chunk)
        chunk = lax.ppermute(chunk, "ctx", [(0, 1), (3, 2)])
    else:
        ids_next = ids
    packed_mixer = pack_mixer(ids_next, trainer_mixer_in, trainer_mixer_out)
    plane_mixer, moved = across_plane(packed_mixer)
    packed_feed = after(pack_feed(after(ids, packed_mixer), trainer_gate_up, trainer_down, feed), *moved)
    plane_feed, _ = across_plane(packed_feed)
    flags = after(live_flags, packed_mixer)
    if line:
        spread = jnp.broadcast_to(flags[:, None], (pages, 128)).astype(jnp.int32)
        came = lax.ppermute(spread, "ctx", [(0, 1), (3, 2)])
        totals = jnp.broadcast_to(jnp.sum(spread + came, axis=0, keepdims=True), (8, 128))
        base = lax.ppermute(totals, "ctx", [(1, 2)])[0, 0]
        theirs = came[:, 0]
        live_here = jnp.concatenate(
            [jnp.where(ctx_index == 1, theirs, flags), jnp.where(ctx_index == 1, flags, theirs)]
        )
        page_start = (base + jnp.cumsum(live_here) - live_here) * page

        across = lax.ppermute(plane_mixer, "ctx", [(1, 2), (2, 1)])
        inward = lax.ppermute(plane_mixer, "ctx", [(0, 1), (3, 2)])
        onward = lax.ppermute(inward, "ctx", [(1, 2), (2, 1)])
        mixer_rows = [plane_mixer, across, inward, onward]
        plane_feed = after(plane_feed, onward)
        normed = normalise(after(page_table, *moved), token_pages, mixer_gain)
        foreign = gather_plane(chunk, across, inward, normed)
    else:
        normed = normalise(page_table, token_pages, mixer_gain)
        foreign = ()
        live_here = flags
        live_total = jnp.broadcast_to(jnp.sum(flags) * page, (8, 128)).astype(jnp.int32)
        page_start = total_before(live_total, ctx_count)[0, 0] + (jnp.cumsum(flags) - flags) * page
        mixer_rows = gather(plane_mixer).arrays
    w_feed = gather(plane_feed)

    rows = live_here.shape[0] * page
    positions = (page_start[:, None] + jnp.arange(page, dtype=jnp.int32)[None, :]).reshape(rows)
    starts = jnp.cumsum(lengths) - lengths
    resets = (jnp.repeat(live_here, page) == 1) & jnp.any(positions[:, None] == starts[None, :], axis=1)
    count = jnp.cumsum(resets.astype(jnp.int32))
    cnt_col = count.reshape(rows, 1)
    cnt_row = count.reshape(-1, 1, page)
    last = count.reshape(-1, page)[:, -1]
    if line:
        *mixer_rows, normed, cnt_col, cnt_row, last = lax.optimization_barrier(
            (*mixer_rows, normed, cnt_col, cnt_row, last)
        )
    w_in, w_out = Rows(mixer_rows, 0, 3 * cols), Rows(mixer_rows, 3 * cols)

    half_rows = pages * page // 2
    table_half = lax.dynamic_slice_in_dim(page_table, rep_index * (pages // 2), pages // 2, 0)
    token_cols = lax.dynamic_slice_in_dim(token_pages, mp_index * kwide, kwide, 2)
    ordered = jnp.take(token_cols, table_half, axis=0).reshape(half_rows, kwide)

    qs, ks, v, fin, pack = project(
        ids, live_here, last, normed, foreign, w_in, decay_floor.reshape(1, cols), cnt_col
    )
    earlier = [lax.ppermute(pack, "ctx", [(1, 2)])] if line else from_earlier(pack, ctx_count)
    terms = mix(ids, last, earlier, qs, ks, v, fin, w_out, cnt_col, cnt_row)
    if line:
        theirs, stage = sum_scatter(terms[2:])
        back = lax.ppermute(theirs.astype(BF), "ctx", [(1, 0), (2, 3)])
        keep, send, *_ = lax.optimization_barrier((terms[0], terms[1], *stage))
        mixed = jnp.where(middle, sum_scatter((keep, send))[0], back.astype(F32))
    else:
        mixed = sum_scatter(terms)[0]
    residual = ordered.astype(F32) + mixed
    mine, other = gather_plane(residual.astype(BF))
    down_terms = feed_forward(ids, mine, other, feed_gain.reshape(4, 1, kwide), w_feed, feed)
    summed = residual + sum_scatter(down_terms)[0]
    live_half = jnp.repeat(
        lax.dynamic_slice_in_dim(live_flags, rep_index * (pages // 2), pages // 2, 0), page
    )
    return jnp.where(live_half[:, None] == 1, summed, 0.0).astype(BF)


def solution(mesh):
    in_specs = (
        P("ctx", None, None),
        P("ctx"),
        P("ctx"),
        P(),
        P(("mp", "rep")),
        P(),
        P(),
        P(None, ("ctx", "mp"), None),
        P(None, ("ctx", "mp")),
        P(None, ("ctx", "mp"), None),
        P(None, ("ctx", "mp")),
    )
    out_specs = P(("ctx", "rep"), "mp")
    return jax.shard_map(shards, mesh=mesh, in_specs=in_specs, out_specs=out_specs, check_vma=False)
```

time: 403 us -> 316 us (0.78)
  waiting for transfers between devices: 222 us -> 174 us
  local copies, waits for them, and re-layouts: 39 us -> 16.1 us
  starting transfers between devices: 68.7 us -> 46 us
  other arithmetic: 9.35 us -> 19.7 us
    ppermute x12 -> x8, waiting for transfers between devices: 140 us -> 79.3 us  [the longest x1 75.9 us: shards(): back = lax.ppermute(theirs.astype(BF), 'ctx', [(1, 0), (2, 3)])]
    ppermute x12 -> x8, starting transfers between devices: 51.6 us -> 19.1 us  [the longest x1 6.86 us: shards(): inward = lax.ppermute(plane_mixer, 'ctx', [(0, 1), (3, 2)])]
    ppermute x15 -> x21, waiting for transfers between devices: 47.4 us -> 72.5 us  [mp_perm(): return lax.ppermute(value, 'mp', [(i, i ^ s) for i in range(4)])]
    ppermute x6 -> x10, waiting for transfers between devices: 35 us -> 21.7 us  [rep_perm(): return lax.ppermute(value, 'rep', [(0, 1), (1, 0)])]
    dynamic_update_slice x13 -> x0, local copies, waits for them, and re-layouts: 9.63 us -> none  [the longest x6 5.18 us: across_plane(): out = lax.dynamic_update_index_in_dim(out, arrived[s], mp_index ^ s, 0)]
    slice x8 -> x3, local copies, waits for them, and re-layouts: 9.24 us -> 0.77 us  [the longest x1 0.51 us: shards(): base = lax.ppermute(totals, 'ctx', [(1, 2)])[0, 0]]
    ppermute x6 -> x10, starting transfers between devices: 5.26 us -> 12.1 us  [rep_perm(): return lax.ppermute(value, 'rep', [(0, 1), (1, 0)])]
    squeeze x10 -> x2, local copies, waits for them, and re-layouts: 5.51 us -> 1.25 us  [across_plane(): return (jnp.concatenate([packed[0], *moved], axis=0), moved)]
  transfers between devices with their start and end apart: 34 -> 40, of which waited for: 24 -> 21; matrix products, arithmetic and copies ran while one was open for 7% -> 8% of each run, Pallas kernels for 7% -> 8%
where the time goes in v3:
time: 316 us; the launch traced here: 315 us
  waiting for transfers between devices  174 us (55%)
  starting transfers between devices  46 us (15%)
  Pallas kernels  45.6 us (14%)
  other arithmetic  19.7 us (6%)
  local copies, waits for them, and re-layouts  16.1 us (5%)
  between operations  13.9 us (4%)
    ppermute x1, waiting for transfers between devices, shards(): back = lax.ppermute(theirs.astype(BF), 'ctx', [(1, 0), (2, 3)])  75.9 us
    ppermute x21, waiting for transfers between devices, mp_perm(): return lax.ppermute(value, 'mp', [(i, i ^ s) for i in range(4)])  72.5 us
    ppermute x10, waiting for transfers between devices, rep_perm(): return lax.ppermute(value, 'rep', [(0, 1), (1, 0)])  21.7 us
    pallas_call x1, Pallas kernels, feed_forward(): call(body, (4,), specs + [ANY] * n, out_spec, out_shape, scratch=weights....  17.6 us
    ppermute x21, starting transfers between devices, mp_perm(): return lax.ppermute(value, 'mp', [(i, i ^ s) for i in range(4)])  14.9 us
    ppermute x10, starting transfers between devices, rep_perm(): return lax.ppermute(value, 'rep', [(0, 1), (1, 0)])  12.1 us
    pallas_call x1, Pallas kernels, project(): call(body, (steps,), [pl.BlockSpec((block, width), lambda i, *_: (i & 3,...  7.97 us
    pallas_call x2, Pallas kernels, normalise(): call(body, (pages,), [pl.BlockSpec((1, page, width), lambda i, t: (t[i],...  7.8 us
  transfers between devices with their start and end apart: 40, of which 21 were waited for; matrix products, arithmetic and copies ran while one was open for 8% of the time, Pallas kernels for 8%

profile of v3, /device:TPU:0, one launch (start us, length us, event | category | flops | bytes accessed | tf_op | source)
XLA Modules:
  0.0 314.9 jit_solution(9755613801724349354)
XLA Ops:
  7.8 2.2 copy-done.1
  12.5 5.7 %collective-permute-start.8 = (bf16[128,2048]{1,0:T(8,128)(2,1)}, bf16[128,2048]{1,0:T(8,128)(2,1)}, u32[]{:S(2)}, u32[]{:S(2)}) collective-permute-start(bf16[128,2048]{1,0:T(8,128)(2,1)} %shard_map.109), channel_id=1, source_target_pairs={{0,8},{24,16},{1,9},{25,17},{2,10},{26,18},{3,11},{27,19},{4,12},{... | collective-permute-start | bytes 1572872 | tf_op jit(solution)/shard_map/ppermute | solution.py:585
  26.3 3.6 %shard_map.114 = bf16[4,128,2176]{2,1,0:T(8,128)(2,1)S(1)} custom-call(s32[9]{0:T(128)S(1)} %stack.134.ids_ref, f32[2,128,5632]{2,1,0:T(8,128)} %refs_3_.1, f32[2,128,5632]{2,1,0:T(8,128)} %refs_3_.1, f32[2,128,5632]{2,1,0:T(8,128)} %refs_3_.1, f32[2,128,5632]{2,1,0:T(8,128)} %refs_3_.1, f32[5632,128]{1,0:T(8,128)S(1)} %copy-done.2, f32[5632,128]{1,0:T(8,128)S(1)} %copy-done.2), custom_call_target="tpu_custom_call" | custom-call | bytes 6684672 | tf_op jit(solution)/shard_map/pallas_call | solution.py:169
  36.1 6.9 %collective-permute-start.4 = (bf16[512,1024]{1,0:T(8,128)(2,1)S(1)}, bf16[512,1024]{1,0:T(8,128)(2,1)}, u32[]{:S(2)}, u32[]{:S(2)}) collective-permute-start(bf16[512,1024]{1,0:T(8,128)(2,1)S(1)} %pad_maximum_fusion.3.refs_5_.refs_6_), channel_id=1, source_target_pairs={{0,8},{24,16},{1,9},{25,17},{2,10},{26,18},{3,11},{27,19},{4,12},{... | collective-permute-start | bytes 3145736 | tf_op jit(solution)/shard_map/ppermute | solution.py:605
  45.4 6.0 %shard_map.111.refs_2_ = bf16[1024,2048]{1,0:T(8,128)(2,1)S(1)} custom-call(s32[8]{0:T(128)S(1)} %copy-done.7, bf16[8,128,2048]{2,1,0:T(8,128)(2,1)} %x_ref.3, f32[1,2048]{1,0:T(1,128)S(1)} %bitcast.206), custom_call_target="tpu_custom_call" | custom-call | flops 8388608 | bytes 8388608 | tf_op jit(solution)/shard_map/pallas_call | solution.py:221
  51.5 6.5 %collective-permute-done.12 = bf16[2,64,2048]{2,1,0:T(8,128)(2,1)S(1)} collective-permute-done((bf16[2,64,2048]{2,1,0:T(8,128)(2,1)S(1)}, bf16[2,64,2048]{2,1,0:T(8,128)(2,1)S(1)}, u32[]{:S(2)}, u32[]{:S(2)}) %collective-permute-start.12) | collective-permute-done | bytes 524320 | tf_op jit(solution)/shard_map/ppermute | solution.py:180
  58.5 3.4 %collective-permute-done.4.refs_7_.refs_8_ = bf16[512,1024]{1,0:T(8,128)(2,1)} collective-permute-done((bf16[512,1024]{1,0:T(8,128)(2,1)S(1)}, bf16[512,1024]{1,0:T(8,128)(2,1)}, u32[]{:S(2)}, u32[]{:S(2)}) %collective-permute-start.4) | collective-permute-done | bytes 1048608 | tf_op jit(solution)/shard_map/ppermute | solution.py:605
  68.0 10.0 %collective-permute-done.32 = bf16[128,2176]{1,0:T(8,128)(2,1)} collective-permute-done((bf16[128,2176]{1,0:T(8,128)(2,1)}, bf16[128,2176]{1,0:T(8,128)(2,1)}, u32[]{:S(2)}, u32[]{:S(2)}) %collective-permute-start.32) | collective-permute-done | bytes 557088 | tf_op jit(solution)/shard_map/ppermute | solution.py:180
  78.0 2.9 pad_maximum_fusion
  83.5 8.0 %shard_map.112 = (bf16[2048,256]{1,0:T(8,128)(2,1)S(1)}, bf16[2048,256]{1,0:T(8,128)(2,1)S(1)}, bf16[2048,256]{1,0:T(8,128)(2,1)S(1)}, f32[16,1,256]{2,1,0:T(1,128)S(1)}, bf16[2,144,128]{2,1,0:T(8,128)(2,1)S(1)}) custom-call(s32[9]{0:T(128)S(1)} %stack.134.ids_ref, s32[16]{0:T(128)S(1)} %get-tuple-element.64.refs_0_, ...), custom_call_target="tpu_custom_call" | custom-call | flops 6442450944 | bytes 12582912 | tf_op jit(solution)/shard_map/pallas_call | solution.py:314
  92.2 7.3 %shard_map.113 = (bf16[2,2,2,256,512]{4,3,2,1,0:T(8,128)(2,1)}, bf16[2,2,2,256,512]{4,3,2,1,0:T(8,128)(2,1)}, bf16[2,2,2,256,512]{4,3,2,1,0:T(8,128)(2,1)}, bf16[2,2,2,256,512]{4,3,2,1,0:T(8,128)(2,1)}) custom-call(s32[9]{0:T(128)S(1)} %stack.134.ids_ref, s32[16]{0:T(128)S(1)} %slice_reduce_fusion.refs_1_.refs_0_, ...), custom_call_target="tpu_custom_call" | custom-call | flops 2147483648 | bytes 8388608 | tf_op jit(solution)/shard_map/pallas_call | solution.py:435
  99.6 4.4 %collective-permute-done.15 = bf16[2,2,2,256,512]{4,3,2,1,0:T(8,128)(2,1)S(1)} collective-permute-done((bf16[2,2,2,256,512]{4,3,2,1,0:T(8,128)(2,1)}, bf16[2,2,2,256,512]{4,3,2,1,0:T(8,128)(2,1)S(1)}, u32[]{:S(2)}, u32[]{:S(2)}) %collective-permute-start.15) | collective-permute-done | bytes 2097184 | tf_op jit(solution)/shard_map/ppermute | solution.py:180
  108.7 10.8 %collective-permute-done.17 = bf16[2,256,512]{2,1,0:T(8,128)(2,1)S(1)} collective-permute-done((bf16[2,256,512]{2,1,0:T(8,128)(2,1)S(1)}, bf16[2,256,512]{2,1,0:T(8,128)(2,1)S(1)}, u32[]{:S(2)}, u32[]{:S(2)}) %collective-permute-start.17) | collective-permute-done | bytes 524320 | tf_op jit(solution)/shard_map/ppermute | solution.py:180
  124.7 5.2 %collective-permute-done.24 = bf16[256,512]{1,0:T(8,128)(2,1)S(1)} collective-permute-done((bf16[256,512]{1,0:T(8,128)(2,1)S(1)}, bf16[256,512]{1,0:T(8,128)(2,1)S(1)}, u32[]{:S(2)}, u32[]{:S(2)}) %collective-permute-start.24) | collective-permute-done | bytes 262176 | tf_op jit(solution)/shard_map/ppermute | solution.py:184
  137.5 7.8 %collective-permute-done.21 = bf16[2,256,512]{2,1,0:T(8,128)(2,1)S(1)} collective-permute-done((bf16[2,256,512]{2,1,0:T(8,128)(2,1)S(1)}, bf16[2,256,512]{2,1,0:T(8,128)(2,1)S(1)}, u32[]{:S(2)}, u32[]{:S(2)}) %collective-permute-start.21) | collective-permute-done | bytes 524320 | tf_op jit(solution)/shard_map/ppermute | solution.py:180
  150.0 3.6 %collective-permute-done.22 = bf16[256,512]{1,0:T(8,128)(2,1)S(1)} collective-permute-done((bf16[256,512]{1,0:T(8,128)(2,1)}, bf16[256,512]{1,0:T(8,128)(2,1)S(1)}, u32[]{:S(2)}, u32[]{:S(2)}) %collective-permute-start.22) | collective-permute-done | bytes 262176 | tf_op jit(solution)/shard_map/ppermute | solution.py:184
  156.9 75.9 %collective-permute-done.25 = bf16[512,512]{1,0:T(8,128)(2,1)S(1)} collective-permute-done((bf16[512,512]{1,0:T(8,128)(2,1)}, bf16[512,512]{1,0:T(8,128)(2,1)S(1)}, u32[]{:S(2)}, u32[]{:S(2)}) %collective-permute-start.25) | collective-permute-done | bytes 524320 | tf_op jit(solution)/shard_map/ppermute | solution.py:646
  236.1 5.5 %collective-permute-done.28 = bf16[256,512]{1,0:T(8,128)(2,1)S(1)} collective-permute-done((bf16[256,512]{1,0:T(8,128)(2,1)S(1)}, bf16[256,512]{1,0:T(8,128)(2,1)S(1)}, u32[]{:S(2)}, u32[]{:S(2)}) %collective-permute-start.28) | collective-permute-done | bytes 262176 | tf_op jit(solution)/shard_map/ppermute | solution.py:184
  243.8 10.8 %collective-permute-done.29 = bf16[2,256,512]{2,1,0:T(8,128)(2,1)S(1)} collective-permute-done((bf16[2,256,512]{2,1,0:T(8,128)(2,1)S(1)}, bf16[2,256,512]{2,1,0:T(8,128)(2,1)S(1)}, u32[]{:S(2)}, u32[]{:S(2)}) %collective-permute-start.29) | collective-permute-done | bytes 524320 | tf_op jit(solution)/shard_map/ppermute | solution.py:180
  257.6 4.3 %collective-permute-done.30.o_ref = bf16[2,2,2,256,512]{4,3,2,1,0:T(8,128)(2,1)} collective-permute-done((bf16[2,2,2,256,512]{4,3,2,1,0:T(8,128)(2,1)S(1)}, bf16[2,2,2,256,512]{4,3,2,1,0:T(8,128)(2,1)}, u32[]{:S(2)}, u32[]{:S(2)}) %collective-permute-start.30) | collective-permute-done | bytes 2097184 | tf_op jit(solution)/shard_map/ppermute | solution.py:180
  261.9 17.6 %shard_map.115 = (bf16[2,2,2,256,512]{4,3,2,1,0:T(8,128)(2,1)S(1)}, bf16[2,2,2,256,512]{4,3,2,1,0:T(8,128)(2,1)S(1)}) custom-call(s32[9]{0:T(128)S(1)} %stack.134.ids_ref, bf16[2,2,2,256,512]{4,3,2,1,0:T(8,128)(2,1)} %copy-done.12, bf16[2,2,2,256,512]{4,3,2,1,0:T(8,128)(2,1)} %collective-permute-done.30.o_ref, f32[4,1,512]{2,1,0:T(1,128)S(1)} %bitcast.208, ...), custom_call_target="tpu_custom_call" | custom-call | flops 9126805504 | bytes 21495808 | tf_op jit(solution)/shard_map/pallas_call | solution.py:538
  279.8 4.0 %collective-permute-done.34 = bf16[2,2,2,256,512]{4,3,2,1,0:T(8,128)(2,1)S(1)} collective-permute-done((bf16[2,2,2,256,512]{4,3,2,1,0:T(8,128)(2,1)S(1)}, bf16[2,2,2,256,512]{4,3,2,1,0:T(8,128)(2,1)S(1)}, u32[]{:S(2)}, u32[]{:S(2)}) %collective-permute-start.34) | collective-permute-done | bytes 2097184 | tf_op jit(solution)/shard_map/ppermute | solution.py:180
  287.2 10.9 %collective-permute-done.37 = bf16[2,256,512]{2,1,0:T(8,128)(2,1)S(1)} collective-permute-done((bf16[2,256,512]{2,1,0:T(8,128)(2,1)S(1)}, bf16[2,256,512]{2,1,0:T(8,128)(2,1)S(1)}, u32[]{:S(2)}, u32[]{:S(2)}) %collective-permute-start.37) | collective-permute-done | bytes 524320 | tf_op jit(solution)/shard_map/ppermute | solution.py:180
  301.1 4.7 %collective-permute-done.38 = bf16[256,512]{1,0:T(8,128)(2,1)S(1)} collective-permute-done((bf16[256,512]{1,0:T(8,128)(2,1)S(1)}, bf16[256,512]{1,0:T(8,128)(2,1)S(1)}, u32[]{:S(2)}, u32[]{:S(2)}) %collective-permute-start.38) | collective-permute-done | bytes 262176 | tf_op jit(solution)/shard_map/ppermute | solution.py:184
  (185 shorter events, 72.9 us)
Async XLA Ops:
  6.5 255.4 %all-gather.3.cloned.1.call-start = ((), (), s32[]{:S(2)}) async-start(), calls=%async_computation | async-start | bytes 11141120 | tf_op jit(solution)/shard_map/all_gather | solution.py:579
  12.5 17.4 %collective-permute-start.8 = (bf16[128,2048]{1,0:T(8,128)(2,1)}, bf16[128,2048]{1,0:T(8,128)(2,1)}, u32[]{:S(2)}, u32[]{:S(2)}) collective-permute-start(bf16[128,2048]{1,0:T(8,128)(2,1)} %shard_map.109), channel_id=1, source_target_pairs={{0,8},{24,16},{1,9},{25,17},{2,10},{26,18},{3,11},{27,19},{4,12},{... | collective-permute-start | bytes 1572872 | tf_op jit(solution)/shard_map/ppermute | solution.py:585
  21.0 13.3 %collective-permute-start.2 = (bf16[128,1024]{1,0:T(8,128)(2,1)S(1)}, bf16[128,1024]{1,0:T(8,128)(2,1)S(1)}, u32[]{:S(2)}, u32[]{:S(2)}) collective-permute-start(bf16[128,1024]{1,0:T(8,128)(2,1)S(1)} %get-tuple-element.82), channel_id=1, source_target_pairs={{0,6},{2,4},{4,2},{6,0},{1,7},{3,5},{5,3},{7,1},{8,14},{10,12},{12... | collective-permute-start | bytes 786440 | tf_op jit(solution)/shard_map/ppermute | solution.py:180
  21.7 13.5 %collective-permute-start.1 = (bf16[128,1024]{1,0:T(8,128)(2,1)S(1)}, bf16[128,1024]{1,0:T(8,128)(2,1)S(1)}, u32[]{:S(2)}, u32[]{:S(2)}) collective-permute-start(bf16[128,1024]{1,0:T(8,128)(2,1)S(1)} %get-tuple-element.83), channel_id=1, source_target_pairs={{0,4},{2,6},{4,0},{6,2},{1,5},{3,7},{5,1},{7,3},{8,12},{10,14},{12... | collective-permute-start | bytes 786440 | tf_op jit(solution)/shard_map/ppermute | solution.py:180
  22.6 12.6 %collective-permute-start = (bf16[128,1024]{1,0:T(8,128)(2,1)S(1)}, bf16[128,1024]{1,0:T(8,128)(2,1)S(1)}, u32[]{:S(2)}, u32[]{:S(2)}) collective-permute-start(bf16[128,1024]{1,0:T(8,128)(2,1)S(1)} %get-tuple-element.84), channel_id=1, source_target_pairs={{0,2},{2,0},{4,6},{6,4},{1,3},{3,1},{5,7},{7,5},{8,10},{10,8},{12,... | collective-permute-start | bytes 786440 | tf_op jit(solution)/shard_map/ppermute | solution.py:180
  31.0 11.9 %collective-permute-start.11 = (bf16[64,2048]{1,0:T(8,128)(2,1)S(1)}, bf16[64,2048]{1,0:T(8,128)(2,1)S(1)}, u32[]{:S(2)}, u32[]{:S(2)}) collective-permute-start(bf16[64,2048]{1,0:T(8,128)(2,1)S(1)} %get-tuple-element.97), channel_id=1, source_target_pairs={{0,1},{1,0},{2,3},{3,2},{4,5},{5,4},{6,7},{7,6},{8,9},{9,8},{10,11... | collective-permute-start | bytes 786440 | tf_op jit(solution)/shard_map/ppermute | solution.py:184
  35.3 28.4 %collective-permute-start.3 = (bf16[512,1024]{1,0:T(8,128)(2,1)S(1)}, bf16[512,1024]{1,0:T(8,128)(2,1)S(1)}, u32[]{:S(2)}, u32[]{:S(2)}) collective-permute-start(bf16[512,1024]{1,0:T(8,128)(2,1)S(1)} %pad_maximum_fusion.3.refs_5_.refs_6_), channel_id=1, source_target_pairs={{8,16},{16,8},{9,17},{17,9},{10,18},{18,10},{11,19},{19,11},{12,20... | collective-permute-start | bytes 3145736 | tf_op jit(solution)/shard_map/ppermute | solution.py:604
  36.1 25.9 %collective-permute-start.4 = (bf16[512,1024]{1,0:T(8,128)(2,1)S(1)}, bf16[512,1024]{1,0:T(8,128)(2,1)}, u32[]{:S(2)}, u32[]{:S(2)}) collective-permute-start(bf16[512,1024]{1,0:T(8,128)(2,1)S(1)} %pad_maximum_fusion.3.refs_5_.refs_6_), channel_id=1, source_target_pairs={{0,8},{24,16},{1,9},{25,17},{2,10},{26,18},{3,11},{27,19},{4,12},{... | collective-permute-start | bytes 3145736 | tf_op jit(solution)/shard_map/ppermute | solution.py:605
  43.0 14.9 %collective-permute-start.12 = (bf16[2,64,2048]{2,1,0:T(8,128)(2,1)S(1)}, bf16[2,64,2048]{2,1,0:T(8,128)(2,1)S(1)}, u32[]{:S(2)}, u32[]{:S(2)}) collective-permute-start(bf16[2,64,2048]{2,1,0:T(8,128)(2,1)S(1)} %get-tuple-element.100), channel_id=1, source_target_pairs={{0,4},{2,6},{4,0},{6,2},{1,5},{3,7},{5,1},{7,3},{8,12},{10,14},{12... | collective-permute-start | bytes 1572872 | tf_op jit(solution)/shard_map/ppermute | solution.py:180
  43.7 18.3 %collective-permute-start.10 = (bf16[2,64,2048]{2,1,0:T(8,128)(2,1)S(1)}, bf16[2,64,2048]{2,1,0:T(8,128)(2,1)S(1)}, u32[]{:S(2)}, u32[]{:S(2)}) collective-permute-start(bf16[2,64,2048]{2,1,0:T(8,128)(2,1)S(1)} %get-tuple-element.94), channel_id=1, source_target_pairs={{0,1},{1,0},{2,3},{3,2},{4,5},{5,4},{6,7},{7,6},{8,9},{9,8},{10,11... | collective-permute-start | bytes 1572872 | tf_op jit(solution)/shard_map/ppermute | solution.py:184
  45.4 22.6 %collective-permute-start.33 = (bf16[128,2176]{1,0:T(8,128)(2,1)}, bf16[128,2176]{1,0:T(8,128)(2,1)}, u32[]{:S(2)}, u32[]{:S(2)}) collective-permute-start(bf16[128,2176]{1,0:T(8,128)(2,1)} %get-tuple-element.78), channel_id=1, source_target_pairs={{0,6},{2,4},{4,2},{6,0},{1,7},{3,5},{5,3},{7,1},{8,14},{10,12},{12... | collective-permute-start | bytes 1671176 | tf_op jit(solution)/shard_map/ppermute | solution.py:180
  57.9 20.1 %collective-permute-start.32 = (bf16[128,2176]{1,0:T(8,128)(2,1)}, bf16[128,2176]{1,0:T(8,128)(2,1)}, u32[]{:S(2)}, u32[]{:S(2)}) collective-permute-start(bf16[128,2176]{1,0:T(8,128)(2,1)} %get-tuple-element.79), channel_id=1, source_target_pairs={{0,4},{2,6},{4,0},{6,2},{1,5},{3,7},{5,1},{7,3},{8,12},{10,14},{12... | collective-permute-start | bytes 1671176 | tf_op jit(solution)/shard_map/ppermute | solution.py:180
  62.0 16.1 %collective-permute-start.31 = (bf16[128,2176]{1,0:T(8,128)(2,1)S(1)}, bf16[128,2176]{1,0:T(8,128)(2,1)}, u32[]{:S(2)}, u32[]{:S(2)}) collective-permute-start(bf16[128,2176]{1,0:T(8,128)(2,1)S(1)} %get-tuple-element.80), channel_id=1, source_target_pairs={{0,2},{2,0},{4,6},{6,4},{1,3},{3,1},{5,7},{7,5},{8,10},{10,8},{12,... | collective-permute-start | bytes 1671176 | tf_op jit(solution)/shard_map/ppermute | solution.py:180
  62.0 19.0 %collective-permute-start.5 = (bf16[512,1024]{1,0:T(8,128)(2,1)}, bf16[512,1024]{1,0:T(8,128)(2,1)}, u32[]{:S(2)}, u32[]{:S(2)}) collective-permute-start(bf16[512,1024]{1,0:T(8,128)(2,1)} %collective-permute-done.4.refs_7_.refs_8_), channel_id=1, source_target_pairs={{8,16},{16,8},{9,17},{17,9},{10,18},{18,10},{11,19},{19,11},{12,20... | collective-permute-start | bytes 3145736 | tf_op jit(solution)/shard_map/ppermute | solution.py:606
  66.0 17.5 %collective-permute-start.13 = (bf16[2,2,2,64,2048]{4,3,2,1,0:T(8,128)(2,1)}, bf16[2,2,2,64,2048]{4,3,2,1,0:T(8,128)(2,1)}, u32[]{:S(2)}, u32[]{:S(2)}) collective-permute-start(bf16[2,2,2,64,2048]{4,3,2,1,0:T(8,128)(2,1)} %pad_maximum_fusion.1.refs_3_), channel_id=1, source_target_pairs={{0,2},{2,0},{4,6},{6,4},{1,3},{3,1},{5,7},{7,5},{8,10},{10,8},{12,... | collective-permute-start | bytes 6291464 | tf_op jit(solution)/shard_map/ppermute | solution.py:180
  105.5 14.0 %collective-permute-start.17 = (bf16[2,256,512]{2,1,0:T(8,128)(2,1)S(1)}, bf16[2,256,512]{2,1,0:T(8,128)(2,1)S(1)}, u32[]{:S(2)}, u32[]{:S(2)}) collective-permute-start(bf16[2,256,512]{2,1,0:T(8,128)(2,1)S(1)} %get-tuple-element.76), channel_id=1, source_target_pairs={{0,4},{2,6},{4,0},{6,2},{1,5},{3,7},{5,1},{7,3},{8,12},{10,14},{12... | collective-permute-start | bytes 1572872 | tf_op jit(solution)/shard_map/ppermute | solution.py:180
  107.2 13.8 %collective-permute-start.16 = (bf16[2,256,512]{2,1,0:T(8,128)(2,1)S(1)}, bf16[2,256,512]{2,1,0:T(8,128)(2,1)S(1)}, u32[]{:S(2)}, u32[]{:S(2)}) collective-permute-start(bf16[2,256,512]{2,1,0:T(8,128)(2,1)S(1)} %get-tuple-element.74), channel_id=1, source_target_pairs={{0,1},{1,0},{2,3},{3,2},{4,5},{5,4},{6,7},{7,6},{8,9},{9,8},{10,11... | collective-permute-start | bytes 1572872 | tf_op jit(solution)/shard_map/ppermute | solution.py:184
  131.6 13.7 %collective-permute-start.21 = (bf16[2,256,512]{2,1,0:T(8,128)(2,1)S(1)}, bf16[2,256,512]{2,1,0:T(8,128)(2,1)S(1)}, u32[]{:S(2)}, u32[]{:S(2)}) collective-permute-start(bf16[2,256,512]{2,1,0:T(8,128)(2,1)S(1)} %get-tuple-element.72), channel_id=1, source_target_pairs={{0,4},{2,6},{4,0},{6,2},{1,5},{3,7},{5,1},{7,3},{8,12},{10,14},{12... | collective-permute-start | bytes 1572872 | tf_op jit(solution)/shard_map/ppermute | solution.py:180
  133.8 13.8 %collective-permute-start.19 = (bf16[2,256,512]{2,1,0:T(8,128)(2,1)S(1)}, bf16[2,256,512]{2,1,0:T(8,128)(2,1)S(1)}, u32[]{:S(2)}, u32[]{:S(2)}) collective-permute-start(bf16[2,256,512]{2,1,0:T(8,128)(2,1)S(1)} %get-tuple-element.70), channel_id=1, source_target_pairs={{0,1},{1,0},{2,3},{3,2},{4,5},{5,4},{6,7},{7,6},{8,9},{9,8},{10,11... | collective-permute-start | bytes 1572872 | tf_op jit(solution)/shard_map/ppermute | solution.py:184
  136.0 96.8 %collective-permute-start.25 = (bf16[512,512]{1,0:T(8,128)(2,1)}, bf16[512,512]{1,0:T(8,128)(2,1)S(1)}, u32[]{:S(2)}, u32[]{:S(2)}) collective-permute-start(bf16[512,512]{1,0:T(8,128)(2,1)} %pad_maximum_fusion.6), channel_id=1, source_target_pairs={{8,0},{16,24},{9,1},{17,25},{10,2},{18,26},{11,3},{19,27},{12,4},{... | collective-permute-start | bytes 1572872 | tf_op jit(solution)/shard_map/ppermute | solution.py:646
  241.7 13.0 %collective-permute-start.29 = (bf16[2,256,512]{2,1,0:T(8,128)(2,1)S(1)}, bf16[2,256,512]{2,1,0:T(8,128)(2,1)S(1)}, u32[]{:S(2)}, u32[]{:S(2)}) collective-permute-start(bf16[2,256,512]{2,1,0:T(8,128)(2,1)S(1)} %get-tuple-element.92), channel_id=1, source_target_pairs={{0,4},{2,6},{4,0},{6,2},{1,5},{3,7},{5,1},{7,3},{8,12},{10,14},{12... | collective-permute-start | bytes 1572872 | tf_op jit(solution)/shard_map/ppermute | solution.py:180
  243.3 12.7 %collective-permute-start.27 = (bf16[2,256,512]{2,1,0:T(8,128)(2,1)S(1)}, bf16[2,256,512]{2,1,0:T(8,128)(2,1)S(1)}, u32[]{:S(2)}, u32[]{:S(2)}) collective-permute-start(bf16[2,256,512]{2,1,0:T(8,128)(2,1)S(1)} %get-tuple-element.86), channel_id=1, source_target_pairs={{0,1},{1,0},{2,3},{3,2},{4,5},{5,4},{6,7},{7,6},{8,9},{9,8},{10,11... | collective-permute-start | bytes 1572872 | tf_op jit(solution)/shard_map/ppermute | solution.py:184
  284.1 14.0 %collective-permute-start.37 = (bf16[2,256,512]{2,1,0:T(8,128)(2,1)S(1)}, bf16[2,256,512]{2,1,0:T(8,128)(2,1)S(1)}, u32[]{:S(2)}, u32[]{:S(2)}) collective-permute-start(bf16[2,256,512]{2,1,0:T(8,128)(2,1)S(1)} %get-tuple-element.68), channel_id=1, source_target_pairs={{0,4},{2,6},{4,0},{6,2},{1,5},{3,7},{5,1},{7,3},{8,12},{10,14},{12... | collective-permute-start | bytes 1572872 | tf_op jit(solution)/shard_map/ppermute | solution.py:180
  285.6 13.8 %collective-permute-start.35 = (bf16[2,256,512]{2,1,0:T(8,128)(2,1)S(1)}, bf16[2,256,512]{2,1,0:T(8,128)(2,1)S(1)}, u32[]{:S(2)}, u32[]{:S(2)}) collective-permute-start(bf16[2,256,512]{2,1,0:T(8,128)(2,1)S(1)} %get-tuple-element.66), channel_id=1, source_target_pairs={{0,1},{1,0},{2,3},{3,2},{4,5},{5,4},{6,7},{7,6},{8,9},{9,8},{10,11... | collective-permute-start | bytes 1572872 | tf_op jit(solution)/shard_map/ppermute | solution.py:184
  (41 other events, 231.5 us)
Sparse Core Ops, SparseCore 0:
  81.1 180.4 all-gather.2

commit v4 on v3

--- a/solution.py
+++ b/solution.py
@@ -62,7 +62,7 @@
     def __init__(self, arrays, low=0, high=None):
         self.arrays = list(arrays)
         self.planes, self.rows, columns = (
-            self.arrays[0].shape if len(self.arrays) == 1 else (len(arrays), *self.arrays[0].shape)
+            self.arrays[0].shape if len(self.arrays) == 1 else (4, *self.arrays[0].shape)
         )
         self.part = slice(low, columns if high is None else high)
         self.scratch = [
@@ -70,23 +70,32 @@
             pltpu.SemaphoreType.DMA((self.planes * 4,)),
         ]
 
-    def copies(self, ids_ref, refs, held, sems):
+    def copies(self, ids_ref, refs, held, sems, plane, ref):
         rows = self.rows // 4
-        for i in range(self.planes):
-            ref, plane = (refs[0].at[i], i) if len(refs) == 1 else (refs[i], ids_ref[3 + i])
-            for s in range(4):
-                to = pl.multiple_of((plane * 4 + (ids_ref[0] ^ s)) * rows, rows)
-                yield pltpu.make_async_copy(
-                    ref.at[pl.ds(s * rows, rows), self.part], held.at[pl.ds(to, rows)], sems.at[4 * i + s]
-                )
-
-    def start(self, *where):
-        for copy in self.copies(*where):
-            copy.start()
-
-    def wait(self, *where):
-        for copy in self.copies(*where):
-            copy.wait()
+        to_plane = plane if len(refs) == 1 else ids_ref[(9 if len(refs) == 6 else 3) + plane]
+        for s in range(4):
+            to = pl.multiple_of((to_plane * 4 + (ids_ref[0] ^ s)) * rows, rows)
+            yield pltpu.make_async_copy(
+                ref.at[pl.ds(s * rows, rows), self.part], held.at[pl.ds(to, rows)], sems.at[4 * plane + s]
+            )
+
+    def start(self, ids_ref, refs, held, sems):
+        def begin(plane, ref):
+            for copy in self.copies(ids_ref, refs, held, sems, plane, ref):
+                copy.start()
+
+        for plane in range(self.planes):
+            if len(refs) == 6 and plane >= 2:
+                pl.when(ids_ref[2] == 1)(functools.partial(begin, plane, refs[2 * plane - 2]))
+                pl.when(ids_ref[2] == 0)(functools.partial(begin, plane, refs[2 * plane - 1]))
+            else:
+                begin(plane, refs[0].at[plane] if len(refs) == 1 else refs[plane])
+
+    def wait(self, ids_ref, refs, held, sems):
+        for plane in range(self.planes):
+            ref = refs[0].at[plane] if len(refs) == 1 else refs[plane]
+            for copy in self.copies(ids_ref, refs, held, sems, plane, ref):
+                copy.wait()
 
 
 def pack_mixer(ids, mixer_in, mixer_out):
@@ -122,16 +131,16 @@
         assert hidden_all == (8 * tiles + 4) * 128
         self.near = tiles * 128
         self.near_up = 2 * self.near + 128
-        self.near_all = self.near_up + self.near + 128
+        self.units = self.near + 128
 
 
 def pack_feed(ids, gate_up, down, feed):
     width = gate_up.shape[1]
-    near, up, both = feed.near, feed.near_up, feed.near_all
+    near, up = feed.near, feed.near_up
+    shapes = [(width, up), (near + 64, width)]
 
     def body(ids_ref, *refs):
-        g_ref, u_ref, gh_ref, uh_ref, d_ref, dh_ref = refs[:6]
-        out_ref = refs[-1]
+        g_ref, u_ref, gh_ref, uh_ref, d_ref, dh_ref, out_ref, down_ref = refs
         odd = (ids_ref[0] ^ pl.program_id(0)) % 2
         out_ref[0, :, 0:near] = g_ref[0].astype(BF)
         lane = lax.broadcasted_iota(jnp.int32, (width, 128), 1)
@@ -140,16 +149,14 @@
         odd_mix = jnp.where(lane < 64, pltpu.roll(gh, 64, 1), uh)
         out_ref[0, :, near : near + 128] = jnp.where(odd == 1, odd_mix, even_mix).astype(BF)
         out_ref[0, :, near + 128 : up] = u_ref[0].astype(BF)
-        out_ref[0, :, up : up + near] = d_ref[...].T.astype(BF)
-        last = jnp.concatenate([dh_ref[...], jnp.zeros((64, width), F32)], axis=0)
-        out_ref[0, :, up + near : both] = last.T.astype(BF)
+        down_ref[0, 0:near] = d_ref[...].astype(BF)
+        down_ref[0, near : near + 64] = dh_ref[...].astype(BF)
 
     def dest(s, r):
         return 4 * r[1] + (r[0] ^ s)
 
     def tile(s, r):
         return feed.half_at + 2 * r[1] + (r[0] ^ s) // 2
-
 
     def cols(i):
         return pl.BlockSpec((1, width, near), lambda s, r: (i, 0, dest(s, r)))
@@ -170,9 +177,9 @@
         body,
         (4,),
         in_specs,
-        pl.BlockSpec((1, width, both), lambda s, r: (s, 0, 0)),
-        jax.ShapeDtypeStruct((4, width, both), BF),
-        cost=(0, 4 * width * both * 6),
+        [pl.BlockSpec((1, *shape), lambda s, r: (s, 0, 0)) for shape in shapes],
+        [jax.ShapeDtypeStruct((4, *shape), BF) for shape in shapes],
+        cost=(0, 4 * width * (up + near + 64) * 6),
     )(ids, *args)
 
 
@@ -240,7 +247,7 @@
     pages = live.shape[0]
     rows = cnt_col.shape[0]
     page = rows // pages
-    group = 2
+    group = 4
     steps = pages // group
 
     n = len(weights.arrays)
@@ -263,10 +270,13 @@
 
         x = x_ref[...]
         if foreign:
-            mine, other = (f[:, 0, 0].reshape(page, width) for f in f_refs)
-            low = (ids_ref[0] & 1) == 0
-            pair = jnp.concatenate([jnp.where(low, mine, other), jnp.where(low, other, mine)], axis=0)
-            x = jnp.where((step >> 2) == ids_ref[8], x, pair)
+            core, y = ids_ref[0] & 1, ids_ref[0] >> 1
+            tiles = []
+            for q in range(group):
+                near, far = ([f[:, 0, dy].reshape(page, width) for dy in range(2)] for f in f_refs)
+                row = [jnp.where(core == q % 2, a, b) for a, b in zip(near, far)]
+                tiles.append(jnp.where(y == q // 2, row[0], row[1]))
+            x = jnp.where((step >> 1) == ids_ref[8], x, jnp.concatenate(tiles, axis=0))
         proj = nn(x, held[...])
         row = lax.broadcasted_iota(jnp.int32, (page, page), 0)
         col = lax.broadcasted_iota(jnp.int32, (page, page), 1)
@@ -315,12 +325,11 @@
         body,
         (steps,),
         [
-            pl.BlockSpec((block, width), lambda i, *_: (i & 3, 0)),
+            pl.BlockSpec((block, width), lambda i, *_: (i & 1, 0)),
         ]
         + [
             pl.BlockSpec(
-                (2, 1, 1, page // 2, width),
-                lambda i, r, *_: (0, ((i >> 1) & 1) ^ r[1], (i & 1) ^ (r[0] >> 1), 0, 0),
+                (2, 1, 2, page // 2, width), lambda i, r, *_: (0, (i & 1) ^ r[1], 0, 0, 0)
             )
         ]
         * len(foreign)
@@ -354,11 +363,11 @@
     heads = cols // HEAD
     pages = fin.shape[0]
     page = rows // pages
-    group = 2
+    group = 4
     steps = pages // group
     width = weights.planes * weights.rows
     n = len(earlier)
-    spans = steps // 4
+    spans = steps // 2
     m = n + 4 + len(weights.arrays)
 
     def body(ids_ref, *refs):
@@ -417,20 +426,20 @@
                 term = nt(hn, held[block_of(ids_ref[0] ^ (2 * dy + dc), width // 4), :]).astype(BF)
                 for span in range(spans):
 
-                    @pl.when((step // 4) ^ ids_ref[8] == span)
+                    @pl.when((step // 2) ^ ids_ref[8] == span)
                     def _(span=span, dc=dc, dy=dy, term=term):
-                        outs[2 * span + dc][0, 0, dy] = term
+                        outs[2 * span + dc][:, 0, dy] = term.reshape(2, block // 2, width // 4)
 
     block = group * page
     rowspec = pl.BlockSpec((block, cols), lambda i, *_: (i, 0))
 
     def terms(span):
         def index(i, r, l):
-            low = 4 * (span ^ r[8])
-            i = jnp.minimum(jnp.maximum(i, low), low + 3) & 3
-            return (i % 2, (i // 2) ^ r[1], 0, 0, 0)
-
-        return pl.BlockSpec((1, 1, 2, block, width // 4), index)
+            low = 2 * (span ^ r[8])
+            i = jnp.minimum(jnp.maximum(i, low), low + 1) & 1
+            return (0, i ^ r[1], 0, 0, 0)
+
+        return pl.BlockSpec((2, 1, 2, block // 2, width // 4), index)
 
     return call(
         body,
@@ -448,7 +457,7 @@
             pl.BlockSpec((group, 1, page), lambda i, *_: (i, 0, 0)),
         ],
         [terms(span) for span in range(spans) for _ in range(2)],
-        [jax.ShapeDtypeStruct((2, 2, 2, block, width // 4), BF)] * (2 * spans),
+        [jax.ShapeDtypeStruct((2, 2, 2, block // 2, width // 4), BF)] * (2 * spans),
         scratch=[pltpu.VMEM((heads, HEAD, HEAD), F32), *weights.scratch],
         prefetch=2,
         cost=(2 * rows * cols * width, rows * width * 2),
@@ -459,11 +468,12 @@
     return (a.astype(F32) + b.astype(F32)).astype(BF)
 
 
-def sum_scatter(terms):
+def sum_scatter(terms, *others):
     mine, other = terms[0], mp_perm(terms[1], 1)
     a_keep, a_send = add(mine[0, 0], other[0, 0]), add(mine[0, 1], other[0, 1])
     b_keep, b_send = add(mine[1, :, 0], other[1, :, 0]), add(mine[1, :, 1], other[1, :, 1])
     a_came, b_came = rep_perm(a_send), mp_perm(b_send, 2)
+    a_came = after(a_came, *others)
     a_send, b_send = add(a_keep[1], a_came[1]), add(b_keep[1], b_came[1])
     a_last, b_last = mp_perm(a_send, 2), rep_perm(b_send)
     a = a_keep[0].astype(F32) + a_came[0].astype(F32) + a_last.astype(F32)
@@ -482,68 +492,88 @@
     return mine, mp_perm(mine, 1)
 
 
-def feed_inputs(ids_ref, m_ref, o_ref, g_ref):
-    mp_index = ids_ref[0]
-    places = [(dy, dc) for dy in range(2) for dc in range(2)]
-    blocks = [(m_ref, o_ref)[dc][0, 0, dy].astype(F32) for dy, dc in places]
-    square = sum(jnp.sum(b * b, axis=-1, keepdims=True) for b in blocks)
-    scale = lax.rsqrt(square / (4 * blocks[0].shape[1]) + EPS)
-    at = [mp_index ^ (2 * dy + dc) for dy, dc in places]
-    return places, at, [(b * scale * g_ref[k]).astype(BF) for k, b in zip(at, blocks)]
-
-
 def block_of(k, rows):
     return pl.ds(pl.multiple_of(k * rows, rows), rows)
 
 
-def total_of(terms):
-    out = None
-    for term in terms:
-        out = term if out is None else out + term
-    return out
-
-
-def feed_specs(mine, gain):
+def feed_up(ids, mine, other, gain, weights, feed):
+    near, up, units = feed.near, feed.near_up, feed.units
     rows, kwide = mine.shape[-2:]
-    spec = pl.BlockSpec((1, 1, 2, rows, kwide), lambda i, r: (i % 2, i // 2, 0, 0, 0))
-    return [spec, spec, whole(gain.shape)], [spec, spec], [jax.ShapeDtypeStruct((2, 2, 2, rows, kwide), BF)] * 2
-
-
-def feed_forward(ids, mine, other, gain, weights, feed):
-    near, up, both = feed.near, feed.near_up, feed.near_all
-    specs, out_spec, out_shape = feed_specs(mine, gain)
-
+    width = 4 * kwide
     n = len(weights.arrays)
+    places = [(dy, dc) for dy in range(2) for dc in range(2)]
 
     def body(ids_ref, m_ref, o_ref, g_ref, *rest):
-        w_refs, outs, (held, sems) = rest[:n], rest[n : n + 2], rest[n + 2 :]
+        w_refs, (out_ref, x_ref, held, sems) = rest[:n], rest[n:]
         first = pl.program_id(0) == 0
         pl.when(first)(lambda: weights.start(ids_ref, w_refs, held, sems))
-        places, at, xs = feed_inputs(ids_ref, m_ref, o_ref, g_ref)
+        blocks = [(m_ref, o_ref)[dc][0, 0, dy].astype(F32) for dy, dc in places]
+        square = sum(jnp.sum(b * b, axis=-1, keepdims=True) for b in blocks)
+        scale = lax.rsqrt(square / width + EPS)
+        for (dy, dc), b in zip(places, blocks):
+            k = ids_ref[0] ^ (2 * dy + dc)
+            x_ref[:, block_of(k, kwide)] = (b * scale * g_ref[k]).astype(BF)
         pl.when(first)(lambda: weights.wait(ids_ref, w_refs, held, sems))
 
-        h = total_of(nn(x, held[block_of(k, kwide), 0:up]) for k, x in zip(at, xs))
-        gate, upward = h[:, 0:near], h[:, near + 128 : up]
-        edge = h[:, near : near + 128]
-        hidden = gate * sigmoid(gate) * upward
+        x = x_ref[...]
+        h = nn(x, held[...])
+        gate, edge, upward = h[:, 0:near], h[:, near : near + 128], h[:, near + 128 : up]
+        out_ref[0, 0, :, 0:near] = (gate * sigmoid(gate) * upward).astype(BF)
         mixed = edge * sigmoid(edge) * pltpu.roll(edge, 64, 1)
         lane = lax.broadcasted_iota(jnp.int32, mixed.shape, 1)
-        mixed = jnp.where(lane < 64, mixed, 0.0)
-        hidden = jnp.concatenate([hidden, mixed], axis=1).astype(BF)
-        for (dy, dc), k in zip(places, at):
-            term = nt(hidden, held[block_of(k, kwide), up:both])
-            outs[dc][0, 0, dy] = term.astype(BF)
-
-    rows, kwide = out_shape[0].shape[-2] * 4, out_shape[0].shape[-1]
+        out_ref[0, 0, :, near:units] = jnp.where(lane < 64, mixed, 0.0).astype(BF)
+
+    spec = pl.BlockSpec((1, 1, 2, rows, kwide), lambda i, r: (i % 2, i // 2, 0, 0, 0))
     return call(
         body,
         (4,),
-        specs + [ANY] * n,
-        out_spec,
-        out_shape,
-        scratch=weights.scratch,
-        cost=(rows * 4 * kwide * both * 2, 4 * kwide * both * 2 + 6 * out_shape[0].size * 2),
+        [spec, spec, whole(gain.shape)] + [ANY] * n,
+        pl.BlockSpec((1, 1, rows, units), lambda i, r: (i % 2, i // 2, 0, 0)),
+        jax.ShapeDtypeStruct((2, 2, rows, units), BF),
+        scratch=[pltpu.VMEM((rows, width), BF), *weights.scratch],
+        cost=(8 * rows * width * up, width * up * 2 + 16 * rows * width),
     )(ids, mine, other, gain, *weights.arrays)
+
+
+def feed_down(ids, hidden, weights, kwide, dc):
+    rows, units = hidden.shape[-2:]
+    used = units - 64
+    parts = 4 if weights.ndim == 3 else 1
+
+    def body(ids_ref, h_ref, w_ref, out_ref, held, sems):
+        def copies():
+            for dy in range(2):
+                k = ids_ref[0] ^ (2 * dy + dc)
+                for s in range(parts):
+                    if parts == 1:
+                        ref, to = w_ref.at[:, block_of(k, kwide)], dy * kwide
+                    else:
+                        ref = w_ref.at[k, pl.ds(s * used, used)]
+                        to = pl.multiple_of(dy * kwide + (ids_ref[0] ^ s) * (kwide // 4), 128)
+                    to = held.at[pl.ds(0, used), pl.ds(to, kwide // parts)]
+                    yield pltpu.make_async_copy(ref, to, sems.at[parts * dy + s])
+
+        @pl.when(pl.program_id(0) == 0)
+        def _():
+            for copy in copies():
+                copy.start()
+            held[used:units, :] = jnp.zeros((units - used, 2 * kwide), BF)
+            for copy in copies():
+                copy.wait()
+
+        term = nn(h_ref[0, 0], held[...]).astype(BF)
+        for dy in range(2):
+            out_ref[0, 0, dy] = term[:, dy * kwide : (dy + 1) * kwide]
+
+    return call(
+        body,
+        (4,),
+        [pl.BlockSpec((1, 1, rows, units), lambda i, r: (i % 2, i // 2, 0, 0)), ANY],
+        pl.BlockSpec((1, 1, 2, rows, kwide), lambda i, r: (i % 2, i // 2, 0, 0, 0)),
+        jax.ShapeDtypeStruct((2, 2, 2, rows, kwide), BF),
+        scratch=[pltpu.VMEM((units, 2 * kwide), BF), pltpu.SemaphoreType.DMA((2 * parts,))],
+        cost=(16 * rows * kwide * units, 4 * kwide * units + 16 * rows * kwide),
+    )(ids, hidden, weights)
 
 
 def shards(
@@ -573,41 +603,42 @@
     order = [ctx_index, 3 - ctx_index, beyond, 3 - beyond]
     own_span = (ctx_index == 1).astype(jnp.int32) if line else 0
     active = middle.astype(jnp.int32) if line else 1
-    ids = jnp.stack([mp_index, rep_index, active, *order, ctx_index, own_span]).astype(jnp.int32)
+    sources = [ctx_index, ctx_index ^ 1, ctx_index ^ jnp.where(middle, 3, 2), ctx_index ^ jnp.where(middle, 2, 3)]
+    ids = jnp.stack([mp_index, rep_index, active, *order, ctx_index, own_span, *sources]).astype(jnp.int32)
 
     def gather(value):
         return Rows([lax.all_gather(value, "ctx", axis=0)])
 
+    packed_mixer = pack_mixer(ids, trainer_mixer_in, trainer_mixer_out)
+    plane_mixer, moved = across_plane(packed_mixer)
+    packed_up, packed_down = pack_feed(after(ids, plane_mixer), trainer_gate_up, trainer_down, feed)
+    plane_up, moved_up = across_plane(after(packed_up, *moved))
+    plane_down, _ = across_plane(after(packed_down, *moved_up))
+    flags = after(live_flags, packed_mixer)
     if line:
         sent = lax.dynamic_slice_in_dim(page_table, rep_index * 4 + mp_index, 1, 0)
-        chunk = normalise(sent, token_pages, mixer_gain)
-        ids_next = after(ids, chunk)
+        chunk = normalise(after(sent, packed_mixer), token_pages, mixer_gain)
         chunk = lax.ppermute(chunk, "ctx", [(0, 1), (3, 2)])
-    else:
-        ids_next = ids
-    packed_mixer = pack_mixer(ids_next, trainer_mixer_in, trainer_mixer_out)
-    plane_mixer, moved = across_plane(packed_mixer)
-    packed_feed = after(pack_feed(after(ids, packed_mixer), trainer_gate_up, trainer_down, feed), *moved)
-    plane_feed, _ = across_plane(packed_feed)
-    flags = after(live_flags, packed_mixer)
-    if line:
         spread = jnp.broadcast_to(flags[:, None], (pages, 128)).astype(jnp.int32)
         came = lax.ppermute(spread, "ctx", [(0, 1), (3, 2)])
         totals = jnp.broadcast_to(jnp.sum(spread + came, axis=0, keepdims=True), (8, 128))
-        base = lax.ppermute(totals, "ctx", [(1, 2)])[0, 0]
+        totals = lax.ppermute(totals, "ctx", [(1, 2)])
+        base = after(totals, plane_mixer)[0, 0]
         theirs = came[:, 0]
         live_here = jnp.concatenate(
             [jnp.where(ctx_index == 1, theirs, flags), jnp.where(ctx_index == 1, flags, theirs)]
         )
         page_start = (base + jnp.cumsum(live_here) - live_here) * page
 
+        plane_mixer = after(plane_mixer, came, totals)
         across = lax.ppermute(plane_mixer, "ctx", [(1, 2), (2, 1)])
         inward = lax.ppermute(plane_mixer, "ctx", [(0, 1), (3, 2)])
+        across, inward = lax.optimization_barrier((across, inward))
         onward = lax.ppermute(inward, "ctx", [(1, 2), (2, 1)])
         mixer_rows = [plane_mixer, across, inward, onward]
-        plane_feed = after(plane_feed, onward)
-        normed = normalise(after(page_table, *moved), token_pages, mixer_gain)
-        foreign = gather_plane(chunk, across, inward, normed)
+        plane_up = after(plane_up, onward)
+        normed = normalise(after(page_table, plane_mixer), token_pages, mixer_gain)
+        foreign = gather_plane(after(chunk, plane_mixer), across, inward, normed)
     else:
         normed = normalise(page_table, token_pages, mixer_gain)
         foreign = ()
@@ -615,10 +646,16 @@
         live_total = jnp.broadcast_to(jnp.sum(flags) * page, (8, 128)).astype(jnp.int32)
         page_start = total_before(live_total, ctx_count)[0, 0] + (jnp.cumsum(flags) - flags) * page
         mixer_rows = gather(plane_mixer).arrays
-    w_feed = gather(plane_feed)
+    w_up = gather(plane_up)
+    w_down = lax.all_gather(plane_down, "ctx", axis=0)
+    if kwide // 4 % 128 or ctx_count != 4:
+        parts = w_down.reshape(ctx_count, 4, -1, w_down.shape[-1])
+        parts = jnp.take(parts, mp_index ^ jnp.arange(4), axis=1)
+        w_down = jnp.transpose(parts, (2, 0, 1, 3)).reshape(-1, width)
 
     rows = live_here.shape[0] * page
     positions = (page_start[:, None] + jnp.arange(page, dtype=jnp.int32)[None, :]).reshape(rows)
+    lengths = after(lengths, plane_mixer)
     starts = jnp.cumsum(lengths) - lengths
     resets = (jnp.repeat(live_here, page) == 1) & jnp.any(positions[:, None] == starts[None, :], axis=1)
     count = jnp.cumsum(resets.astype(jnp.int32))
@@ -639,7 +676,10 @@
     qs, ks, v, fin, pack = project(
         ids, live_here, last, normed, foreign, w_in, decay_floor.reshape(1, cols), cnt_col
     )
-    earlier = [lax.ppermute(pack, "ctx", [(1, 2)])] if line else from_earlier(pack, ctx_count)
+    if line:
+        earlier = [lax.ppermute(pack, "ctx", [(1, 2)])]
+    else:
+        earlier = from_earlier(pack, ctx_count)
     terms = mix(ids, last, earlier, qs, ks, v, fin, w_out, cnt_col, cnt_row)
     if line:
         theirs, stage = sum_scatter(terms[2:])
@@ -650,8 +690,9 @@
         mixed = sum_scatter(terms)[0]
     residual = ordered.astype(F32) + mixed
     mine, other = gather_plane(residual.astype(BF))
-    down_terms = feed_forward(ids, mine, other, feed_gain.reshape(4, 1, kwide), w_feed, feed)
-    summed = residual + sum_scatter(down_terms)[0]
+    hidden = feed_up(ids, mine, other, feed_gain.reshape(4, 1, kwide), w_up, feed)
+    send = feed_down(ids, hidden, w_down, kwide, 1)
+    summed = residual + sum_scatter((feed_down(ids, hidden, w_down, kwide, 0), send))[0]
     live_half = jnp.repeat(
         lax.dynamic_slice_in_dim(live_flags, rep_index * (pages // 2), pages // 2, 0), page
     )

time: 316 us -> 307 us (0.972)
  waiting for transfers between devices: 174 us -> 137 us
  other arithmetic: 19.7 us -> 31.6 us
  starting transfers between devices: 46 us -> 55.7 us
  local copies, waits for them, and re-layouts: 16.1 us -> 20.3 us
    ppermute x1, waiting for transfers between devices: 75.9 us -> 32.4 us  [shards(): back = lax.ppermute(theirs.astype(BF), 'ctx', [(1, 0), (2, 3)])]
    ppermute x21 -> x24, waiting for transfers between devices: 72.5 us -> 61.4 us  [mp_perm(): return lax.ppermute(value, 'mp', [(i, i ^ s) for i in range(4)])]
    ppermute x1, waiting for transfers between devices: 0.01 us -> 9.22 us  [shards(): came = lax.ppermute(spread, 'ctx', [(0, 1), (3, 2)])]
    ppermute x10, waiting for transfers between devices: 21.7 us -> 29.8 us  [rep_perm(): return lax.ppermute(value, 'rep', [(0, 1), (1, 0)])]
    another operation x9, other arithmetic: 0.89 us -> 6.03 us
    ppermute x21 -> x24, starting transfers between devices: 14.9 us -> 19.5 us  [mp_perm(): return lax.ppermute(value, 'mp', [(i, i ^ s) for i in range(4)])]
    all_gather x0 -> x1, waiting for transfers between devices: none -> 4.53 us  [shards(): w_down = lax.all_gather(plane_down, 'ctx', axis=0)]
    ppermute x1, waiting for transfers between devices: 3.41 us -> 0.01 us  [shards(): inward = lax.ppermute(plane_mixer, 'ctx', [(0, 1), (3, 2)])]
  transfers between devices with their start and end apart: 40 -> 44, of which waited for: 21 -> 23; matrix products, arithmetic and copies ran while one was open for 8% -> 13% of each run, Pallas kernels for 8% -> 13%
where the time goes in v4:
time: 307 us; the launch traced here: 306 us
  waiting for transfers between devices  137 us (45%)
  starting transfers between devices  55.7 us (18%)
  Pallas kernels  46.7 us (15%)
  other arithmetic  31.6 us (10%)
  local copies, waits for them, and re-layouts  20.3 us (7%)
  between operations  14 us (5%)
    ppermute x24, waiting for transfers between devices, mp_perm(): return lax.ppermute(value, 'mp', [(i, i ^ s) for i in range(4)])  61.4 us
    ppermute x1, waiting for transfers between devices, shards(): back = lax.ppermute(theirs.astype(BF), 'ctx', [(1, 0), (2, 3)])  32.4 us
    ppermute x10, waiting for transfers between devices, rep_perm(): return lax.ppermute(value, 'rep', [(0, 1), (1, 0)])  29.8 us
    ppermute x24, starting transfers between devices, mp_perm(): return lax.ppermute(value, 'mp', [(i, i ^ s) for i in range(4)])  19.5 us
    ppermute x10, starting transfers between devices, rep_perm(): return lax.ppermute(value, 'rep', [(0, 1), (1, 0)])  12.9 us
    pallas_call x1, Pallas kernels, feed_up(): call(body, (4,), [spec, spec, whole(gain.shape)] + [ANY] * n, pl.BlockSpe...  12.1 us
    ppermute x1, starting transfers between devices, shards(): inward = lax.ppermute(plane_mixer, 'ctx', [(0, 1), (3, 2)])  9.88 us
    ppermute x1, waiting for transfers between devices, shards(): came = lax.ppermute(spread, 'ctx', [(0, 1), (3, 2)])  9.22 us
  transfers between devices with their start and end apart: 44, of which 23 were waited for; matrix products, arithmetic and copies ran while one was open for 13% of the time, Pallas kernels for 13%

profile of v4, /device:TPU:0, one launch (start us, length us, event | category | flops | bytes accessed | tf_op | source)
XLA Modules:
  0.0 305.7 jit_solution(18025433345322344550)
XLA Ops:
  14.1 5.0 %collective-permute-start.8 = (bf16[128,2048]{1,0:T(8,128)(2,1)S(1)}, bf16[128,2048]{1,0:T(8,128)(2,1)S(1)}, u32[]{:S(2)}, u32[]{:S(2)}) collective-permute-start(bf16[128,2048]{1,0:T(8,128)(2,1)S(1)} %shard_map.111), channel_id=1, source_target_pairs={{0,8},{24,16},{1,9},{25,17},{2,10},{26,18},{3,11},{27,19},{4,12},{... | collective-permute-start | bytes 1572872 | tf_op jit(solution)/shard_map/ppermute | solution.py:621
  22.4 9.2 %collective-permute-done.3 = s32[8,128]{0,1:T(8,128)S(1)} collective-permute-done((s32[8,128]{0,1:T(8,128)S(1)}, s32[8,128]{0,1:T(8,128)S(1)}, u32[]{:S(2)}, u32[]{:S(2)}) %collective-permute-start.3) | collective-permute-done | bytes 4128 | tf_op jit(solution)/shard_map/ppermute | solution.py:623
  37.9 9.9 %collective-permute-start.6 = (bf16[512,1024]{1,0:T(8,128)(2,1)}, bf16[512,1024]{1,0:T(8,128)(2,1)}, u32[]{:S(2)}, u32[]{:S(2)}) collective-permute-start(bf16[512,1024]{1,0:T(8,128)(2,1)} %pad_maximum_fusion.3.refs_5_.refs_6_), channel_id=1, source_target_pairs={{0,8},{24,16},{1,9},{25,17},{2,10},{26,18},{3,11},{27,19},{4,12},{... | collective-permute-start | bytes 3145736 | tf_op jit(solution)/shard_map/ppermute | solution.py:635
  50.6 6.4 %collective-permute-done.9 = bf16[64,2048]{1,0:T(8,128)(2,1)S(1)} collective-permute-done((bf16[64,2048]{1,0:T(8,128)(2,1)S(1)}, bf16[64,2048]{1,0:T(8,128)(2,1)S(1)}, u32[]{:S(2)}, u32[]{:S(2)}) %collective-permute-start.9) | collective-permute-done | bytes 262176 | tf_op jit(solution)/shard_map/ppermute | solution.py:187
  59.9 3.3 %shard_map.114 = (bf16[4,128,1408]{2,1,0:T(8,128)(2,1)S(1)}, bf16[4,704,128]{2,1,0:T(8,128)(2,1)S(1)}) custom-call(s32[13]{0:T(128)S(1)} %stack.147.ids_ref, f32[2,128,5632]{2,1,0:T(8,128)} %refs_3_.1, f32[2,128,5632]{2,1,0:T(8,128)} %refs_3_.1, f32[2,128,5632]{2,1,0:T(8,128)} %refs_3_.1, f32[2,128,5632]{2,1,0:T(8,128)} %refs_3_.1, ...), custom_call_target="tpu_custom_call" | custom-call | bytes 6488064 | tf_op jit(solution)/shard_map/pallas_call | solution.py:176
  64.1 6.0 %shard_map.110.refs_2_ = bf16[1024,2048]{1,0:T(8,128)(2,1)S(1)} custom-call(s32[8]{0:T(128)S(1)} %copy-done.10, bf16[8,128,2048]{2,1,0:T(8,128)(2,1)} %x_ref.3, f32[1,2048]{1,0:T(1,128)S(1)} %bitcast.218), custom_call_target="tpu_custom_call" | custom-call | flops 8388608 | bytes 8388608 | tf_op jit(solution)/shard_map/pallas_call | solution.py:228
  88.0 8.2 %collective-permute-done.32 = bf16[128,1408]{1,0:T(8,128)(2,1)} collective-permute-done((bf16[128,1408]{1,0:T(8,128)(2,1)S(1)}, bf16[128,1408]{1,0:T(8,128)(2,1)}, u32[]{:S(2)}, u32[]{:S(2)}) %collective-permute-start.32) | collective-permute-done | bytes 360480 | tf_op jit(solution)/shard_map/ppermute | solution.py:187
  101.0 8.2 %shard_map.112 = (bf16[2048,256]{1,0:T(8,128)(2,1)S(1)}, bf16[2048,256]{1,0:T(8,128)(2,1)S(1)}, bf16[2048,256]{1,0:T(8,128)(2,1)S(1)}, f32[16,1,256]{2,1,0:T(1,128)S(1)}, bf16[2,144,128]{2,1,0:T(8,128)(2,1)S(1)}) custom-call(s32[13]{0:T(128)S(1)} %stack.147.ids_ref, s32[16]{0:T(128)S(1)} %get-tuple-element.78.refs_0_, ...), custom_call_target="tpu_custom_call" | custom-call | flops 6442450944 | bytes 12582912 | tf_op jit(solution)/shard_map/pallas_call | solution.py:324
  110.0 6.2 %shard_map.113 = (bf16[2,2,2,256,512]{4,3,2,1,0:T(8,128)(2,1)}, bf16[2,2,2,256,512]{4,3,2,1,0:T(8,128)(2,1)}, bf16[2,2,2,256,512]{4,3,2,1,0:T(8,128)(2,1)}, bf16[2,2,2,256,512]{4,3,2,1,0:T(8,128)(2,1)}) custom-call(s32[13]{0:T(128)S(1)} %stack.147.ids_ref, s32[16]{0:T(128)S(1)} %slice_reduce_fusion.refs_1_.refs_0_, ...), custom_call_target="tpu_custom_call" | custom-call | flops 2147483648 | bytes 8388608 | tf_op jit(solution)/shard_map/pallas_call | solution.py:444
  116.3 4.4 %collective-permute-done.15 = bf16[2,2,2,256,512]{4,3,2,1,0:T(8,128)(2,1)S(1)} collective-permute-done((bf16[2,2,2,256,512]{4,3,2,1,0:T(8,128)(2,1)}, bf16[2,2,2,256,512]{4,3,2,1,0:T(8,128)(2,1)S(1)}, u32[]{:S(2)}, u32[]{:S(2)}) %collective-permute-start.15) | collective-permute-done | bytes 2097184 | tf_op jit(solution)/shard_map/ppermute | solution.py:187
  125.4 10.8 %collective-permute-done.16 = bf16[2,256,512]{2,1,0:T(8,128)(2,1)} collective-permute-done((bf16[2,256,512]{2,1,0:T(8,128)(2,1)S(1)}, bf16[2,256,512]{2,1,0:T(8,128)(2,1)}, u32[]{:S(2)}, u32[]{:S(2)}) %collective-permute-start.16) | collective-permute-done | bytes 524320 | tf_op jit(solution)/shard_map/ppermute | solution.py:191
  144.7 5.0 %collective-permute-done.24 = bf16[256,512]{1,0:T(8,128)(2,1)S(1)} collective-permute-done((bf16[256,512]{1,0:T(8,128)(2,1)S(1)}, bf16[256,512]{1,0:T(8,128)(2,1)S(1)}, u32[]{:S(2)}, u32[]{:S(2)}) %collective-permute-start.24) | collective-permute-done | bytes 262176 | tf_op jit(solution)/shard_map/ppermute | solution.py:191
  155.8 3.1 %collective-permute-done.23 = bf16[256,512]{1,0:T(8,128)(2,1)S(1)} collective-permute-done((bf16[256,512]{1,0:T(8,128)(2,1)S(1)}, bf16[256,512]{1,0:T(8,128)(2,1)S(1)}, u32[]{:S(2)}, u32[]{:S(2)}) %collective-permute-start.23) | collective-permute-done | bytes 262176 | tf_op jit(solution)/shard_map/ppermute | solution.py:187
  161.7 7.7 %collective-permute-done.21 = bf16[2,256,512]{2,1,0:T(8,128)(2,1)S(1)} collective-permute-done((bf16[2,256,512]{2,1,0:T(8,128)(2,1)S(1)}, bf16[2,256,512]{2,1,0:T(8,128)(2,1)S(1)}, u32[]{:S(2)}, u32[]{:S(2)}) %collective-permute-start.21) | collective-permute-done | bytes 524320 | tf_op jit(solution)/shard_map/ppermute | solution.py:187
  182.5 32.4 %collective-permute-done.25 = bf16[512,512]{1,0:T(8,128)(2,1)S(1)} collective-permute-done((bf16[512,512]{1,0:T(8,128)(2,1)}, bf16[512,512]{1,0:T(8,128)(2,1)S(1)}, u32[]{:S(2)}, u32[]{:S(2)}) %collective-permute-start.25) | collective-permute-done | bytes 524320 | tf_op jit(solution)/shard_map/ppermute | solution.py:686
  218.7 5.3 %collective-permute-done.28 = bf16[256,512]{1,0:T(8,128)(2,1)S(1)} collective-permute-done((bf16[256,512]{1,0:T(8,128)(2,1)S(1)}, bf16[256,512]{1,0:T(8,128)(2,1)S(1)}, u32[]{:S(2)}, u32[]{:S(2)}) %collective-permute-start.28) | collective-permute-done | bytes 262176 | tf_op jit(solution)/shard_map/ppermute | solution.py:191
  227.2 10.0 %collective-permute-done.29 = bf16[2,256,512]{2,1,0:T(8,128)(2,1)S(1)} collective-permute-done((bf16[2,256,512]{2,1,0:T(8,128)(2,1)S(1)}, bf16[2,256,512]{2,1,0:T(8,128)(2,1)S(1)}, u32[]{:S(2)}, u32[]{:S(2)}) %collective-permute-start.29) | collective-permute-done | bytes 524320 | tf_op jit(solution)/shard_map/ppermute | solution.py:187
  240.4 2.6 collective-permute-done.30
  247.9 12.1 %shard_map.115.h_ref = bf16[2,2,256,768]{3,2,1,0:T(8,128)(2,1)S(1)} custom-call(s32[13]{0:T(128)S(1)} %stack.147.ids_ref, bf16[2,2,2,256,512]{4,3,2,1,0:T(8,128)(2,1)S(1)} %copy-done.4, bf16[2,2,2,256,512]{4,3,2,1,0:T(8,128)(2,1)S(1)} %copy-done.5, f32[4,1,512]{2,1,0:T(1,128)S(1)} %bitcast.220, bf16[4,512,1408]{2,1,0:T(8,128)(2,1)} %bitcast.233), custom_call_target="tpu_custom_call" | custom-call | flops 5905580032 | bytes 14155776 | tf_op jit(solution)/shard_map/pallas_call | solution.py:527
  260.0 4.5 %all-gather.7.cloned.1.call-done = bf16[11264,128]{1,0:T(8,128)(2,1)} async-done(((bf16[2816,128]{1,0:T(8,128)(2,1)}), bf16[11264,128]{1,0:T(8,128)(2,1)}) %all-gather.7.cloned.1.call-update) | async-done | bytes 2883600 | tf_op jit(solution)/shard_map/all_gather | solution.py:650
  264.6 4.4 %shard_map.117 = bf16[2,2,2,256,512]{4,3,2,1,0:T(8,128)(2,1)S(1)} custom-call(s32[13]{0:T(128)S(1)} %stack.147.ids_ref, bf16[2,2,256,768]{3,2,1,0:T(8,128)(2,1)S(1)} %shard_map.115.h_ref, bf16[4,2816,128]{2,1,0:T(8,128)(2,1)} %bitcast.222), custom_call_target="tpu_custom_call" | custom-call | flops 1610612736 | bytes 3670016 | tf_op jit(solution)/shard_map/pallas_call | solution.py:568
  269.1 4.4 %shard_map.116 = bf16[2,2,2,256,512]{4,3,2,1,0:T(8,128)(2,1)S(1)} custom-call(s32[13]{0:T(128)S(1)} %stack.147.ids_ref, bf16[2,2,256,768]{3,2,1,0:T(8,128)(2,1)S(1)} %shard_map.115.h_ref, bf16[4,2816,128]{2,1,0:T(8,128)(2,1)} %bitcast.223), custom_call_target="tpu_custom_call" | custom-call | flops 1610612736 | bytes 3670016 | tf_op jit(solution)/shard_map/pallas_call | solution.py:568
  277.3 10.9 %collective-permute-done.40 = bf16[2,256,512]{2,1,0:T(8,128)(2,1)S(1)} collective-permute-done((bf16[2,256,512]{2,1,0:T(8,128)(2,1)S(1)}, bf16[2,256,512]{2,1,0:T(8,128)(2,1)S(1)}, u32[]{:S(2)}, u32[]{:S(2)}) %collective-permute-start.40) | collective-permute-done | bytes 524320 | tf_op jit(solution)/shard_map/ppermute | solution.py:187
  291.5 4.8 %collective-permute-done.41 = bf16[256,512]{1,0:T(8,128)(2,1)S(1)} collective-permute-done((bf16[256,512]{1,0:T(8,128)(2,1)S(1)}, bf16[256,512]{1,0:T(8,128)(2,1)S(1)}, u32[]{:S(2)}, u32[]{:S(2)}) %collective-permute-start.41) | collective-permute-done | bytes 262176 | tf_op jit(solution)/shard_map/ppermute | solution.py:191
  (212 shorter events, 107.0 us)
Async XLA Ops:
  6.5 238.2 %all-gather.5.cloned.1.call-start = ((), (), s32[]{:S(2)}) async-start(), calls=%async_computation | async-start | bytes 7208960 | tf_op jit(solution)/shard_map/all_gather | solution.py:610
  14.1 20.4 %collective-permute-start.8 = (bf16[128,2048]{1,0:T(8,128)(2,1)S(1)}, bf16[128,2048]{1,0:T(8,128)(2,1)S(1)}, u32[]{:S(2)}, u32[]{:S(2)}) collective-permute-start(bf16[128,2048]{1,0:T(8,128)(2,1)S(1)} %shard_map.111), channel_id=1, source_target_pairs={{0,8},{24,16},{1,9},{25,17},{2,10},{26,18},{3,11},{27,19},{4,12},{... | collective-permute-start | bytes 1572872 | tf_op jit(solution)/shard_map/ppermute | solution.py:621
  19.1 13.2 %collective-permute-start.2 = (bf16[128,1024]{1,0:T(8,128)(2,1)S(1)}, bf16[128,1024]{1,0:T(8,128)(2,1)S(1)}, u32[]{:S(2)}, u32[]{:S(2)}) collective-permute-start(bf16[128,1024]{1,0:T(8,128)(2,1)S(1)} %get-tuple-element.96), channel_id=1, source_target_pairs={{0,6},{2,4},{4,2},{6,0},{1,7},{3,5},{5,3},{7,1},{8,14},{10,12},{12... | collective-permute-start | bytes 786440 | tf_op jit(solution)/shard_map/ppermute | solution.py:187
  19.9 13.5 %collective-permute-start.1 = (bf16[128,1024]{1,0:T(8,128)(2,1)S(1)}, bf16[128,1024]{1,0:T(8,128)(2,1)S(1)}, u32[]{:S(2)}, u32[]{:S(2)}) collective-permute-start(bf16[128,1024]{1,0:T(8,128)(2,1)S(1)} %get-tuple-element.97), channel_id=1, source_target_pairs={{0,4},{2,6},{4,0},{6,2},{1,5},{3,7},{5,1},{7,3},{8,12},{10,14},{12... | collective-permute-start | bytes 786440 | tf_op jit(solution)/shard_map/ppermute | solution.py:187
  34.6 14.7 %collective-permute-start.11 = (bf16[64,2048]{1,0:T(8,128)(2,1)S(1)}, bf16[64,2048]{1,0:T(8,128)(2,1)S(1)}, u32[]{:S(2)}, u32[]{:S(2)}) collective-permute-start(bf16[64,2048]{1,0:T(8,128)(2,1)S(1)} %get-tuple-element.115), channel_id=1, source_target_pairs={{0,1},{1,0},{2,3},{3,2},{4,5},{5,4},{6,7},{7,6},{8,9},{9,8},{10,11... | collective-permute-start | bytes 786440 | tf_op jit(solution)/shard_map/ppermute | solution.py:191
  36.2 34.0 %collective-permute-start.5 = (bf16[512,1024]{1,0:T(8,128)(2,1)}, bf16[512,1024]{1,0:T(8,128)(2,1)}, u32[]{:S(2)}, u32[]{:S(2)}) collective-permute-start(bf16[512,1024]{1,0:T(8,128)(2,1)} %pad_maximum_fusion.3.refs_5_.refs_6_), channel_id=1, source_target_pairs={{8,16},{16,8},{9,17},{17,9},{10,18},{18,10},{11,19},{19,11},{12,20... | collective-permute-start | bytes 3145736 | tf_op jit(solution)/shard_map/ppermute | solution.py:634
  37.9 32.3 %collective-permute-start.6 = (bf16[512,1024]{1,0:T(8,128)(2,1)}, bf16[512,1024]{1,0:T(8,128)(2,1)}, u32[]{:S(2)}, u32[]{:S(2)}) collective-permute-start(bf16[512,1024]{1,0:T(8,128)(2,1)} %pad_maximum_fusion.3.refs_5_.refs_6_), channel_id=1, source_target_pairs={{0,8},{24,16},{1,9},{25,17},{2,10},{26,18},{3,11},{27,19},{4,12},{... | collective-permute-start | bytes 3145736 | tf_op jit(solution)/shard_map/ppermute | solution.py:635
  50.1 22.5 %collective-permute-start.12 = (bf16[2,64,2048]{2,1,0:T(8,128)(2,1)}, bf16[2,64,2048]{2,1,0:T(8,128)(2,1)}, u32[]{:S(2)}, u32[]{:S(2)}) collective-permute-start(bf16[2,64,2048]{2,1,0:T(8,128)(2,1)} %get-tuple-element.118), channel_id=1, source_target_pairs={{0,4},{2,6},{4,0},{6,2},{1,5},{3,7},{5,1},{7,3},{8,12},{10,14},{12... | collective-permute-start | bytes 1572872 | tf_op jit(solution)/shard_map/ppermute | solution.py:187
  58.1 15.7 %collective-permute-start.10 = (bf16[2,64,2048]{2,1,0:T(8,128)(2,1)}, bf16[2,64,2048]{2,1,0:T(8,128)(2,1)}, u32[]{:S(2)}, u32[]{:S(2)}) collective-permute-start(bf16[2,64,2048]{2,1,0:T(8,128)(2,1)} %get-tuple-element.112), channel_id=1, source_target_pairs={{0,1},{1,0},{2,3},{3,2},{4,5},{5,4},{6,7},{7,6},{8,9},{9,8},{10,11... | collective-permute-start | bytes 1572872 | tf_op jit(solution)/shard_map/ppermute | solution.py:191
  70.2 28.4 %collective-permute-start.7 = (bf16[512,1024]{1,0:T(8,128)(2,1)}, bf16[512,1024]{1,0:T(8,128)(2,1)}, u32[]{:S(2)}, u32[]{:S(2)}) collective-permute-start(bf16[512,1024]{1,0:T(8,128)(2,1)} %collective-permute-done.6.refs_7_.refs_8_), channel_id=1, source_target_pairs={{8,16},{16,8},{9,17},{17,9},{10,18},{18,10},{11,19},{19,11},{12,20... | collective-permute-start | bytes 3145736 | tf_op jit(solution)/shard_map/ppermute | solution.py:637
  75.2 25.8 %collective-permute-start.13 = (bf16[2,2,2,64,2048]{4,3,2,1,0:T(8,128)(2,1)S(1)}, bf16[2,2,2,64,2048]{4,3,2,1,0:T(8,128)(2,1)}, u32[]{:S(2)}, u32[]{:S(2)}) collective-permute-start(bf16[2,2,2,64,2048]{4,3,2,1,0:T(8,128)(2,1)S(1)} %pad_maximum_fusion.refs_3_), channel_id=1, source_target_pairs={{0,2},{2,0},{4,6},{6,4},{1,3},{3,1},{5,7},{7,5},{8,10},{10,8},{12,... | collective-permute-start | bytes 6291464 | tf_op jit(solution)/shard_map/ppermute | solution.py:187
  78.9 17.3 %collective-permute-start.32 = (bf16[128,1408]{1,0:T(8,128)(2,1)S(1)}, bf16[128,1408]{1,0:T(8,128)(2,1)}, u32[]{:S(2)}, u32[]{:S(2)}) collective-permute-start(bf16[128,1408]{1,0:T(8,128)(2,1)S(1)} %get-tuple-element.93), channel_id=1, source_target_pairs={{0,4},{2,6},{4,0},{6,2},{1,5},{3,7},{5,1},{7,3},{8,12},{10,14},{12... | collective-permute-start | bytes 1081352 | tf_op jit(solution)/shard_map/ppermute | solution.py:187
  79.4 16.8 %collective-permute-start.31 = (bf16[128,1408]{1,0:T(8,128)(2,1)S(1)}, bf16[128,1408]{1,0:T(8,128)(2,1)}, u32[]{:S(2)}, u32[]{:S(2)}) collective-permute-start(bf16[128,1408]{1,0:T(8,128)(2,1)S(1)} %get-tuple-element.94), channel_id=1, source_target_pairs={{0,2},{2,0},{4,6},{6,4},{1,3},{3,1},{5,7},{7,5},{8,10},{10,8},{12,... | collective-permute-start | bytes 1081352 | tf_op jit(solution)/shard_map/ppermute | solution.py:187
  98.6 166.0 %all-gather.7.cloned.1.call-start = ((), (), s32[]{:S(2)}) async-start(), calls=%async_computation.1 | async-start | bytes 3604480 | tf_op jit(solution)/shard_map/all_gather | solution.py:650
  122.1 14.1 %collective-permute-start.16 = (bf16[2,256,512]{2,1,0:T(8,128)(2,1)S(1)}, bf16[2,256,512]{2,1,0:T(8,128)(2,1)}, u32[]{:S(2)}, u32[]{:S(2)}) collective-permute-start(bf16[2,256,512]{2,1,0:T(8,128)(2,1)S(1)} %get-tuple-element.88), channel_id=1, source_target_pairs={{0,1},{1,0},{2,3},{3,2},{4,5},{5,4},{6,7},{7,6},{8,9},{9,8},{10,11... | collective-permute-start | bytes 1572872 | tf_op jit(solution)/shard_map/ppermute | solution.py:191
  123.8 13.9 %collective-permute-start.17 = (bf16[2,256,512]{2,1,0:T(8,128)(2,1)S(1)}, bf16[2,256,512]{2,1,0:T(8,128)(2,1)}, u32[]{:S(2)}, u32[]{:S(2)}) collective-permute-start(bf16[2,256,512]{2,1,0:T(8,128)(2,1)S(1)} %get-tuple-element.90), channel_id=1, source_target_pairs={{0,4},{2,6},{4,0},{6,2},{1,5},{3,7},{5,1},{7,3},{8,12},{10,14},{12... | collective-permute-start | bytes 1572872 | tf_op jit(solution)/shard_map/ppermute | solution.py:187
  137.6 14.7 %collective-permute-start.18 = (bf16[2,2,2,256,512]{4,3,2,1,0:T(8,128)(2,1)}, bf16[2,2,2,256,512]{4,3,2,1,0:T(8,128)(2,1)}, u32[]{:S(2)}, u32[]{:S(2)}) collective-permute-start(bf16[2,2,2,256,512]{4,3,2,1,0:T(8,128)(2,1)} %get-tuple-element.68), channel_id=1, source_target_pairs={{0,2},{2,0},{4,6},{6,4},{1,3},{3,1},{5,7},{7,5},{8,10},{10,8},{12,... | collective-permute-start | bytes 6291464 | tf_op jit(solution)/shard_map/ppermute | solution.py:187
  141.7 32.3 %collective-permute-start.36 = (bf16[704,128]{1,0:T(8,128)(2,1)S(1)}, bf16[704,128]{1,0:T(8,128)(2,1)S(1)}, u32[]{:S(2)}, u32[]{:S(2)}) collective-permute-start(bf16[704,128]{1,0:T(8,128)(2,1)S(1)} %get-tuple-element.100), channel_id=1, source_target_pairs={{0,6},{2,4},{4,2},{6,0},{1,7},{3,5},{5,3},{7,1},{8,14},{10,12},{12... | collective-permute-start | bytes 540680 | tf_op jit(solution)/shard_map/ppermute | solution.py:187
  143.1 32.5 %collective-permute-start.35 = (bf16[704,128]{1,0:T(8,128)(2,1)S(1)}, bf16[704,128]{1,0:T(8,128)(2,1)S(1)}, u32[]{:S(2)}, u32[]{:S(2)}) collective-permute-start(bf16[704,128]{1,0:T(8,128)(2,1)S(1)} %get-tuple-element.101), channel_id=1, source_target_pairs={{0,4},{2,6},{4,0},{6,2},{1,5},{3,7},{5,1},{7,3},{8,12},{10,14},{12... | collective-permute-start | bytes 540680 | tf_op jit(solution)/shard_map/ppermute | solution.py:187
  143.7 31.9 %collective-permute-start.34 = (bf16[704,128]{1,0:T(8,128)(2,1)S(1)}, bf16[704,128]{1,0:T(8,128)(2,1)S(1)}, u32[]{:S(2)}, u32[]{:S(2)}) collective-permute-start(bf16[704,128]{1,0:T(8,128)(2,1)S(1)} %get-tuple-element.102), channel_id=1, source_target_pairs={{0,2},{2,0},{4,6},{6,4},{1,3},{3,1},{5,7},{7,5},{8,10},{10,8},{12,... | collective-permute-start | bytes 540680 | tf_op jit(solution)/shard_map/ppermute | solution.py:187
  153.8 15.6 %collective-permute-start.21 = (bf16[2,256,512]{2,1,0:T(8,128)(2,1)S(1)}, bf16[2,256,512]{2,1,0:T(8,128)(2,1)S(1)}, u32[]{:S(2)}, u32[]{:S(2)}) collective-permute-start(bf16[2,256,512]{2,1,0:T(8,128)(2,1)S(1)} %get-tuple-element.86), channel_id=1, source_target_pairs={{0,4},{2,6},{4,0},{6,2},{1,5},{3,7},{5,1},{7,3},{8,12},{10,14},{12... | collective-permute-start | bytes 1572872 | tf_op jit(solution)/shard_map/ppermute | solution.py:187
  169.4 45.6 %collective-permute-start.25 = (bf16[512,512]{1,0:T(8,128)(2,1)}, bf16[512,512]{1,0:T(8,128)(2,1)S(1)}, u32[]{:S(2)}, u32[]{:S(2)}) collective-permute-start(bf16[512,512]{1,0:T(8,128)(2,1)} %pad_maximum_fusion.7), channel_id=1, source_target_pairs={{8,0},{16,24},{9,1},{17,25},{10,2},{18,26},{11,3},{19,27},{12,4},{... | collective-permute-start | bytes 1572872 | tf_op jit(solution)/shard_map/ppermute | solution.py:686
  273.8 14.4 %collective-permute-start.40 = (bf16[2,256,512]{2,1,0:T(8,128)(2,1)S(1)}, bf16[2,256,512]{2,1,0:T(8,128)(2,1)S(1)}, u32[]{:S(2)}, u32[]{:S(2)}) collective-permute-start(bf16[2,256,512]{2,1,0:T(8,128)(2,1)S(1)} %get-tuple-element.82), channel_id=1, source_target_pairs={{0,4},{2,6},{4,0},{6,2},{1,5},{3,7},{5,1},{7,3},{8,12},{10,14},{12... | collective-permute-start | bytes 1572872 | tf_op jit(solution)/shard_map/ppermute | solution.py:187
  275.7 14.1 %collective-permute-start.38 = (bf16[2,256,512]{2,1,0:T(8,128)(2,1)S(1)}, bf16[2,256,512]{2,1,0:T(8,128)(2,1)S(1)}, u32[]{:S(2)}, u32[]{:S(2)}) collective-permute-start(bf16[2,256,512]{2,1,0:T(8,128)(2,1)S(1)} %get-tuple-element.80), channel_id=1, source_target_pairs={{0,1},{1,0},{2,3},{3,2},{4,5},{5,4},{6,7},{7,6},{8,9},{9,8},{10,11... | collective-permute-start | bytes 1572872 | tf_op jit(solution)/shard_map/ppermute | solution.py:191
  (51 other events, 394.4 us)
Sparse Core Ops, SparseCore 0:
  98.7 105.3 all-gather.4
  205.7 58.8 all-gather.6

commit v5 on v4

--- a/solution.py
+++ b/solution.py
@@ -12,6 +12,7 @@
 BF = jnp.bfloat16
 F32 = jnp.float32
 VMEM_LIMIT = 48 * 1024 * 1024
+FEED_LIMIT = 62 * 1024 * 1024
 
 
 def nt(a, b):
@@ -30,7 +31,7 @@
     return 1.0 / (1.0 + jnp.exp(-v))
 
 
-def call(body, grid, in_specs, out_specs, out_shape, scratch=(), prefetch=1, cost=None):
+def call(body, grid, in_specs, out_specs, out_shape, scratch=(), prefetch=1, cost=None, limit=VMEM_LIMIT):
     return pl.pallas_call(
         body,
         out_shape=out_shape,
@@ -42,7 +43,7 @@
             scratch_shapes=list(scratch),
         ),
         compiler_params=pltpu.CompilerParams(
-            dimension_semantics=("arbitrary",) * len(grid), vmem_limit_bytes=VMEM_LIMIT
+            dimension_semantics=("arbitrary",) * len(grid), vmem_limit_bytes=limit
         ),
         cost_estimate=None
         if cost is None
@@ -233,6 +234,18 @@
         jax.ShapeDtypeStruct((pages * page, width), BF),
         cost=(pages * page * width * 4, pages * page * width * 4),
     )(table, token_pages, gain.reshape(1, width))
+
+
+def reset_counts(live_here, page_start, lengths, page):
+    rows = live_here.shape[0] * page
+    positions = (page_start[:, None] + jnp.arange(page, dtype=jnp.int32)[None, :]).reshape(rows)
+    starts = jnp.cumsum(lengths) - lengths
+    resets = (jnp.repeat(live_here, page) == 1) & jnp.any(positions[:, None] == starts[None, :], axis=1)
+    count = jnp.cumsum(resets.astype(jnp.int32))
+    cnt_col = count.reshape(rows, 1)
+    cnt_row = count.reshape(-1, 1, page)
+    last = count.reshape(-1, page)[:, -1]
+    return cnt_col, cnt_row, last
 
 
 def step_state(state, ks, v, same_last, keep, final):
@@ -481,58 +494,76 @@
     return jnp.concatenate([a, b], axis=0), (a_came, b_came)
 
 
-def gather_plane(value, *others):
+def gather_core(value):
     half = value.shape[0] // 2
     a, b = value[:half], value[half:]
     a_y, b_x = mp_perm(a, 2), rep_perm(b)
     a_pair, b_pair = jnp.stack([a, a_y]), jnp.stack([b, b_x])
     a_x, b_y = rep_perm(a_pair), mp_perm(b_pair, 2)
-    mine = jnp.stack([jnp.stack([a_pair, a_x]), jnp.stack([b_pair, b_y], axis=1)])
-    mine = after(mine, *others)
-    return mine, mp_perm(mine, 1)
+    return jnp.stack([jnp.stack([a_pair, a_x]), jnp.stack([b_pair, b_y], axis=1)])
+
+
+def gather_pieces(value):
+    half = value.shape[0] // 2
+    a, b = value[:half], value[half:]
+    a_y, b_x = mp_perm(a, 2), rep_perm(b)
+    a_pair, b_pair = jnp.stack([a, a_y]), jnp.stack([b, b_x])
+    a_x, b_y = rep_perm(a_pair), mp_perm(b_pair, 2)
+    mine = [a_pair, a_x, b_pair, b_y]
+    return [*mine, *(mp_perm(piece, 1) for piece in mine)]
 
 
 def block_of(k, rows):
     return pl.ds(pl.multiple_of(k * rows, rows), rows)
 
 
-def feed_up(ids, mine, other, gain, weights, feed):
+def feed_up(ids, pieces, gain, weights, feed):
     near, up, units = feed.near, feed.near_up, feed.units
-    rows, kwide = mine.shape[-2:]
+    rows, kwide = pieces[0].shape[-2:]
     width = 4 * kwide
     n = len(weights.arrays)
     places = [(dy, dc) for dy in range(2) for dc in range(2)]
 
-    def body(ids_ref, m_ref, o_ref, g_ref, *rest):
-        w_refs, (out_ref, x_ref, held, sems) = rest[:n], rest[n:]
-        first = pl.program_id(0) == 0
-        pl.when(first)(lambda: weights.start(ids_ref, w_refs, held, sems))
-        blocks = [(m_ref, o_ref)[dc][0, 0, dy].astype(F32) for dy, dc in places]
-        square = sum(jnp.sum(b * b, axis=-1, keepdims=True) for b in blocks)
-        scale = lax.rsqrt(square / width + EPS)
-        for (dy, dc), b in zip(places, blocks):
-            k = ids_ref[0] ^ (2 * dy + dc)
-            x_ref[:, block_of(k, kwide)] = (b * scale * g_ref[k]).astype(BF)
-        pl.when(first)(lambda: weights.wait(ids_ref, w_refs, held, sems))
-
-        x = x_ref[...]
-        h = nn(x, held[...])
-        gate, edge, upward = h[:, 0:near], h[:, near : near + 128], h[:, near + 128 : up]
-        out_ref[0, 0, :, 0:near] = (gate * sigmoid(gate) * upward).astype(BF)
-        mixed = edge * sigmoid(edge) * pltpu.roll(edge, 64, 1)
-        lane = lax.broadcasted_iota(jnp.int32, mixed.shape, 1)
-        out_ref[0, 0, :, near:units] = jnp.where(lane < 64, mixed, 0.0).astype(BF)
-
-    spec = pl.BlockSpec((1, 1, 2, rows, kwide), lambda i, r: (i % 2, i // 2, 0, 0, 0))
+    def body(ids_ref, *rest):
+        p_refs, g_ref, w_refs = rest[:8], rest[8], rest[9 : 9 + n]
+        out_ref, x_ref, held, sems = rest[9 + n :]
+        dx = pl.program_id(0)
+        pl.when(dx == 0)(lambda: weights.start(ids_ref, w_refs, held, sems))
+        for ab in range(2):
+            blocks = []
+            for dy, dc in places:
+                first, second, third, fourth = p_refs[4 * dc : 4 * dc + 4]
+                if ab == 0:
+                    blocks.append(jnp.where(dx == 0, first[dy], second[dy]).astype(F32))
+                else:
+                    blocks.append((third, fourth)[dy][0].astype(F32))
+            square = sum(jnp.sum(b * b, axis=-1, keepdims=True) for b in blocks)
+            scale = lax.rsqrt(square / width + EPS)
+            for (dy, dc), b in zip(places, blocks):
+                k = ids_ref[0] ^ (2 * dy + dc)
+                x_ref[ab, :, block_of(k, kwide)] = (b * scale * g_ref[k]).astype(BF)
+        pl.when(dx == 0)(lambda: weights.wait(ids_ref, w_refs, held, sems))
+
+        for ab in range(2):
+            h = nn(x_ref[ab], held[...])
+            gate, edge, upward = h[:, 0:near], h[:, near : near + 128], h[:, near + 128 : up]
+            out_ref[ab, 0, :, 0:near] = (gate * sigmoid(gate) * upward).astype(BF)
+            mixed = edge * sigmoid(edge) * pltpu.roll(edge, 64, 1)
+            lane = lax.broadcasted_iota(jnp.int32, mixed.shape, 1)
+            out_ref[ab, 0, :, near:units] = jnp.where(lane < 64, mixed, 0.0).astype(BF)
+
+    pair = whole((2, rows, kwide))
+    one = pl.BlockSpec((1, rows, kwide), lambda i, r: (i, 0, 0))
     return call(
         body,
-        (4,),
-        [spec, spec, whole(gain.shape)] + [ANY] * n,
-        pl.BlockSpec((1, 1, rows, units), lambda i, r: (i % 2, i // 2, 0, 0)),
+        (2,),
+        [pair, pair, one, one] * 2 + [whole(gain.shape)] + [ANY] * n,
+        pl.BlockSpec((2, 1, rows, units), lambda i, r: (0, i, 0, 0)),
         jax.ShapeDtypeStruct((2, 2, rows, units), BF),
-        scratch=[pltpu.VMEM((rows, width), BF), *weights.scratch],
+        scratch=[pltpu.VMEM((2, rows, width), BF), *weights.scratch],
         cost=(8 * rows * width * up, width * up * 2 + 16 * rows * width),
-    )(ids, mine, other, gain, *weights.arrays)
+        limit=FEED_LIMIT,
+    )(ids, *pieces, gain, *weights.arrays)
 
 
 def feed_down(ids, hidden, weights, kwide, dc):
@@ -611,16 +642,18 @@
 
     packed_mixer = pack_mixer(ids, trainer_mixer_in, trainer_mixer_out)
     plane_mixer, moved = across_plane(packed_mixer)
-    packed_up, packed_down = pack_feed(after(ids, plane_mixer), trainer_gate_up, trainer_down, feed)
-    plane_up, moved_up = across_plane(after(packed_up, *moved))
-    plane_down, _ = across_plane(after(packed_down, *moved_up))
     flags = after(live_flags, packed_mixer)
     if line:
         sent = lax.dynamic_slice_in_dim(page_table, rep_index * 4 + mp_index, 1, 0)
         chunk = normalise(after(sent, packed_mixer), token_pages, mixer_gain)
-        chunk = lax.ppermute(chunk, "ctx", [(0, 1), (3, 2)])
         spread = jnp.broadcast_to(flags[:, None], (pages, 128)).astype(jnp.int32)
         came = lax.ppermute(spread, "ctx", [(0, 1), (3, 2)])
+        chunk = after(chunk, came)
+        ids_feed = after(ids, chunk)
+        chunk = lax.ppermute(chunk, "ctx", [(0, 1), (3, 2)])
+        packed_up, packed_down = pack_feed(ids_feed, trainer_gate_up, trainer_down, feed)
+        plane_up, moved_up = across_plane(after(packed_up, *moved))
+        plane_down, _ = across_plane(after(packed_down, *moved_up))
         totals = jnp.broadcast_to(jnp.sum(spread + came, axis=0, keepdims=True), (8, 128))
         totals = lax.ppermute(totals, "ctx", [(1, 2)])
         base = after(totals, plane_mixer)[0, 0]
@@ -630,22 +663,31 @@
         )
         page_start = (base + jnp.cumsum(live_here) - live_here) * page
 
-        plane_mixer = after(plane_mixer, came, totals)
+        plane_mixer = after(plane_mixer, came, totals, packed_up, packed_down, chunk)
         across = lax.ppermute(plane_mixer, "ctx", [(1, 2), (2, 1)])
         inward = lax.ppermute(plane_mixer, "ctx", [(0, 1), (3, 2)])
-        across, inward = lax.optimization_barrier((across, inward))
+        normed = normalise(after(page_table, plane_mixer), token_pages, mixer_gain)
+        counts = reset_counts(live_here, page_start, after(lengths, plane_mixer), page)
+        mine = gather_core(chunk)
+        across, inward, normed, counts, mine = lax.optimization_barrier(
+            (across, inward, normed, counts, mine)
+        )
         onward = lax.ppermute(inward, "ctx", [(1, 2), (2, 1)])
         mixer_rows = [plane_mixer, across, inward, onward]
         plane_up = after(plane_up, onward)
-        normed = normalise(after(page_table, plane_mixer), token_pages, mixer_gain)
-        foreign = gather_plane(after(chunk, plane_mixer), across, inward, normed)
+        foreign = (mine, mp_perm(mine, 1))
     else:
+        packed_up, packed_down = pack_feed(ids, trainer_gate_up, trainer_down, feed)
+        plane_up, moved_up = across_plane(after(packed_up, *moved))
+        plane_down, _ = across_plane(after(packed_down, *moved_up))
         normed = normalise(page_table, token_pages, mixer_gain)
         foreign = ()
         live_here = flags
         live_total = jnp.broadcast_to(jnp.sum(flags) * page, (8, 128)).astype(jnp.int32)
         page_start = total_before(live_total, ctx_count)[0, 0] + (jnp.cumsum(flags) - flags) * page
+        counts = reset_counts(live_here, page_start, lengths, page)
         mixer_rows = gather(plane_mixer).arrays
+    cnt_col, cnt_row, last = counts
     w_up = gather(plane_up)
     w_down = lax.all_gather(plane_down, "ctx", axis=0)
     if kwide // 4 % 128 or ctx_count != 4:
@@ -653,19 +695,6 @@
         parts = jnp.take(parts, mp_index ^ jnp.arange(4), axis=1)
         w_down = jnp.transpose(parts, (2, 0, 1, 3)).reshape(-1, width)
 
-    rows = live_here.shape[0] * page
-    positions = (page_start[:, None] + jnp.arange(page, dtype=jnp.int32)[None, :]).reshape(rows)
-    lengths = after(lengths, plane_mixer)
-    starts = jnp.cumsum(lengths) - lengths
-    resets = (jnp.repeat(live_here, page) == 1) & jnp.any(positions[:, None] == starts[None, :], axis=1)
-    count = jnp.cumsum(resets.astype(jnp.int32))
-    cnt_col = count.reshape(rows, 1)
-    cnt_row = count.reshape(-1, 1, page)
-    last = count.reshape(-1, page)[:, -1]
-    if line:
-        *mixer_rows, normed, cnt_col, cnt_row, last = lax.optimization_barrier(
-            (*mixer_rows, normed, cnt_col, cnt_row, last)
-        )
     w_in, w_out = Rows(mixer_rows, 0, 3 * cols), Rows(mixer_rows, 3 * cols)
 
     half_rows = pages * page // 2
@@ -689,8 +718,8 @@
     else:
         mixed = sum_scatter(terms)[0]
     residual = ordered.astype(F32) + mixed
-    mine, other = gather_plane(residual.astype(BF))
-    hidden = feed_up(ids, mine, other, feed_gain.reshape(4, 1, kwide), w_up, feed)
+    pieces = gather_pieces(residual.astype(BF))
+    hidden = feed_up(ids, pieces, feed_gain.reshape(4, 1, kwide), w_up, feed)
     send = feed_down(ids, hidden, w_down, kwide, 1)
     summed = residual + sum_scatter((feed_down(ids, hidden, w_down, kwide, 0), send))[0]
     live_half = jnp.repeat(

time: 307 us -> 302 us (0.984)
  other arithmetic: 31.6 us -> 23.9 us
  waiting for transfers between devices: 137 us -> 144 us
    ppermute x1, waiting for transfers between devices: 9.22 us -> 0.01 us  [shards(): came = lax.ppermute(spread, 'ctx', [(0, 1), (3, 2)])]
    all_gather x1, waiting for transfers between devices: 4.53 us -> 12.6 us  [shards(): w_down = lax.all_gather(plane_down, 'ctx', axis=0)]
    another operation x19 -> x16, other arithmetic: 11 us -> 4.8 us
    ppermute x1, starting transfers between devices: 1.29 us -> 4.93 us  [shards(): came = lax.ppermute(spread, 'ctx', [(0, 1), (3, 2)])]
    ppermute x10, waiting for transfers between devices: 29.8 us -> 33.5 us  [rep_perm(): return lax.ppermute(value, 'rep', [(0, 1), (1, 0)])]
    ppermute x24 -> x27, waiting for transfers between devices: 61.4 us -> 64.6 us  [mp_perm(): return lax.ppermute(value, 'mp', [(i, i ^ s) for i in range(4)])]
    unnamed x62 -> x74, local copies, waits for them, and re-layouts: 8.62 us -> 9.7 us
    ppermute x24 -> x27, starting transfers between devices: 19.5 us -> 19.7 us  [mp_perm(): return lax.ppermute(value, 'mp', [(i, i ^ s) for i in range(4)])]
  transfers between devices with their start and end apart: 44 -> 47, of which waited for: 23 -> 28; matrix products, arithmetic and copies ran while one was open for 13% -> 10% of each run, Pallas kernels for 13% -> 14%
where the time goes in v5:
time: 302 us; the launch traced here: 301 us
  waiting for transfers between devices  144 us (48%)
  starting transfers between devices  53.5 us (18%)
  Pallas kernels  48.9 us (16%)
  other arithmetic  23.9 us (8%)
  local copies, waits for them, and re-layouts  17.4 us (6%)
  between operations  14 us (5%)
    ppermute x27, waiting for transfers between devices, mp_perm(): return lax.ppermute(value, 'mp', [(i, i ^ s) for i in range(4)])  64.6 us
    ppermute x10, waiting for transfers between devices, rep_perm(): return lax.ppermute(value, 'rep', [(0, 1), (1, 0)])  33.5 us
    ppermute x1, waiting for transfers between devices, shards(): back = lax.ppermute(theirs.astype(BF), 'ctx', [(1, 0), (2, 3)])  31.2 us
    ppermute x27, starting transfers between devices, mp_perm(): return lax.ppermute(value, 'mp', [(i, i ^ s) for i in range(4)])  19.7 us
    pallas_call x1, Pallas kernels, feed_up(): call(body, (2,), [pair, pair, one, one] * 2 + [whole(gain.shape)] + [ANY]...  14.4 us
    ppermute x10, starting transfers between devices, rep_perm(): return lax.ppermute(value, 'rep', [(0, 1), (1, 0)])  13 us
    all_gather x1, waiting for transfers between devices, shards(): w_down = lax.all_gather(plane_down, 'ctx', axis=0)  12.6 us
    unnamed x74, local copies, waits for them, and re-layouts  9.7 us
  transfers between devices with their start and end apart: 47, of which 28 were waited for; matrix products, arithmetic and copies ran while one was open for 10% of the time, Pallas kernels for 14%

profile of v5, /device:TPU:0, one launch (start us, length us, event | category | flops | bytes accessed | tf_op | source)
XLA Modules:
  0.0 301.1 jit_solution(10696938229888358742)
XLA Ops:
  11.1 4.9 %collective-permute-start.3 = (s32[8,128]{0,1:T(8,128)S(1)}, s32[8,128]{0,1:T(8,128)S(1)}, u32[]{:S(2)}, u32[]{:S(2)}) collective-permute-start(s32[8,128]{0,1:T(8,128)S(1)} %broadcast_in_dim.56), channel_id=1, source_target_pairs={{0,8},{24,16},{1,9},{25,17},{2,10},{26,18},{3,11},{27,19},{4,12},{... | collective-permute-start | bytes 12296 | tf_op jit(solution)/shard_map/ppermute | solution.py:650
  25.8 3.3 %shard_map.111 = (bf16[4,128,1408]{2,1,0:T(8,128)(2,1)S(1)}, bf16[4,704,128]{2,1,0:T(8,128)(2,1)S(1)}) custom-call(s32[13]{0:T(128)S(1)} %stack.120.ids_ref, f32[2,128,5632]{2,1,0:T(8,128)} %refs_3_.1, f32[2,128,5632]{2,1,0:T(8,128)} %refs_3_.1, f32[2,128,5632]{2,1,0:T(8,128)} %refs_3_.1, f32[2,128,5632]{2,1,0:T(8,128)} %refs_3_.1, ...), custom_call_target="tpu_custom_call" | custom-call | bytes 6488064 | tf_op jit(solution)/shard_map/pallas_call | solution.py:177
  36.5 8.3 %collective-permute-start.7 = (bf16[512,1024]{1,0:T(8,128)(2,1)S(1)}, bf16[512,1024]{1,0:T(8,128)(2,1)}, u32[]{:S(2)}, u32[]{:S(2)}) collective-permute-start(bf16[512,1024]{1,0:T(8,128)(2,1)S(1)} %pad_maximum_fusion.2.refs_5_.refs_6_), channel_id=1, source_target_pairs={{0,8},{24,16},{1,9},{25,17},{2,10},{26,18},{3,11},{27,19},{4,12},{... | collective-permute-start | bytes 3145736 | tf_op jit(solution)/shard_map/ppermute | solution.py:668
  49.9 4.3 %collective-permute-done.10 = bf16[64,2048]{1,0:T(8,128)(2,1)S(1)} collective-permute-done((bf16[64,2048]{1,0:T(8,128)(2,1)S(1)}, bf16[64,2048]{1,0:T(8,128)(2,1)S(1)}, u32[]{:S(2)}, u32[]{:S(2)}) %collective-permute-start.10) | collective-permute-done | bytes 262176 | tf_op jit(solution)/shard_map/ppermute | solution.py:192
  57.3 6.0 %shard_map.112.refs_2_ = bf16[1024,2048]{1,0:T(8,128)(2,1)S(1)} custom-call(s32[8]{0:T(128)S(1)} %copy-done.13, bf16[8,128,2048]{2,1,0:T(8,128)(2,1)} %x_ref.3, f32[1,2048]{1,0:T(1,128)S(1)} %bitcast.206), custom_call_target="tpu_custom_call" | custom-call | flops 8388608 | bytes 8388608 | tf_op jit(solution)/shard_map/pallas_call | solution.py:229
  63.4 3.5 %collective-permute-done.11 = bf16[2,64,2048]{2,1,0:T(8,128)(2,1)S(1)} collective-permute-done((bf16[2,64,2048]{2,1,0:T(8,128)(2,1)S(1)}, bf16[2,64,2048]{2,1,0:T(8,128)(2,1)S(1)}, u32[]{:S(2)}, u32[]{:S(2)}) %collective-permute-start.11) | collective-permute-done | bytes 524320 | tf_op jit(solution)/shard_map/ppermute | solution.py:188
  72.9 8.8 %collective-permute-done.36 = bf16[128,1408]{1,0:T(8,128)(2,1)S(1)} collective-permute-done((bf16[128,1408]{1,0:T(8,128)(2,1)S(1)}, bf16[128,1408]{1,0:T(8,128)(2,1)S(1)}, u32[]{:S(2)}, u32[]{:S(2)}) %collective-permute-start.36) | collective-permute-done | bytes 360480 | tf_op jit(solution)/shard_map/ppermute | solution.py:188
  81.7 6.7 %collective-permute-done.35 = bf16[128,1408]{1,0:T(8,128)(2,1)S(1)} collective-permute-done((bf16[128,1408]{1,0:T(8,128)(2,1)S(1)}, bf16[128,1408]{1,0:T(8,128)(2,1)S(1)}, u32[]{:S(2)}, u32[]{:S(2)}) %collective-permute-start.35) | collective-permute-done | bytes 360480 | tf_op jit(solution)/shard_map/ppermute | solution.py:188
  94.3 7.9 %shard_map.113 = (bf16[2048,256]{1,0:T(8,128)(2,1)S(1)}, bf16[2048,256]{1,0:T(8,128)(2,1)S(1)}, bf16[2048,256]{1,0:T(8,128)(2,1)S(1)}, f32[16,1,256]{2,1,0:T(1,128)S(1)}, bf16[2,144,128]{2,1,0:T(8,128)(2,1)S(1)}) custom-call(s32[13]{0:T(128)S(1)} %stack.120.ids_ref, s32[16]{0:T(128)S(1)} %get-tuple-element.70.refs_0_, ...), custom_call_target="tpu_custom_call" | custom-call | flops 6442450944 | bytes 12582912 | tf_op jit(solution)/shard_map/pallas_call | solution.py:337
  103.1 6.1 %shard_map.114 = (bf16[2,2,2,256,512]{4,3,2,1,0:T(8,128)(2,1)}, bf16[2,2,2,256,512]{4,3,2,1,0:T(8,128)(2,1)}, bf16[2,2,2,256,512]{4,3,2,1,0:T(8,128)(2,1)}, bf16[2,2,2,256,512]{4,3,2,1,0:T(8,128)(2,1)}) custom-call(s32[13]{0:T(128)S(1)} %stack.120.ids_ref, s32[16]{0:T(128)S(1)} %slice_reduce_fusion.refs_1_.refs_0_, ...), custom_call_target="tpu_custom_call" | custom-call | flops 2147483648 | bytes 8388608 | tf_op jit(solution)/shard_map/pallas_call | solution.py:457
  109.6 4.0 %collective-permute-done.15 = bf16[2,2,2,256,512]{4,3,2,1,0:T(8,128)(2,1)S(1)} collective-permute-done((bf16[2,2,2,256,512]{4,3,2,1,0:T(8,128)(2,1)}, bf16[2,2,2,256,512]{4,3,2,1,0:T(8,128)(2,1)S(1)}, u32[]{:S(2)}, u32[]{:S(2)}) %collective-permute-start.15) | collective-permute-done | bytes 2097184 | tf_op jit(solution)/shard_map/ppermute | solution.py:188
  118.4 11.1 %collective-permute-done.16 = bf16[2,256,512]{2,1,0:T(8,128)(2,1)} collective-permute-done((bf16[2,256,512]{2,1,0:T(8,128)(2,1)S(1)}, bf16[2,256,512]{2,1,0:T(8,128)(2,1)}, u32[]{:S(2)}, u32[]{:S(2)}) %collective-permute-start.16) | collective-permute-done | bytes 524320 | tf_op jit(solution)/shard_map/ppermute | solution.py:192
  139.7 4.3 %collective-permute-done.38 = bf16[704,128]{1,0:T(8,128)(2,1)S(1)} collective-permute-done((bf16[704,128]{1,0:T(8,128)(2,1)S(1)}, bf16[704,128]{1,0:T(8,128)(2,1)S(1)}, u32[]{:S(2)}, u32[]{:S(2)}) %collective-permute-start.38) | collective-permute-done | bytes 180256 | tf_op jit(solution)/shard_map/ppermute | solution.py:188
  158.7 6.6 %collective-permute-done.21 = bf16[2,256,512]{2,1,0:T(8,128)(2,1)S(1)} collective-permute-done((bf16[2,256,512]{2,1,0:T(8,128)(2,1)S(1)}, bf16[2,256,512]{2,1,0:T(8,128)(2,1)S(1)}, u32[]{:S(2)}, u32[]{:S(2)}) %collective-permute-start.21) | collective-permute-done | bytes 524320 | tf_op jit(solution)/shard_map/ppermute | solution.py:188
  168.7 3.9 %collective-permute-done.22 = bf16[256,512]{1,0:T(8,128)(2,1)S(1)} collective-permute-done((bf16[256,512]{1,0:T(8,128)(2,1)S(1)}, bf16[256,512]{1,0:T(8,128)(2,1)S(1)}, u32[]{:S(2)}, u32[]{:S(2)}) %collective-permute-start.22) | collective-permute-done | bytes 262176 | tf_op jit(solution)/shard_map/ppermute | solution.py:192
  175.5 31.2 %collective-permute-done.25 = bf16[512,512]{1,0:T(8,128)(2,1)S(1)} collective-permute-done((bf16[512,512]{1,0:T(8,128)(2,1)}, bf16[512,512]{1,0:T(8,128)(2,1)S(1)}, u32[]{:S(2)}, u32[]{:S(2)}) %collective-permute-start.25) | collective-permute-done | bytes 524320 | tf_op jit(solution)/shard_map/ppermute | solution.py:715
  210.4 4.6 %collective-permute-done.26 = bf16[256,512]{1,0:T(8,128)(2,1)S(1)} collective-permute-done((bf16[256,512]{1,0:T(8,128)(2,1)S(1)}, bf16[256,512]{1,0:T(8,128)(2,1)S(1)}, u32[]{:S(2)}, u32[]{:S(2)}) %collective-permute-start.26) | collective-permute-done | bytes 262176 | tf_op jit(solution)/shard_map/ppermute | solution.py:188
  219.2 8.8 %collective-permute-done.27.rest_1_ = bf16[2,256,512]{2,1,0:T(8,128)(2,1)S(1)} collective-permute-done((bf16[2,256,512]{2,1,0:T(8,128)(2,1)S(1)}, bf16[2,256,512]{2,1,0:T(8,128)(2,1)S(1)}, u32[]{:S(2)}, u32[]{:S(2)}) %collective-permute-start.27) | collective-permute-done | bytes 524320 | tf_op jit(solution)/shard_map/ppermute | solution.py:192
  231.6 14.4 %shard_map.115.h_ref = bf16[2,2,256,768]{3,2,1,0:T(8,128)(2,1)} custom-call(s32[13]{0:T(128)} %copy-done.11, bf16[2,256,512]{2,1,0:T(8,128)(2,1)} %copy-done.26, bf16[2,256,512]{2,1,0:T(8,128)(2,1)} %copy-done.32, bf16[2,256,512]{2,1,0:T(8,128)(2,1)} %copy-done.27, bf16[2,256,512]{2,1,0:T(8,128)(2,1)} %copy-done.33, bf16[2,256,512]{2,1,0:T(8,128)(2,1)} %copy-done.34, ...), custom_call_target="tpu_custom_call" | custom-call | flops 5905580032 | bytes 14155776 | tf_op jit(solution)/shard_map/pallas_call | solution.py:557
  246.0 12.6 %all-gather.7.cloned.1.call-done = bf16[11264,128]{1,0:T(8,128)(2,1)} async-done(((bf16[2816,128]{1,0:T(8,128)(2,1)}), bf16[11264,128]{1,0:T(8,128)(2,1)}) %all-gather.7.cloned.1.call-update) | async-done | bytes 2883600 | tf_op jit(solution)/shard_map/all_gather | solution.py:692
  260.0 4.4 %shard_map.117 = bf16[2,2,2,256,512]{4,3,2,1,0:T(8,128)(2,1)S(1)} custom-call(s32[13]{0:T(128)S(1)} %copy-done.12, bf16[2,2,256,768]{3,2,1,0:T(8,128)(2,1)S(1)} %copy-done.3, bf16[4,2816,128]{2,1,0:T(8,128)(2,1)} %bitcast.209), custom_call_target="tpu_custom_call" | custom-call | flops 1610612736 | bytes 3670016 | tf_op jit(solution)/shard_map/pallas_call | solution.py:599
  264.5 4.4 %shard_map.116 = bf16[2,2,2,256,512]{4,3,2,1,0:T(8,128)(2,1)S(1)} custom-call(s32[13]{0:T(128)S(1)} %copy-done.12, bf16[2,2,256,768]{3,2,1,0:T(8,128)(2,1)S(1)} %copy-done.3, bf16[4,2816,128]{2,1,0:T(8,128)(2,1)} %bitcast.210), custom_call_target="tpu_custom_call" | custom-call | flops 1610612736 | bytes 3670016 | tf_op jit(solution)/shard_map/pallas_call | solution.py:599
  272.7 10.9 %collective-permute-done.43 = bf16[2,256,512]{2,1,0:T(8,128)(2,1)S(1)} collective-permute-done((bf16[2,256,512]{2,1,0:T(8,128)(2,1)S(1)}, bf16[2,256,512]{2,1,0:T(8,128)(2,1)S(1)}, u32[]{:S(2)}, u32[]{:S(2)}) %collective-permute-start.43) | collective-permute-done | bytes 524320 | tf_op jit(solution)/shard_map/ppermute | solution.py:188
  286.9 4.8 %collective-permute-done.44 = bf16[256,512]{1,0:T(8,128)(2,1)S(1)} collective-permute-done((bf16[256,512]{1,0:T(8,128)(2,1)S(1)}, bf16[256,512]{1,0:T(8,128)(2,1)S(1)}, u32[]{:S(2)}, u32[]{:S(2)}) %collective-permute-start.44) | collective-permute-done | bytes 262176 | tf_op jit(solution)/shard_map/ppermute | solution.py:192
  (225 shorter events, 101.3 us)
Async XLA Ops:
  6.5 225.1 %all-gather.5.cloned.1.call-start = ((), (), s32[]{:S(2)}) async-start(), calls=%async_computation | async-start | bytes 7208960 | tf_op jit(solution)/shard_map/all_gather | solution.py:641
  11.1 11.6 %collective-permute-start.3 = (s32[8,128]{0,1:T(8,128)S(1)}, s32[8,128]{0,1:T(8,128)S(1)}, u32[]{:S(2)}, u32[]{:S(2)}) collective-permute-start(s32[8,128]{0,1:T(8,128)S(1)} %broadcast_in_dim.56), channel_id=1, source_target_pairs={{0,8},{24,16},{1,9},{25,17},{2,10},{26,18},{3,11},{27,19},{4,12},{... | collective-permute-start | bytes 12296 | tf_op jit(solution)/shard_map/ppermute | solution.py:650
  17.0 13.0 %collective-permute-start.2 = (bf16[128,1024]{1,0:T(8,128)(2,1)}, bf16[128,1024]{1,0:T(8,128)(2,1)}, u32[]{:S(2)}, u32[]{:S(2)}) collective-permute-start(bf16[128,1024]{1,0:T(8,128)(2,1)} %get-tuple-element.88), channel_id=1, source_target_pairs={{0,6},{2,4},{4,2},{6,0},{1,7},{3,5},{5,3},{7,1},{8,14},{10,12},{12... | collective-permute-start | bytes 786440 | tf_op jit(solution)/shard_map/ppermute | solution.py:188
  17.7 13.9 %collective-permute-start.1 = (bf16[128,1024]{1,0:T(8,128)(2,1)}, bf16[128,1024]{1,0:T(8,128)(2,1)}, u32[]{:S(2)}, u32[]{:S(2)}) collective-permute-start(bf16[128,1024]{1,0:T(8,128)(2,1)} %get-tuple-element.89), channel_id=1, source_target_pairs={{0,4},{2,6},{4,0},{6,2},{1,5},{3,7},{5,1},{7,3},{8,12},{10,14},{12... | collective-permute-start | bytes 786440 | tf_op jit(solution)/shard_map/ppermute | solution.py:188
  18.6 13.0 %collective-permute-start = (bf16[128,1024]{1,0:T(8,128)(2,1)}, bf16[128,1024]{1,0:T(8,128)(2,1)}, u32[]{:S(2)}, u32[]{:S(2)}) collective-permute-start(bf16[128,1024]{1,0:T(8,128)(2,1)} %get-tuple-element.90), channel_id=1, source_target_pairs={{0,2},{2,0},{4,6},{6,4},{1,3},{3,1},{5,7},{7,5},{8,10},{10,8},{12,... | collective-permute-start | bytes 786440 | tf_op jit(solution)/shard_map/ppermute | solution.py:188
  22.7 13.1 %collective-permute-start.5 = (bf16[128,2048]{1,0:T(8,128)(2,1)S(1)}, bf16[128,2048]{1,0:T(8,128)(2,1)}, u32[]{:S(2)}, u32[]{:S(2)}) collective-permute-start(bf16[128,2048]{1,0:T(8,128)(2,1)S(1)} %shard_map.110), channel_id=1, source_target_pairs={{0,8},{24,16},{1,9},{25,17},{2,10},{26,18},{3,11},{27,19},{4,12},{... | collective-permute-start | bytes 1572872 | tf_op jit(solution)/shard_map/ppermute | solution.py:653
  35.8 33.4 %collective-permute-start.6 = (bf16[512,1024]{1,0:T(8,128)(2,1)S(1)}, bf16[512,1024]{1,0:T(8,128)(2,1)S(1)}, u32[]{:S(2)}, u32[]{:S(2)}) collective-permute-start(bf16[512,1024]{1,0:T(8,128)(2,1)S(1)} %pad_maximum_fusion.2.refs_5_.refs_6_), channel_id=1, source_target_pairs={{8,16},{16,8},{9,17},{17,9},{10,18},{18,10},{11,19},{19,11},{12,20... | collective-permute-start | bytes 3145736 | tf_op jit(solution)/shard_map/ppermute | solution.py:667
  36.5 32.7 %collective-permute-start.7 = (bf16[512,1024]{1,0:T(8,128)(2,1)S(1)}, bf16[512,1024]{1,0:T(8,128)(2,1)}, u32[]{:S(2)}, u32[]{:S(2)}) collective-permute-start(bf16[512,1024]{1,0:T(8,128)(2,1)S(1)} %pad_maximum_fusion.2.refs_5_.refs_6_), channel_id=1, source_target_pairs={{0,8},{24,16},{1,9},{25,17},{2,10},{26,18},{3,11},{27,19},{4,12},{... | collective-permute-start | bytes 3145736 | tf_op jit(solution)/shard_map/ppermute | solution.py:668
  54.3 12.5 %collective-permute-start.11 = (bf16[2,64,2048]{2,1,0:T(8,128)(2,1)S(1)}, bf16[2,64,2048]{2,1,0:T(8,128)(2,1)S(1)}, u32[]{:S(2)}, u32[]{:S(2)}) collective-permute-start(bf16[2,64,2048]{2,1,0:T(8,128)(2,1)S(1)} %get-tuple-element.106), channel_id=1, source_target_pairs={{0,4},{2,6},{4,0},{6,2},{1,5},{3,7},{5,1},{7,3},{8,12},{10,14},{12... | collective-permute-start | bytes 1572872 | tf_op jit(solution)/shard_map/ppermute | solution.py:188
  56.1 11.5 %collective-permute-start.9 = (bf16[2,64,2048]{2,1,0:T(8,128)(2,1)S(1)}, bf16[2,64,2048]{2,1,0:T(8,128)(2,1)S(1)}, u32[]{:S(2)}, u32[]{:S(2)}) collective-permute-start(bf16[2,64,2048]{2,1,0:T(8,128)(2,1)S(1)} %get-tuple-element.100), channel_id=1, source_target_pairs={{0,1},{1,0},{2,3},{3,2},{4,5},{5,4},{6,7},{7,6},{8,9},{9,8},{10,11... | collective-permute-start | bytes 1572872 | tf_op jit(solution)/shard_map/ppermute | solution.py:192
  69.2 20.4 %collective-permute-start.13 = (bf16[512,1024]{1,0:T(8,128)(2,1)}, bf16[512,1024]{1,0:T(8,128)(2,1)}, u32[]{:S(2)}, u32[]{:S(2)}) collective-permute-start(bf16[512,1024]{1,0:T(8,128)(2,1)} %collective-permute-done.7.refs_7_.refs_8_), channel_id=1, source_target_pairs={{8,16},{16,8},{9,17},{17,9},{10,18},{18,10},{11,19},{19,11},{12,20... | collective-permute-start | bytes 3145736 | tf_op jit(solution)/shard_map/ppermute | solution.py:675
  71.1 17.3 %collective-permute-start.35 = (bf16[128,1408]{1,0:T(8,128)(2,1)S(1)}, bf16[128,1408]{1,0:T(8,128)(2,1)S(1)}, u32[]{:S(2)}, u32[]{:S(2)}) collective-permute-start(bf16[128,1408]{1,0:T(8,128)(2,1)S(1)} %get-tuple-element.85), channel_id=1, source_target_pairs={{0,4},{2,6},{4,0},{6,2},{1,5},{3,7},{5,1},{7,3},{8,12},{10,14},{12... | collective-permute-start | bytes 1081352 | tf_op jit(solution)/shard_map/ppermute | solution.py:188
  72.0 16.4 %collective-permute-start.34 = (bf16[128,1408]{1,0:T(8,128)(2,1)S(1)}, bf16[128,1408]{1,0:T(8,128)(2,1)S(1)}, u32[]{:S(2)}, u32[]{:S(2)}) collective-permute-start(bf16[128,1408]{1,0:T(8,128)(2,1)S(1)} %get-tuple-element.86), channel_id=1, source_target_pairs={{0,2},{2,0},{4,6},{6,4},{1,3},{3,1},{5,7},{7,5},{8,10},{10,8},{12,... | collective-permute-start | bytes 1081352 | tf_op jit(solution)/shard_map/ppermute | solution.py:188
  89.6 169.0 %all-gather.7.cloned.1.call-start = ((), (), s32[]{:S(2)}) async-start(), calls=%async_computation.1 | async-start | bytes 3604480 | tf_op jit(solution)/shard_map/all_gather | solution.py:692
  115.2 14.3 %collective-permute-start.16 = (bf16[2,256,512]{2,1,0:T(8,128)(2,1)S(1)}, bf16[2,256,512]{2,1,0:T(8,128)(2,1)}, u32[]{:S(2)}, u32[]{:S(2)}) collective-permute-start(bf16[2,256,512]{2,1,0:T(8,128)(2,1)S(1)} %get-tuple-element.80), channel_id=1, source_target_pairs={{0,1},{1,0},{2,3},{3,2},{4,5},{5,4},{6,7},{7,6},{8,9},{9,8},{10,11... | collective-permute-start | bytes 1572872 | tf_op jit(solution)/shard_map/ppermute | solution.py:192
  117.9 13.7 %collective-permute-start.17 = (bf16[2,256,512]{2,1,0:T(8,128)(2,1)S(1)}, bf16[2,256,512]{2,1,0:T(8,128)(2,1)S(1)}, u32[]{:S(2)}, u32[]{:S(2)}) collective-permute-start(bf16[2,256,512]{2,1,0:T(8,128)(2,1)S(1)} %get-tuple-element.82), channel_id=1, source_target_pairs={{0,4},{2,6},{4,0},{6,2},{1,5},{3,7},{5,1},{7,3},{8,12},{10,14},{12... | collective-permute-start | bytes 1572872 | tf_op jit(solution)/shard_map/ppermute | solution.py:188
  131.6 16.4 %collective-permute-start.18 = (bf16[2,2,2,256,512]{4,3,2,1,0:T(8,128)(2,1)}, bf16[2,2,2,256,512]{4,3,2,1,0:T(8,128)(2,1)}, u32[]{:S(2)}, u32[]{:S(2)}) collective-permute-start(bf16[2,2,2,256,512]{4,3,2,1,0:T(8,128)(2,1)} %get-tuple-element.63), channel_id=1, source_target_pairs={{0,2},{2,0},{4,6},{6,4},{1,3},{3,1},{5,7},{7,5},{8,10},{10,8},{12,... | collective-permute-start | bytes 6291464 | tf_op jit(solution)/shard_map/ppermute | solution.py:188
  149.7 15.5 %collective-permute-start.21 = (bf16[2,256,512]{2,1,0:T(8,128)(2,1)S(1)}, bf16[2,256,512]{2,1,0:T(8,128)(2,1)S(1)}, u32[]{:S(2)}, u32[]{:S(2)}) collective-permute-start(bf16[2,256,512]{2,1,0:T(8,128)(2,1)S(1)} %get-tuple-element.78), channel_id=1, source_target_pairs={{0,4},{2,6},{4,0},{6,2},{1,5},{3,7},{5,1},{7,3},{8,12},{10,14},{12... | collective-permute-start | bytes 1572872 | tf_op jit(solution)/shard_map/ppermute | solution.py:188
  152.6 13.6 %collective-permute-start.19 = (bf16[2,256,512]{2,1,0:T(8,128)(2,1)S(1)}, bf16[2,256,512]{2,1,0:T(8,128)(2,1)S(1)}, u32[]{:S(2)}, u32[]{:S(2)}) collective-permute-start(bf16[2,256,512]{2,1,0:T(8,128)(2,1)S(1)} %get-tuple-element.76), channel_id=1, source_target_pairs={{0,1},{1,0},{2,3},{3,2},{4,5},{5,4},{6,7},{7,6},{8,9},{9,8},{10,11... | collective-permute-start | bytes 1572872 | tf_op jit(solution)/shard_map/ppermute | solution.py:192
  157.2 49.5 %collective-permute-start.25 = (bf16[512,512]{1,0:T(8,128)(2,1)}, bf16[512,512]{1,0:T(8,128)(2,1)S(1)}, u32[]{:S(2)}, u32[]{:S(2)}) collective-permute-start(bf16[512,512]{1,0:T(8,128)(2,1)} %pad_maximum_fusion.6), channel_id=1, source_target_pairs={{8,0},{16,24},{9,1},{17,25},{10,2},{18,26},{11,3},{19,27},{12,4},{... | collective-permute-start | bytes 1572872 | tf_op jit(solution)/shard_map/ppermute | solution.py:715
  215.0 12.9 %collective-permute-start.27 = (bf16[2,256,512]{2,1,0:T(8,128)(2,1)S(1)}, bf16[2,256,512]{2,1,0:T(8,128)(2,1)S(1)}, u32[]{:S(2)}, u32[]{:S(2)}) collective-permute-start(bf16[2,256,512]{2,1,0:T(8,128)(2,1)S(1)} %pad_maximum_fusion.7.rest_0_), channel_id=1, source_target_pairs={{0,1},{1,0},{2,3},{3,2},{4,5},{5,4},{6,7},{7,6},{8,9},{9,8},{10,11... | collective-permute-start | bytes 1572872 | tf_op jit(solution)/shard_map/ppermute | solution.py:192
  217.0 12.5 %collective-permute-start.29 = (bf16[2,256,512]{2,1,0:T(8,128)(2,1)S(1)}, bf16[2,256,512]{2,1,0:T(8,128)(2,1)S(1)}, u32[]{:S(2)}, u32[]{:S(2)}) collective-permute-start(bf16[2,256,512]{2,1,0:T(8,128)(2,1)S(1)} %pad_maximum_fusion.8.rest_2_), channel_id=1, source_target_pairs={{0,4},{2,6},{4,0},{6,2},{1,5},{3,7},{5,1},{7,3},{8,12},{10,14},{12... | collective-permute-start | bytes 1572872 | tf_op jit(solution)/shard_map/ppermute | solution.py:188
  269.2 14.4 %collective-permute-start.43 = (bf16[2,256,512]{2,1,0:T(8,128)(2,1)S(1)}, bf16[2,256,512]{2,1,0:T(8,128)(2,1)S(1)}, u32[]{:S(2)}, u32[]{:S(2)}) collective-permute-start(bf16[2,256,512]{2,1,0:T(8,128)(2,1)S(1)} %get-tuple-element.74), channel_id=1, source_target_pairs={{0,4},{2,6},{4,0},{6,2},{1,5},{3,7},{5,1},{7,3},{8,12},{10,14},{12... | collective-permute-start | bytes 1572872 | tf_op jit(solution)/shard_map/ppermute | solution.py:188
  271.1 14.2 %collective-permute-start.41 = (bf16[2,256,512]{2,1,0:T(8,128)(2,1)S(1)}, bf16[2,256,512]{2,1,0:T(8,128)(2,1)S(1)}, u32[]{:S(2)}, u32[]{:S(2)}) collective-permute-start(bf16[2,256,512]{2,1,0:T(8,128)(2,1)S(1)} %get-tuple-element.72), channel_id=1, source_target_pairs={{0,1},{1,0},{2,3},{3,2},{4,5},{5,4},{6,7},{7,6},{8,9},{9,8},{10,11... | collective-permute-start | bytes 1572872 | tf_op jit(solution)/shard_map/ppermute | solution.py:192
  (60 other events, 477.6 us)
Sparse Core Ops, SparseCore 0:
  89.8 108.3 all-gather.4
  199.7 58.8 all-gather.6
